TPU v7x, 512 devices: a whole 4x8x8 slice. The times are simulated.
512 devices in a mesh: wide: 32 (over y, z_hi, core), narrow: 16 (over z_lo, x).
Axes of the slice: x: 4, y: 8, z: 8 (z_hi: 2, z_lo: 4; z = z_hi * 4 + z_lo), core: 2. Of those that a mesh axis runs over, the one named last changes fastest.
Arguments:
- pooled: bfloat16 [262144, 1024], P(('wide', 'narrow')), may hold values from -6 to 6
- cotangent: bfloat16 [262144, 512], P(('wide', 'narrow')), may hold values from -6 to 6
- w_first: bfloat16 [1024, 1024], P('narrow'), may hold values from -0.1875 to 0.1875
- b_first: float32 [1024], replicated, may hold values from -5 to 5
- w_second: bfloat16 [1024, 512], P('narrow'), may hold values from -0.1875 to 0.1875
- counts: bfloat16 [8, 256, 262144], P(None, 'narrow', 'wide'), may hold values from 0 to 3, as said below
- row_ids: int32 [8, 256], P(None, 'narrow'), may hold values from 0 to 63, as said below
- table: float32 [8, 1024, 128], P(None, 'narrow'), may hold values from -6 to 6
- accum: float32 [8, 1024, 128], P(None, 'narrow'), may hold values from 0.1 to 10
Outputs:
- new_table: float32 [8, 1024, 128], P(None, 'narrow')
- new_accum: float32 [8, 1024, 128], P(None, 'narrow')
Inputs may be any that keep to these rules, and one draw needn't show every extreme that they name: `counts`: each entry is zero where the sample does not look up the active row, else a positive lookup weight. `row_ids`: for each table, the 16 ids of one owner (slots j * 16 to (j + 1) * 16 - 1) are distinct.
All inputs are finite; a program needn't handle non-finite values.
Results may differ from a plain program's by a relative error of at most 0.0038.
Values may be sent and summed in bfloat16 or wider, within the bound.
No kernel may reach another device: no remote copies, remote signals or barrier semaphores. Data moves between devices by JAX's collectives and lax.ppermute only.
A program may use at most 128 MiB of HBM per device.

v0:
```python
import math

import jax
import jax.numpy as jnp
from jax import lax
from jax.sharding import PartitionSpec as P

clip_factor = 0.5
learn_rate = 0.05
epsilon = 1e-08


def side_by_side(arrays, axis, dim, along):
    ends, at = ([], 0)
    for a in arrays[:-1]:
        at += a.shape[along]
        ends.append(at)
    both = jnp.concatenate(arrays, axis=along)
    return tuple(jnp.split(lax.all_gather(both, axis, axis=dim, tiled=True), ends, axis=along))


def in_blocks(value, dim, length):
    before, after = (value.shape[:dim], value.shape[dim + 1 :])
    return jnp.moveaxis(value.reshape(*before, length, -1, *after), dim, 0)


def cut_rows(length, count):
    unit = 8 if length >= 8 * count else 1
    return [length // unit * k // count * unit for k in range(1, count)]


def joined_along(parts, dim):
    shape = list(parts.shape[1:])
    shape[dim] *= parts.shape[0]
    return jnp.moveaxis(parts, 0, dim).reshape(shape)


def cut_exchange(value, axis, pieces, split_dim, concat_dim):
    parts = in_blocks(value, split_dim, lax.axis_size(axis))
    cut = max(range(1, max(2, parts.ndim - 1)), key=lambda d: parts.shape[d])
    finished = []
    for piece in jnp.split(parts, cut_rows(parts.shape[cut], pieces), axis=cut):
        if piece.size:
            finished.append(lax.all_to_all(piece, axis, split_axis=0, concat_axis=0, tiled=True))
    return joined_along(jnp.concatenate(finished, axis=cut), concat_dim)


def sum_at_owner(value, axis, dim):
    parts = in_blocks(value, dim, lax.axis_size(axis))
    arrived = lax.all_to_all(parts, axis, split_axis=0, concat_axis=0, tiled=True)
    return arrived.sum(axis=0)


def tower_back(inputs, cotangent, w_first, b_first, w_second):
    hidden_in = jnp.dot(inputs, w_first, preferred_element_type=jnp.float32) + b_first
    back_hidden = lax.dot_general(
        cotangent, w_second, (((1,), (1,)), ((), ())), preferred_element_type=jnp.float32
    )
    sigmoid_val = jax.nn.sigmoid(hidden_in)
    slopes = sigmoid_val * (1.0 + hidden_in * (1.0 - sigmoid_val))
    deltas = (back_hidden * slopes).astype(jnp.bfloat16)
    return lax.dot_general(
        deltas, w_first, (((1,), (1,)), ((), ())), preferred_element_type=jnp.float32
    ).astype(jnp.bfloat16)


def clip_rows(grads, limit):
    norms = jnp.sqrt(jnp.sum(grads * grads, axis=-1, keepdims=True))
    return grads * (limit / jnp.maximum(norms, limit))


def adagrad_rows(current, old_acc, summed):
    new_acc = old_acc + summed * summed
    return (current - learn_rate * summed / (jnp.sqrt(new_acc) + epsilon), new_acc)


def shards(pooled, cotangent, w_first, b_first, w_second, counts, row_ids, table, accum):
    full_first, full_second = side_by_side((w_first, w_second), "narrow", 0, 1)
    grad_in = tower_back(pooled, cotangent, full_first, b_first, full_second)
    tables = counts.shape[0]
    slots = counts.shape[1]
    bags = counts.shape[2]
    emb = table.shape[2]
    samples = pooled.shape[0]
    scale = 1.0 / math.sqrt(bags)
    limit = clip_factor * math.sqrt(emb)
    regrouped = cut_exchange(counts, "narrow", 2, 2, 1)
    local_grad = grad_in.reshape(samples, tables, emb)
    grads = sum_at_owner(
        jnp.einsum(
            "tab,btd->atd", regrouped, local_grad, preferred_element_type=jnp.float32
        ).reshape(slots * lax.axis_size("narrow"), tables * emb),
        "narrow",
        0,
    ).reshape(slots, tables, emb)
    clipped = clip_rows(grads * scale, limit)
    table_index = jnp.arange(tables, dtype=jnp.int32)[:, None]
    current = jnp.transpose(table[table_index, row_ids], (1, 0, 2))
    old_acc = jnp.transpose(accum[table_index, row_ids], (1, 0, 2))
    share = sum_at_owner(clipped.reshape(slots * tables, emb), "wide", 0)
    share_rows = share.shape[0]
    offset = lax.axis_index("wide") * share_rows
    mine_rows = lax.dynamic_slice_in_dim(
        current.reshape(slots * tables, emb), offset, share_rows, 0
    )
    mine_acc = lax.dynamic_slice_in_dim(old_acc.reshape(slots * tables, emb), offset, share_rows, 0)
    share_new, share_acc = adagrad_rows(mine_rows, mine_acc, share)
    gathered_rows, gathered_acc = side_by_side((share_new, share_acc), "wide", 0, 1)
    new_rows = gathered_rows.reshape(slots, tables, emb)
    new_acc = gathered_acc.reshape(slots, tables, emb)
    new_table = table.at[table_index, row_ids].set(jnp.transpose(new_rows, (1, 0, 2)))
    new_accum = accum.at[table_index, row_ids].set(jnp.transpose(new_acc, (1, 0, 2)))
    return (new_table, new_accum)


def solution(mesh):
    in_specs = (
        P(("wide", "narrow"), None),
        P(("wide", "narrow"), None),
        P("narrow", None),
        P(),
        P("narrow", None),
        P(None, "narrow", "wide"),
        P(None, "narrow"),
        P(None, "narrow", None),
        P(None, "narrow", None),
    )
    out_specs = (P(None, "narrow", None), P(None, "narrow", None))
    return jax.shard_map(shards, mesh=mesh, in_specs=in_specs, out_specs=out_specs, check_vma=False)
```

profile of v0, /device:TPU:1, one launch (start us, length us, event | category | flops | bytes accessed | tf_op | source)
XLA Modules:
  0.0 257.7 jit_solution(1986286430375578265)
XLA Ops:
  7.2 1.8 copy.71
  9.0 0.9 copy.72
  9.9 1.6 pad_maximum_fusion
  11.6 2.4 copy.63
  14.0 0.2 bitcast_bitcast_fusion
  14.2 1.2 fusion.25
  15.4 1.5 copy.53
  17.0 10.4 %all-to-all-start.1 = ((bf16[16,8,8,512]{3,2,1,0:T(8,128)(2,1)}), bf16[16,8,8,512]{3,2,1,0:T(8,128)(2,1)S(1)}, u32[]{:S(2)}, u32[]{:S(2)}) async-start(bf16[16,8,8,512]{3,2,1,0:T(8,128)(2,1)} %copy.53), calls=%async_computation.1 | async-start | bytes 2097152 | tf_op jit(solution)/shard_map/all_to_all | solution.py:44
  27.3 1.8 copy.52
  29.2 30.0 %all-to-all-done.1 = bf16[16,8,8,512]{3,2,1,0:T(8,128)(2,1)S(1)} async-done(((bf16[16,8,8,512]{3,2,1,0:T(8,128)(2,1)}), bf16[16,8,8,512]{3,2,1,0:T(8,128)(2,1)S(1)}, u32[]{:S(2)}, u32[]{:S(2)}) %all-to-all-start.1) | async-done | bytes 1048608 | tf_op jit(solution)/shard_map/all_to_all | solution.py:44
  59.2 49.5 %all_to_all.20 = bf16[16,8,8,512]{3,2,1,0:T(8,128)(2,1)S(1)} all-to-all(bf16[16,8,8,512]{3,2,1,0:T(8,128)(2,1)S(1)} %copy.52), channel_id=1, replica_groups=mesh['wide'=32,'narrow'=16] {'narrow'}, dimensions={0} | all-to-all | bytes 2097152 | tf_op jit(solution)/shard_map/all_to_all | solution.py:44
  108.7 0.3 maximum_bitcast_fusion
  108.9 0.2 copy.54
  109.2 4.2 %fusion.9 = f32[1024,512]{1,0:T(8,128)} fusion(bf16[512,1024]{1,0:T(8,128)(2,1)S(1)} %copy-done, bf16[1024,1536]{1,0:T(8,128)(2,1)} %all-gather.3.cloned.1.call-done), kind=kOutput, calls=%fused_computation.17 | convolution fusion | flops 1073741824 | bytes 5242880 | tf_op jit(solution)/shard_map/dot_general | solution.py:55
  113.4 6.0 %fusion.11 = bf16[512,1024]{1,0:T(8,128)(2,1)} fusion(bf16[1024,1536]{1,0:T(8,128)(2,1)} %all-gather.3.cloned.1.call-done, f32[1024,512]{1,0:T(8,128)} %fusion.9, bf16[512,512]{1,0:T(8,128)(2,1)} %param.10, f32[1024]{0:T(1024)S(1)} %copy-done.5), kind=kOutput, calls=%fused_computation.19 | convolution fusion | flops 1616379904 | bytes 6819840 | tf_op jit(solution)/shard_map/dot_general | solution.py:62
  119.4 2.3 copy.61
  121.7 3.1 %convolution_bitcast_fusion = f32[256,8,128]{0,2,1:T(8,128)} fusion(bf16[512,8,128]{0,2,1:T(8,128)(2,1)} %bitcast.82, bf16[8,256,512]{2,1,0:T(8,128)(2,1)S(1)} %bitcast.80), kind=kOutput, calls=%fused_computation.20 | convolution fusion | flops 268435456 | bytes 4194304 | tf_op jit(solution)/shard_map/tab,btd->atd/dot_general | solution.py:90
  124.8 1.6 copy.56
  126.5 1.1 reshape_reshape.4
  127.6 8.5 %all-to-all-start.2 = ((f32[16,16,1024]{2,1,0:T(8,128)}), f32[16,16,1024]{2,1,0:T(8,128)S(1)}, u32[]{:S(2)}, u32[]{:S(2)}) async-start(f32[16,16,1024]{2,1,0:T(8,128)} %reshape_reshape.4), calls=%async_computation.2 | async-start | bytes 2097152 | tf_op jit(solution)/shard_map/all_to_all | solution.py:50
  136.2 0.1 reshape.72
  136.3 1.2 gather_fusion.1
  137.6 1.2 gather_fusion
  138.8 16.7 %all-to-all-done.2 = f32[16,16,1024]{2,1,0:T(8,128)S(1)} async-done(((f32[16,16,1024]{2,1,0:T(8,128)}), f32[16,16,1024]{2,1,0:T(8,128)S(1)}, u32[]{:S(2)}, u32[]{:S(2)}) %all-to-all-start.2) | async-done | bytes 1048608 | tf_op jit(solution)/shard_map/all_to_all | solution.py:50
  155.6 0.1 reduce_sum.28
  155.8 0.7 broadcast_multiply_fusion
  156.5 19.6 %all-to-all-start.3 = ((f32[32,4,128]{2,1,0:T(4,128)}), f32[32,4,128]{2,1,0:T(4,128)S(1)}, u32[]{:S(2)}, u32[]{:S(2)}) async-start(f32[32,4,128]{2,1,0:T(4,128)} %broadcast_multiply_fusion), calls=%async_computation.3 | async-start | bytes 131072 | tf_op jit(solution)/shard_map/all_to_all | solution.py:50
  176.2 12.2 %all-to-all-done.3 = f32[32,4,128]{2,1,0:T(4,128)S(1)} async-done(((f32[32,4,128]{2,1,0:T(4,128)}), f32[32,4,128]{2,1,0:T(4,128)S(1)}, u32[]{:S(2)}, u32[]{:S(2)}) %all-to-all-start.3) | async-done | bytes 65568 | tf_op jit(solution)/shard_map/all_to_all | solution.py:50
  188.4 47.7 %all-gather = f32[32,4,256]{2,1,0:T(4,128)S(1)} all-gather(f32[1,4,256]{2,1,0:T(4,128)S(1)} %maximum_bitcast_fusion.1), channel_id=1, replica_groups=mesh['wide'=32,'narrow'=16] {'wide'}, dimensions={0}, use_global_device_ids=true | all-gather | bytes 135168 | tf_op jit(solution)/shard_map/all_gather | solution.py:19
  236.3 6.9 %scatter_fusion = f32[8,64,128]{2,1,0:T(8,128)S(1)} fusion(f32[8,64,128]{2,1,0:T(8,128)S(1)} %copy-done.2, s32[128]{0:T(128)S(1)} %reshape.72, f32[128,128]{1,0:T(8,128)S(1)} %bitcast.85), kind=kCustom, calls=%fused_computation.2 | custom fusion | bytes 197632 | tf_op jit(solution)/shard_map/scatter | solution.py:111
  243.2 6.9 %scatter_fusion.1 = f32[8,64,128]{2,1,0:T(8,128)S(1)} fusion(f32[8,64,128]{2,1,0:T(8,128)S(1)} %copy.72, s32[128]{0:T(128)S(1)} %reshape.72, f32[128,128]{1,0:T(8,128)S(1)} %bitcast.84), kind=kCustom, calls=%fused_computation.3 | custom fusion | bytes 197632 | tf_op jit(solution)/shard_map/scatter | solution.py:112
  250.1 0.7 copy-done.1
  (30 shorter events, 0.6 us)
Async XLA Ops:
  7.2 102.0 %copy-start = (bf16[512,1024]{1,0:T(8,128)(2,1)S(1)}, bf16[512,1024]{1,0:T(8,128)(2,1)}, u32[]{:S(2)}) copy-start(bf16[512,1024]{1,0:T(8,128)(2,1)} %param.9) | copy-start | bytes 3145732
  7.2 102.0 %all-gather.3.cloned.1.call-start = ((), (), s32[]{:S(2)}) async-start(), calls=%async_computation.4 | async-start | bytes 3342336 | tf_op jit(solution)/shard_map/all_gather | solution.py:19
  17.0 42.2 %all-to-all-start.1 = ((bf16[16,8,8,512]{3,2,1,0:T(8,128)(2,1)}), bf16[16,8,8,512]{3,2,1,0:T(8,128)(2,1)S(1)}, u32[]{:S(2)}, u32[]{:S(2)}) async-start(bf16[16,8,8,512]{3,2,1,0:T(8,128)(2,1)} %copy.53), calls=%async_computation.1 | async-start | bytes 2097152 | tf_op jit(solution)/shard_map/all_to_all | solution.py:44
  109.1 4.3 %copy-start.5 = (f32[1024]{0:T(1024)S(1)}, f32[1024]{0:T(1024)}, u32[]{:S(2)}) copy-start(f32[1024]{0:T(1024)} %param.12) | copy-start | bytes 12292
  126.4 9.7 %copy-start.4 = (s32[8,16]{1,0:T(8,128)S(1)}, s32[8,16]{1,0:T(8,128)}, u32[]{:S(2)}) copy-start(s32[8,16]{1,0:T(8,128)} %param.15) | copy-start | bytes 1540
  126.4 11.1 %copy-start.2 = (f32[8,64,128]{2,1,0:T(8,128)S(1)}, f32[8,64,128]{2,1,0:T(8,128)}, u32[]{:S(2)}) copy-start(f32[8,64,128]{2,1,0:T(8,128)} %copy.71) | copy-start | bytes 786436
  127.6 27.9 %all-to-all-start.2 = ((f32[16,16,1024]{2,1,0:T(8,128)}), f32[16,16,1024]{2,1,0:T(8,128)S(1)}, u32[]{:S(2)}, u32[]{:S(2)}) async-start(f32[16,16,1024]{2,1,0:T(8,128)} %reshape_reshape.4), calls=%async_computation.2 | async-start | bytes 2097152 | tf_op jit(solution)/shard_map/all_to_all | solution.py:50
  156.5 31.8 %all-to-all-start.3 = ((f32[32,4,128]{2,1,0:T(4,128)}), f32[32,4,128]{2,1,0:T(4,128)S(1)}, u32[]{:S(2)}, u32[]{:S(2)}) async-start(f32[32,4,128]{2,1,0:T(4,128)} %broadcast_multiply_fusion), calls=%async_computation.3 | async-start | bytes 131072 | tf_op jit(solution)/shard_map/all_to_all | solution.py:50
  243.2 6.9 %copy-start.3 = (f32[8,64,128]{2,1,0:T(8,128)}, f32[8,64,128]{2,1,0:T(8,128)S(1)}, u32[]{:S(2)}) copy-start(f32[8,64,128]{2,1,0:T(8,128)S(1)} %scatter_fusion) | copy-start | bytes 786436
  250.1 0.7 copy-start.1
Sparse Core Ops, SparseCore 0:
  11.7 95.0 all-gather.2
where the time goes:
time: 258 us
  blocking collectives  97.2 us (38%)
  waiting for transfers between devices  58.9 us (23%)
  starting transfers between devices  38.5 us (15%)
  local copies, waits for them, and re-layouts  32.5 us (13%)
  between operations  14.3 us (6%)
  matrix products  13.3 us (5%)
  other arithmetic  2.88 us (1%)
    all_to_all x1, blocking collectives, cut_exchange(): lax.all_to_all(piece, axis, split_axis=0, concat_axis=0, tiled=True)  49.5 us
    all_gather x1, blocking collectives, side_by_side(): lax.all_gather(both, axis, axis=dim, tiled=True)  47.7 us
    all_to_all x1, waiting for transfers between devices, cut_exchange(): lax.all_to_all(piece, axis, split_axis=0, concat_axis=0, tiled=True)  30 us
    all_to_all x2, waiting for transfers between devices, sum_at_owner(): lax.all_to_all(parts, axis, split_axis=0, concat_axis=0, tiled=True)  28.8 us
    all_to_all x2, starting transfers between devices, sum_at_owner(): lax.all_to_all(parts, axis, split_axis=0, concat_axis=0, tiled=True)  28.1 us
    all_to_all x1, starting transfers between devices, cut_exchange(): lax.all_to_all(piece, axis, split_axis=0, concat_axis=0, tiled=True)  10.4 us
    scatter x1, local copies, waits for them, and re-layouts, shards(): table.at[table_index, row_ids].set(jnp.transpose(new_rows, (1, 0, 2)))  6.9 us
    scatter x1, local copies, waits for them, and re-layouts, shards(): accum.at[table_index, row_ids].set(jnp.transpose(new_acc, (1, 0, 2)))  6.9 us
  transfers between devices with their start and end apart: 4, of which 3 were waited for; matrix products, arithmetic and copies ran while one was open for 4% of the time, Pallas kernels for 0%

commit v1 on v0

v1 whole, which is shorter than its diff:
```python
import functools
import math

import jax
import jax.numpy as jnp
from jax import lax
from jax.experimental import pallas as pl
from jax.experimental.pallas import tpu as pltpu
from jax.sharding import PartitionSpec as P

clip_factor = 0.5
learn_rate = 0.05
epsilon = 1e-08

N_Y, N_HI, N_CORE = 8, 2, 2
bf16, f32 = jnp.bfloat16, jnp.float32
VMEM = pl.BlockSpec(memory_space=pltpu.VMEM)
SMEM = pl.BlockSpec(memory_space=pltpu.SMEM)
MIB = 1 << 20


def wide_at(y, hi, core):
    return (y * N_HI + hi) * N_CORE + core


Y_GROUPS = [[wide_at(y, h, c) for y in range(N_Y)] for h in range(N_HI) for c in range(N_CORE)]
YZ_GROUPS = [[wide_at(y, h, c) for y in range(N_Y) for h in range(N_HI)] for c in range(N_CORE)]
CORE_SWAP = [(w, w ^ 1) for w in range(N_Y * N_HI * N_CORE)]


def call(body, out_shape, in_specs, scratch=(), flops=0, nbytes=0, limit=48):
    return pl.pallas_call(
        body,
        out_shape=out_shape,
        in_specs=in_specs,
        out_specs=jax.tree.map(lambda _: VMEM, out_shape),
        scratch_shapes=list(scratch),
        compiler_params=pltpu.CompilerParams(vmem_limit_bytes=limit * MIB),
        cost_estimate=pl.CostEstimate(flops=flops, bytes_accessed=nbytes, transcendentals=0),
    )


def tower_body(core_ref, own_ref, other_ref, pooled_ref, cot_ref, bias_ref, grad_ref, first, second, deltas):
    core = core_ref[0]
    owners = own_ref.shape[1]
    rows = first.shape[0] // owners
    half = rows // 2
    for ref, side in ((own_ref, core), (other_ref, 1 - core)):
        for n in range(owners):
            at = pl.multiple_of(n * rows + side * half, 32)
            for y in range(N_Y):
                first[pl.ds(at, half), y * 128 : (y + 1) * 128] = ref[y, n, :half, :]
                lower = pl.multiple_of(at + (y % 2) * 16, 16)
                second[pl.ds(lower, 16), (y // 2) * 128 : (y // 2 + 1) * 128] = ref[y, n, half:, :]
    inner = first.shape[1]
    step = 256
    across = (((1,), (1,)), ((), ()))
    for at in range(0, inner, step):
        cols = slice(at, at + step)
        hidden = jnp.dot(pooled_ref[...], first[:, cols], preferred_element_type=f32) + bias_ref[:, cols]
        back = lax.dot_general(cot_ref[...], second[cols, :], across, preferred_element_type=f32)
        gate = jax.nn.sigmoid(hidden)
        deltas[:, cols] = (back * (gate * (1.0 + hidden * (1.0 - gate)))).astype(bf16)
    for at in range(0, first.shape[0], step):
        cols = slice(at, at + step)
        grad_ref[:, cols] = lax.dot_general(
            deltas[...], first[cols, :], across, preferred_element_type=f32
        ).astype(bf16)


def partial_body(counts_ref, grad_ref, out_ref):
    owners, tables, act, bags = counts_ref.shape
    emb = grad_ref.shape[1] // tables
    for t in range(tables):
        cols = slice(t * emb, (t + 1) * emb)
        lookups = counts_ref[:, t, :, :].reshape(owners * act, bags)
        part = jnp.dot(lookups, grad_ref[:, cols], preferred_element_type=f32)
        out_ref[:, :, cols] = part.reshape(owners, act, emb).astype(bf16)


def clip_body(scale, limit, core_ref, parts_ref, keep_ref, send_ref, rows):
    peers, act, width = parts_ref.shape
    emb = rows.shape[1]
    total = parts_ref[0].astype(f32)
    for n in range(1, peers):
        total = total + parts_ref[n].astype(f32)
    total = total * scale
    for t in range(width // emb):
        grads = total[:, t * emb : (t + 1) * emb]
        norms = jnp.sqrt(jnp.sum(grads * grads, axis=-1, keepdims=True))
        rows[t * act : (t + 1) * act, :] = grads * (limit / jnp.maximum(norms, limit))
    core = core_ref[0]
    half = rows.shape[0] // 2
    keep_ref[...] = rows[pl.ds(pl.multiple_of(core * half, 8), half), :]
    send_ref[...] = rows[pl.ds(pl.multiple_of((1 - core) * half, 8), half), :]


def pair_body(keep_ref, got_ref, out_ref):
    both = (keep_ref[...] + got_ref[...]).astype(bf16)
    for n in range(out_ref.shape[0]):
        out_ref[n] = both


def share_body(parts_ref, out_ref):
    total = parts_ref[0].astype(f32)
    for n in range(1, parts_ref.shape[0]):
        total = total + parts_ref[n].astype(f32)
    out_ref[...] = total


def update_body(core_ref, ids_ref, mine_ref, other_ref, table_ref, accum_ref, new_table_ref, new_accum_ref, dense):
    tables, act = ids_ref.shape
    per_core = tables // 2
    core = core_ref[0]
    dense[...] = jnp.zeros_like(dense)
    for ref, side in ((mine_ref, core), (other_ref, 1 - core)):
        for t in range(per_core):
            for a in range(act):
                table = side * per_core + t
                row = ids_ref[table, a]
                dense[table, pl.ds(row, 1), :] = ref[pl.ds(t * act + a, 1), :]
    for t in range(tables):
        summed = dense[t]
        new_acc = accum_ref[t] + summed * summed
        new_accum_ref[t] = new_acc
        new_table_ref[t] = table_ref[t] - learn_rate * summed / (jnp.sqrt(new_acc) + epsilon)


def shards(pooled, cotangent, w_first, b_first, w_second, counts, row_ids, table, accum):
    tables, act, bags = counts.shape
    emb = table.shape[2]
    samples = pooled.shape[0]
    inner, top = w_first.shape[1], w_second.shape[1]
    owners = lax.axis_size("narrow")
    scale = 1.0 / math.sqrt(bags)
    limit = clip_factor * math.sqrt(emb)
    wide = lax.axis_index("wide")
    core = wide % N_CORE
    y = wide // (N_HI * N_CORE)
    core_at = core.reshape(1).astype(jnp.int32)

    half = w_first.shape[0] // 2
    piece = jnp.concatenate(
        [
            lax.dynamic_slice(w_first, (core * half, y * 128), (half, 128)),
            lax.dynamic_slice(w_second, (core * half + (y % 2) * 16, (y // 2) * 128), (16, 128)),
        ],
        axis=0,
    )
    spread = lax.all_to_all(
        jnp.broadcast_to(piece[None], (owners, *piece.shape)), "narrow", 0, 0, tiled=True
    )
    by_owner = jnp.transpose(counts.reshape(tables, act, owners, samples), (2, 0, 1, 3))
    by_owner, spread = lax.optimization_barrier((by_owner, spread))
    own = lax.all_gather(spread, "wide", axis=0, axis_index_groups=Y_GROUPS)
    regrouped = lax.all_to_all(by_owner, "narrow", 0, 0, tiled=True)
    other = lax.ppermute(own, "wide", CORE_SWAP)

    grad_in = call(
        tower_body,
        jax.ShapeDtypeStruct((samples, owners * w_first.shape[0]), bf16),
        [SMEM] + [VMEM] * 5,
        [
            pltpu.VMEM((owners * w_first.shape[0], inner), bf16),
            pltpu.VMEM((inner, top), bf16),
            pltpu.VMEM((samples, inner), bf16),
        ],
        flops=2 * samples * inner * (2 * inner + top),
        nbytes=8 * MIB,
    )(core_at, own, other, pooled, cotangent, b_first.reshape(1, -1))

    parts = call(
        partial_body,
        jax.ShapeDtypeStruct((owners, act, tables * emb), bf16),
        [VMEM] * 2,
        flops=2 * owners * act * samples * tables * emb,
        nbytes=4 * MIB,
    )(regrouped, grad_in)
    arrived = lax.all_to_all(parts, "narrow", 0, 0, tiled=True)

    rows = tables * act
    half_rows = jax.ShapeDtypeStruct((rows // 2, emb), f32)
    keep, send = call(
        functools.partial(clip_body, scale, limit),
        (half_rows, half_rows),
        [SMEM, VMEM],
        [pltpu.VMEM((rows, emb), f32)],
        nbytes=MIB,
    )(core_at, arrived)
    got = lax.ppermute(send, "wide", CORE_SWAP)
    copies = call(
        pair_body, jax.ShapeDtypeStruct((N_Y * N_HI, rows // 2, emb), bf16), [VMEM] * 2, nbytes=MIB
    )(keep, got)
    shares = lax.all_to_all(copies, "wide", 0, 0, axis_index_groups=YZ_GROUPS, tiled=True)
    mine = call(share_body, half_rows, [VMEM], nbytes=MIB)(shares)
    theirs = lax.ppermute(mine, "wide", CORE_SWAP)
    whole = jax.ShapeDtypeStruct(table.shape, f32)
    return call(
        update_body,
        (whole, whole),
        [SMEM, SMEM] + [VMEM] * 4,
        [pltpu.VMEM(table.shape, f32)],
        nbytes=2 * MIB,
    )(core_at, row_ids, mine, theirs, table, accum)


def solution(mesh):
    in_specs = (
        P(("wide", "narrow"), None),
        P(("wide", "narrow"), None),
        P("narrow", None),
        P(),
        P("narrow", None),
        P(None, "narrow", "wide"),
        P(None, "narrow"),
        P(None, "narrow", None),
        P(None, "narrow", None),
    )
    out_specs = (P(None, "narrow", None), P(None, "narrow", None))
    return jax.shard_map(shards, mesh=mesh, in_specs=in_specs, out_specs=out_specs, check_vma=False)
```

time: 258 us -> 149 us (0.58)
  blocking collectives: 97.2 us -> 43.1 us
  local copies, waits for them, and re-layouts: 32.5 us -> 9.72 us
  waiting for transfers between devices: 58.9 us -> 45.5 us
  matrix products: 13.3 us -> 0 us
  starting transfers between devices: 38.5 us -> 29.5 us
  Pallas kernels: 0 us -> 6.11 us
  other arithmetic: 2.88 us -> 0.01 us
    all_to_all x3 -> x2, waiting for transfers between devices: 58.8 us -> 5.09 us  [the longest x1 5.08 us: shards(): lax.all_to_all(jnp.broadcast_to(piece[None], (owners, *piece.shape)), 'na...]
    all_gather x1 -> x0, blocking collectives: 47.7 us -> none  [side_by_side(): lax.all_gather(both, axis, axis=dim, tiled=True)]
    all_gather x1, waiting for transfers between devices: 0.02 us -> 35.5 us  [shards(): own = lax.all_gather(spread, 'wide', axis=0, axis_index_groups=Y_GROUPS)]
    all_to_all x3 -> x2, starting transfers between devices: 38.5 us -> 14.8 us  [the longest x1 10.4 us: shards(): lax.all_to_all(jnp.broadcast_to(piece[None], (owners, *piece.shape)), 'na...]
    ppermute x0 -> x3, starting transfers between devices: none -> 14.7 us  [the longest x1 6.67 us: shards(): other = lax.ppermute(own, 'wide', CORE_SWAP)]
    scatter x2 -> x0, local copies, waits for them, and re-layouts: 13.8 us -> none  [the longest x1 6.9 us: shards(): table.at[table_index, row_ids].set(jnp.transpose(new_rows, (1, 0, 2)))]
    dot_general x3 -> x0, matrix products: 13.3 us -> none  [the longest x1 6.01 us: tower_back(): lax.dot_general(deltas, w_first, (((1,), (1,)), ((), ())), preferred_elem...]
    all_to_all x1 -> x2, blocking collectives: 49.5 us -> 43.1 us  [the longest x1 21.7 us: shards(): lax.all_to_all(copies, 'wide', 0, 0, axis_index_groups=YZ_GROUPS, tiled=T...]
  transfers between devices with their start and end apart: 4 -> 6, of which waited for: 3 -> 5; matrix products, arithmetic and copies ran while one was open for 4% -> 2% of each run, Pallas kernels for 0% -> 2%
where the time goes in v1:
time: 149 us; the launch traced here: 148 us
  waiting for transfers between devices  45.5 us (31%)
  blocking collectives  43.1 us (29%)
  starting transfers between devices  29.5 us (20%)
  between operations  14.2 us (10%)
  local copies, waits for them, and re-layouts  9.72 us (7%)
  Pallas kernels  6.11 us (4%)
    all_gather x1, waiting for transfers between devices, shards(): own = lax.all_gather(spread, 'wide', axis=0, axis_index_groups=Y_GROUPS)  35.5 us
    all_to_all x1, blocking collectives, shards(): lax.all_to_all(copies, 'wide', 0, 0, axis_index_groups=YZ_GROUPS, tiled=T...  21.7 us
    all_to_all x1, blocking collectives, shards(): arrived = lax.all_to_all(parts, 'narrow', 0, 0, tiled=True)  21.4 us
    all_to_all x1, starting transfers between devices, shards(): lax.all_to_all(jnp.broadcast_to(piece[None], (owners, *piece.shape)), 'na...  10.4 us
    ppermute x1, starting transfers between devices, shards(): other = lax.ppermute(own, 'wide', CORE_SWAP)  6.67 us
    all_to_all x1, waiting for transfers between devices, shards(): lax.all_to_all(jnp.broadcast_to(piece[None], (owners, *piece.shape)), 'na...  5.08 us
    all_to_all x1, starting transfers between devices, shards(): regrouped = lax.all_to_all(by_owner, 'narrow', 0, 0, tiled=True)  4.41 us
    unnamed x16, local copies, waits for them, and re-layouts  4.37 us
  transfers between devices with their start and end apart: 6, of which 5 were waited for; matrix products, arithmetic and copies ran while one was open for 2% of the time, Pallas kernels for 2%

profile of v1, /device:TPU:1, one launch (start us, length us, event | category | flops | bytes accessed | tf_op | source)
XLA Modules:
  0.0 148.1 jit_solution(15819396101660283607)
XLA Ops:
  7.2 0.7 dynamic_slice.7
  7.9 0.7 dynamic_slice.6
  8.6 0.7 broadcast_in_dim.2
  9.3 10.4 %all-to-all-start = ((bf16[16,48,128]{2,1,0:T(8,128)(2,1)}), bf16[16,48,128]{2,1,0:T(8,128)(2,1)S(1)}, u32[]{:S(2)}, u32[]{:S(2)}) async-start(bf16[16,48,128]{2,1,0:T(8,128)(2,1)} %broadcast_in_dim.2), calls=%async_computation | async-start | bytes 393216 | tf_op jit(solution)/shard_map/all_to_all | solution.py:150
  19.7 0.0 all-gather.3.cloned.1.call-start
  19.8 3.3 %copy.15 = bf16[8,2,16,8,512]{4,3,1,0,2:T(8,128)(2,1)} copy(bf16[8,2,16,8,512]{4,3,2,1,0:T(8,128)(2,1)} %bitcast.14) | data formatting | bytes 4194304 | tf_op jit(solution)/shard_map/reshape | solution.py:153
  23.0 5.1 %all-to-all-done = bf16[16,48,128]{2,1,0:T(8,128)(2,1)S(1)} async-done(((bf16[16,48,128]{2,1,0:T(8,128)(2,1)}), bf16[16,48,128]{2,1,0:T(8,128)(2,1)S(1)}, u32[]{:S(2)}, u32[]{:S(2)}) %all-to-all-start) | async-done | bytes 196640 | tf_op jit(solution)/shard_map/all_to_all | solution.py:150
  28.1 0.7 copy-done.7
  28.8 0.0 all-gather.3.cloned.1.call-update
  28.8 0.0 copy-start.6
  28.8 4.4 %all-to-all-start.1 = ((bf16[16,8,16,512]{3,2,1,0:T(8,128)(2,1)}), bf16[16,8,16,512]{3,2,1,0:T(8,128)(2,1)S(1)}, u32[]{:S(2)}, u32[]{:S(2)}) async-start(bf16[16,8,16,512]{3,2,1,0:T(8,128)(2,1)} %bitcast.13), calls=%async_computation.1 | async-start | bytes 4194304 | tf_op jit(solution)/shard_map/all_to_all | solution.py:156
  33.2 35.5 %all-gather.3.cloned.1.call-done = bf16[128,48,128]{2,1,0:T(8,128)(2,1)} async-done(((bf16[16,48,128]{2,1,0:T(8,128)(2,1)}), bf16[128,48,128]{2,1,0:T(8,128)(2,1)}) %all-gather.3.cloned.1.call-update) | async-done | bytes 1572880 | tf_op jit(solution)/shard_map/all_gather | solution.py:155
  68.7 6.7 %collective-permute-start = (bf16[8,16,48,128]{3,2,1,0:T(8,128)(2,1)}, bf16[8,16,48,128]{3,2,1,0:T(8,128)(2,1)S(1)}, u32[]{:S(2)}, u32[]{:S(2)}) collective-permute-start(bf16[8,16,48,128]{3,2,1,0:T(8,128)(2,1)} %bitcast.10), channel_id=1, source_target_pairs={{0,16},{16,0},{32,48},{48,32},{64,80},{80,64},{96,112},{112,96},{1... | collective-permute-start | bytes 4718600 | tf_op jit(solution)/shard_map/ppermute | solution.py:157
  75.4 3.2 %collective-permute-done.other_ref = bf16[8,16,48,128]{3,2,1,0:T(8,128)(2,1)S(1)} collective-permute-done((bf16[8,16,48,128]{3,2,1,0:T(8,128)(2,1)}, bf16[8,16,48,128]{3,2,1,0:T(8,128)(2,1)S(1)}, u32[]{:S(2)}, u32[]{:S(2)}) %collective-permute-start) | collective-permute-done | bytes 1572896 | tf_op jit(solution)/shard_map/ppermute | solution.py:157
  78.6 0.0 copy-done.6
  78.6 1.4 copy-done.3
  80.0 1.2 copy-done.4
  81.2 1.0 copy-done.5
  82.3 3.5 %shard_map.104.grad_ref = bf16[512,1024]{1,0:T(8,128)(2,1)S(1)} custom-call(s32[1]{0:T(128)} %bitcast.core_ref, bf16[8,16,48,128]{3,2,1,0:T(8,128)(2,1)S(1)} %bitcast.11, bf16[8,16,48,128]{3,2,1,0:T(8,128)(2,1)S(1)} %collective-permute-done.other_ref, bf16[512,1024]{1,0:T(8,128)(2,1)S(1)} %copy-done.4, bf16[512,512]{1,0:T(8,128)(2,1)S(1)} %copy-done.5, ...), custom_call_target="tpu_custom_call" | custom-call | flops 2684354560 | bytes 8388608 | tf_op jit(solution)/shard_map/pallas_call | solution.py:159
  85.8 0.0 all-to-all-done.1.counts_ref
  85.8 0.7 shard_map.105
  86.5 0.0 copy-start
  86.6 0.0 copy-start.1
  86.6 0.0 copy-start.2
  86.6 21.4 %all_to_all.20.parts_ref = bf16[16,16,1024]{2,1,0:T(8,128)(2,1)S(1)} all-to-all(bf16[16,16,1024]{2,1,0:T(8,128)(2,1)S(1)} %shard_map.105), channel_id=1, replica_groups=mesh['wide'=32,'narrow'=16] {'narrow'}, dimensions={0} | all-to-all | bytes 1048576 | tf_op jit(solution)/shard_map/all_to_all | solution.py:179
  107.9 0.2 shard_map.106
  108.1 4.2 %collective-permute-start.1 = (f32[64,128]{1,0:T(8,128)S(1)}, f32[64,128]{1,0:T(8,128)S(1)}, u32[]{:S(2)}, u32[]{:S(2)}) collective-permute-start(f32[64,128]{1,0:T(8,128)S(1)} %get-tuple-element.9), channel_id=1, source_target_pairs={{0,16},{16,0},{32,48},{48,32},{64,80},{80,64},{96,112},{112,96},{1... | collective-permute-start | bytes 98312 | tf_op jit(solution)/shard_map/ppermute | solution.py:190
  112.3 0.8 collective-permute-done.1.got_ref
  113.2 21.7 %all_to_all.21.parts_ref = bf16[16,64,128]{2,1,0:T(8,128)(2,1)S(1)} all-to-all(bf16[16,64,128]{2,1,0:T(8,128)(2,1)S(1)} %shard_map.107), channel_id=1, replica_groups={{0,32,64,96,128,160,192,224,256,288,320,352,384,416,448,480},{16,48,80,..., dimensions={0} | all-to-all | bytes 524288 | tf_op jit(solution)/shard_map/all_to_all | solution.py:194
  134.9 3.8 %collective-permute-start.2 = (f32[64,128]{1,0:T(8,128)S(1)}, f32[64,128]{1,0:T(8,128)S(1)}, u32[]{:S(2)}, u32[]{:S(2)}) collective-permute-start(f32[64,128]{1,0:T(8,128)S(1)} %shard_map.108.mine_ref), channel_id=1, source_target_pairs={{0,16},{16,0},{32,48},{48,32},{64,80},{80,64},{96,112},{112,96},{1... | collective-permute-start | bytes 98312 | tf_op jit(solution)/shard_map/ppermute | solution.py:196
  138.8 0.8 collective-permute-done.2.other_ref
  139.6 1.6 %shard_map.109 = (f32[8,64,128]{2,1,0:T(8,128)}, f32[8,64,128]{2,1,0:T(8,128)}) custom-call(s32[1]{0:T(128)} %bitcast.core_ref, s32[8,16]{1,0:T(8,128)S(1)} %copy-done.2, f32[64,128]{1,0:T(8,128)S(1)} %shard_map.108.mine_ref, f32[64,128]{1,0:T(8,128)S(1)} %collective-permute-done.2.other_ref, f32[8,64,128]{2,1,0:T(8,128)S(1)} %copy-done, ...), custom_call_target="tpu_custom_call" | custom-call | bytes 2097152 | tf_op jit(solution)/shard_map/pallas_call | solution.py:198
  (10 shorter events, 0.1 us)
Async XLA Ops:
  9.3 18.8 %all-to-all-start = ((bf16[16,48,128]{2,1,0:T(8,128)(2,1)}), bf16[16,48,128]{2,1,0:T(8,128)(2,1)S(1)}, u32[]{:S(2)}, u32[]{:S(2)}) async-start(bf16[16,48,128]{2,1,0:T(8,128)(2,1)} %broadcast_in_dim.2), calls=%async_computation | async-start | bytes 393216 | tf_op jit(solution)/shard_map/all_to_all | solution.py:150
  19.7 49.0 %all-gather.3.cloned.1.call-start = ((), (), s32[]{:S(2)}) async-start(), calls=%async_computation.4 | async-start | bytes 1769472 | tf_op jit(solution)/shard_map/all_gather | solution.py:155
  28.1 0.7 copy-start.7
  28.8 49.8 %copy-start.6 = (f32[1024]{0:T(1024)S(1)}, f32[1024]{0:T(1024)}, u32[]{:S(2)}) copy-start(f32[1024]{0:T(1024)} %param.12) | copy-start | bytes 12292
  28.8 57.0 %all-to-all-start.1 = ((bf16[16,8,16,512]{3,2,1,0:T(8,128)(2,1)}), bf16[16,8,16,512]{3,2,1,0:T(8,128)(2,1)S(1)}, u32[]{:S(2)}, u32[]{:S(2)}) async-start(bf16[16,8,16,512]{3,2,1,0:T(8,128)(2,1)} %bitcast.13), calls=%async_computation.1 | async-start | bytes 4194304 | tf_op jit(solution)/shard_map/all_to_all | solution.py:156
  68.7 9.9 %collective-permute-start = (bf16[8,16,48,128]{3,2,1,0:T(8,128)(2,1)}, bf16[8,16,48,128]{3,2,1,0:T(8,128)(2,1)S(1)}, u32[]{:S(2)}, u32[]{:S(2)}) collective-permute-start(bf16[8,16,48,128]{3,2,1,0:T(8,128)(2,1)} %bitcast.10), channel_id=1, source_target_pairs={{0,16},{16,0},{32,48},{48,32},{64,80},{80,64},{96,112},{112,96},{1... | collective-permute-start | bytes 4718600 | tf_op jit(solution)/shard_map/ppermute | solution.py:157
  78.6 1.4 copy-start.3
  80.0 1.2 copy-start.4
  81.2 1.0 copy-start.5
  86.5 53.1 %copy-start = (f32[8,64,128]{2,1,0:T(8,128)S(1)}, f32[8,64,128]{2,1,0:T(8,128)}, u32[]{:S(2)}) copy-start(f32[8,64,128]{2,1,0:T(8,128)} %table_ref.1) | copy-start | bytes 786436
  86.6 53.1 %copy-start.1 = (f32[8,64,128]{2,1,0:T(8,128)S(1)}, f32[8,64,128]{2,1,0:T(8,128)}, u32[]{:S(2)}) copy-start(f32[8,64,128]{2,1,0:T(8,128)} %accum_ref.1) | copy-start | bytes 786436
  86.6 53.0 %copy-start.2 = (s32[8,16]{1,0:T(8,128)S(1)}, s32[8,16]{1,0:T(8,128)}, u32[]{:S(2)}) copy-start(s32[8,16]{1,0:T(8,128)} %ids_ref.1) | copy-start | bytes 1540
  108.1 5.0 %collective-permute-start.1 = (f32[64,128]{1,0:T(8,128)S(1)}, f32[64,128]{1,0:T(8,128)S(1)}, u32[]{:S(2)}, u32[]{:S(2)}) collective-permute-start(f32[64,128]{1,0:T(8,128)S(1)} %get-tuple-element.9), channel_id=1, source_target_pairs={{0,16},{16,0},{32,48},{48,32},{64,80},{80,64},{96,112},{112,96},{1... | collective-permute-start | bytes 98312 | tf_op jit(solution)/shard_map/ppermute | solution.py:190
  134.9 4.7 %collective-permute-start.2 = (f32[64,128]{1,0:T(8,128)S(1)}, f32[64,128]{1,0:T(8,128)S(1)}, u32[]{:S(2)}, u32[]{:S(2)}) collective-permute-start(f32[64,128]{1,0:T(8,128)S(1)} %shard_map.108.mine_ref), channel_id=1, source_target_pairs={{0,16},{16,0},{32,48},{48,32},{64,80},{80,64},{96,112},{112,96},{1... | collective-permute-start | bytes 98312 | tf_op jit(solution)/shard_map/ppermute | solution.py:196
Sparse Core Ops, SparseCore 0:
  28.9 39.7 all-gather.2

commit v2 on v1

v2 whole, which is shorter than its diff:
```python
import functools
import math

import jax
import jax.numpy as jnp
from jax import lax
from jax.experimental import pallas as pl
from jax.experimental.pallas import tpu as pltpu
from jax.sharding import PartitionSpec as P

clip_factor = 0.5
learn_rate = 0.05
epsilon = 1e-08

N_Y, N_HI, N_CORE = 8, 2, 2
bf16, f32 = jnp.bfloat16, jnp.float32
VMEM = pl.BlockSpec(memory_space=pltpu.VMEM)
SMEM = pl.BlockSpec(memory_space=pltpu.SMEM)
HBM = pl.BlockSpec(memory_space=pltpu.HBM)
MIB = 1 << 20


def wide_at(y, hi, core):
    return (y * N_HI + hi) * N_CORE + core


YC_GROUPS = [
    [wide_at(y, h, c) for y in range(N_Y) for c in range(N_CORE)] for h in range(N_HI)
]
YZ_GROUPS = [[wide_at(y, h, c) for y in range(N_Y) for h in range(N_HI)] for c in range(N_CORE)]
CORE_SWAP = [(w, w ^ 1) for w in range(N_Y * N_HI * N_CORE)]


def chip_pairs(owners):
    return [
        [wide_at(y, h, c) * owners + n for n in range(owners) for c in range(N_CORE)]
        for y in range(N_Y)
        for h in range(N_HI)
    ]


def call(body, out_shape, in_specs, scratch=(), flops=0, nbytes=0, limit=16):
    return pl.pallas_call(
        body,
        out_shape=out_shape,
        in_specs=in_specs,
        out_specs=jax.tree.map(lambda _: VMEM, out_shape),
        scratch_shapes=list(scratch),
        compiler_params=pltpu.CompilerParams(vmem_limit_bytes=limit * MIB),
        cost_estimate=pl.CostEstimate(flops=flops, bytes_accessed=nbytes, transcendentals=0),
    )


def piece_body(at_ref, first_ref, second_ref, out_ref, held, sems):
    core, y = at_ref[0], at_ref[1]
    half = first_ref.shape[0] // N_CORE
    top = pl.multiple_of(core * half, 32)
    low = pl.multiple_of(core * half + (y % 2) * 16, 16)
    copies = [
        pltpu.make_async_copy(
            first_ref.at[pl.ds(top, half), pl.ds(pl.multiple_of(y * 128, 128), 128)],
            held.at[pl.ds(0, half), :],
            sems.at[0],
        ),
        pltpu.make_async_copy(
            second_ref.at[pl.ds(low, 16), pl.ds(pl.multiple_of((y // 2) * 128, 128), 128)],
            held.at[pl.ds(half, 16), :],
            sems.at[1],
        ),
    ]
    for copy in copies:
        copy.start()
    for copy in copies:
        copy.wait()
    for n in range(out_ref.shape[0]):
        out_ref[n] = held[...]


def tower_body(pieces_ref, pooled_ref, cot_ref, bias_ref, grad_ref, first, second, deltas, sems):
    owners, rows, inner = first.shape
    half = rows // N_CORE
    copies = []
    for y in range(N_Y):
        for c in range(N_CORE):
            p = y * N_CORE + c
            copies.append(
                pltpu.make_async_copy(
                    pieces_ref.at[p, :, pl.ds(0, half), :],
                    first.at[:, pl.ds(c * half, half), pl.ds(y * 128, 128)],
                    sems.at[0, p],
                )
            )
            copies.append(
                pltpu.make_async_copy(
                    pieces_ref.at[p, :, pl.ds(half, 16), :],
                    second.at[:, pl.ds(c * half + (y % 2) * 16, 16), pl.ds((y // 2) * 128, 128)],
                    sems.at[1, p],
                )
            )
    for copy in copies:
        copy.start()
    for copy in copies:
        copy.wait()
    step = 256
    across = (((1,), (1,)), ((), ()))
    per = step // rows
    for k in range(inner // step):
        cols = slice(k * step, (k + 1) * step)
        columns = first[:, :, cols].reshape(owners * rows, step)
        units = second[k * per : (k + 1) * per].reshape(step, second.shape[2])
        hidden = jnp.dot(pooled_ref[...], columns, preferred_element_type=f32) + bias_ref[:, cols]
        back = lax.dot_general(cot_ref[...], units, across, preferred_element_type=f32)
        gate = jax.nn.sigmoid(hidden)
        deltas[:, cols] = (back * (gate * (1.0 + hidden * (1.0 - gate)))).astype(bf16)
    for k in range(owners * rows // step):
        features = first[k * per : (k + 1) * per].reshape(step, inner)
        grad_ref[:, k * step : (k + 1) * step] = lax.dot_general(
            deltas[...], features, across, preferred_element_type=f32
        ).astype(bf16)


def partial_body(counts_ref, grad_ref, out_ref):
    owners, tables, act, bags = counts_ref.shape
    emb = grad_ref.shape[1] // tables
    per = tables // N_CORE
    for t in range(tables):
        lookups = counts_ref[:, t, :, :].reshape(owners * act, bags)
        part = jnp.dot(lookups, grad_ref[:, t * emb : (t + 1) * emb], preferred_element_type=f32)
        at = (t % per) * emb
        out_ref[:, t // per, :, at : at + emb] = part.reshape(owners, act, emb).astype(bf16)


def clip_body(scale, limit, parts_ref, out_ref, rows):
    owners, cores, act, width = parts_ref.shape
    emb = rows.shape[1]
    for c in range(cores):
        total = parts_ref[0, c].astype(f32)
        for n in range(1, owners):
            total = total + parts_ref[n, c].astype(f32)
        total = total * scale
        for t in range(width // emb):
            grads = total[:, t * emb : (t + 1) * emb]
            norms = jnp.sqrt(jnp.sum(grads * grads, axis=-1, keepdims=True))
            clipped = grads * (limit / jnp.maximum(norms, limit))
            at = slice(t * act, (t + 1) * act)
            rows[at, :] = clipped if c == 0 else rows[at, :] + clipped
    both = rows[...].astype(bf16)
    for n in range(out_ref.shape[0]):
        out_ref[n] = both


def share_body(parts_ref, out_ref):
    total = parts_ref[0].astype(f32)
    for n in range(1, parts_ref.shape[0]):
        total = total + parts_ref[n].astype(f32)
    out_ref[...] = total


def update_body(core_ref, ids_ref, mine_ref, other_ref, table_ref, accum_ref, new_table_ref, new_accum_ref, dense):
    tables, act = ids_ref.shape
    per_core = tables // 2
    core = core_ref[0]
    dense[...] = jnp.zeros_like(dense)
    for ref, side in ((mine_ref, core), (other_ref, 1 - core)):
        for t in range(per_core):
            for a in range(act):
                table = side * per_core + t
                row = ids_ref[table, a]
                dense[table, pl.ds(row, 1), :] = ref[pl.ds(t * act + a, 1), :]
    for t in range(tables):
        summed = dense[t]
        new_acc = accum_ref[t] + summed * summed
        new_accum_ref[t] = new_acc
        new_table_ref[t] = table_ref[t] - learn_rate * summed / (jnp.sqrt(new_acc) + epsilon)


def shards(pooled, cotangent, w_first, b_first, w_second, counts, row_ids, table, accum):
    tables, act, bags = counts.shape
    emb = table.shape[2]
    samples = pooled.shape[0]
    inner, top = w_first.shape[1], w_second.shape[1]
    owners = lax.axis_size("narrow")
    scale = 1.0 / math.sqrt(bags)
    limit = clip_factor * math.sqrt(emb)
    wide = lax.axis_index("wide").astype(jnp.int32)
    core = jnp.bitwise_and(wide, N_CORE - 1)
    y = jnp.right_shift(wide, 2)
    core_at = core.reshape(1)
    half = w_first.shape[0] // N_CORE

    piece = call(
        piece_body,
        jax.ShapeDtypeStruct((owners, half + 16, 128), bf16),
        [SMEM, HBM, HBM],
        [pltpu.VMEM((half + 16, 128), bf16), pltpu.SemaphoreType.DMA((2,))],
        nbytes=MIB // 4,
        limit=2,
    )(jnp.stack([core, y]), w_first, w_second)
    spread = lax.all_to_all(piece, "narrow", 0, 0, tiled=True)
    by_owner = jnp.transpose(counts.reshape(tables, act, owners, samples), (2, 0, 1, 3))
    by_owner, spread = lax.optimization_barrier((by_owner, spread))
    pieces = lax.all_gather(spread, "wide", axis=0, axis_index_groups=YC_GROUPS)
    regrouped = lax.all_to_all(by_owner, "narrow", 0, 0, tiled=True)

    grad_in = call(
        tower_body,
        jax.ShapeDtypeStruct((samples, owners * w_first.shape[0]), bf16),
        [HBM] + [VMEM] * 3,
        [
            pltpu.VMEM((owners, w_first.shape[0], inner), bf16),
            pltpu.VMEM((owners, w_second.shape[0], top), bf16),
            pltpu.VMEM((samples, inner), bf16),
            pltpu.SemaphoreType.DMA((2, N_Y * N_CORE)),
        ],
        flops=2 * samples * inner * (2 * inner + top),
        nbytes=8 * MIB,
    )(pieces, pooled, cotangent, b_first.reshape(1, -1))

    parts = call(
        partial_body,
        jax.ShapeDtypeStruct((owners, N_CORE, act, tables // N_CORE * emb), bf16),
        [VMEM] * 2,
        flops=2 * owners * act * samples * tables * emb,
        nbytes=4 * MIB,
    )(regrouped, grad_in)
    arrived = lax.all_to_all(
        parts.reshape(owners * N_CORE, act, -1),
        ("wide", "narrow"),
        0,
        0,
        axis_index_groups=chip_pairs(owners),
        tiled=True,
    )

    half_rows = tables * act // N_CORE
    copies = call(
        functools.partial(clip_body, scale, limit),
        jax.ShapeDtypeStruct((N_Y * N_HI, half_rows, emb), bf16),
        [VMEM],
        [pltpu.VMEM((half_rows, emb), f32)],
        nbytes=MIB,
    )(arrived.reshape(parts.shape))
    shares = lax.all_to_all(copies, "wide", 0, 0, axis_index_groups=YZ_GROUPS, tiled=True)
    mine = call(share_body, jax.ShapeDtypeStruct((half_rows, emb), f32), [VMEM], nbytes=MIB)(shares)
    theirs = lax.ppermute(mine, "wide", CORE_SWAP)
    whole = jax.ShapeDtypeStruct(table.shape, f32)
    return call(
        update_body,
        (whole, whole),
        [SMEM, SMEM] + [VMEM] * 4,
        [pltpu.VMEM(table.shape, f32)],
        nbytes=2 * MIB,
    )(core_at, row_ids, mine, theirs, table, accum)


def solution(mesh):
    in_specs = (
        P(("wide", "narrow"), None),
        P(("wide", "narrow"), None),
        P("narrow", None),
        P(),
        P("narrow", None),
        P(None, "narrow", "wide"),
        P(None, "narrow"),
        P(None, "narrow", None),
        P(None, "narrow", None),
    )
    out_specs = (P(None, "narrow", None), P(None, "narrow", None))
    return jax.shard_map(shards, mesh=mesh, in_specs=in_specs, out_specs=out_specs, check_vma=False)
```

time: 149 us -> 148 us (level)
  starting transfers between devices: 29.5 us -> 18.5 us
  blocking collectives: 43.1 us -> 49.5 us
  Pallas kernels: 6.11 us -> 7.94 us
    ppermute x2 -> x0, starting transfers between devices: 10.8 us -> none  [the longest x1 6.67 us: shards(): other = lax.ppermute(own, 'wide', CORE_SWAP)]
    all_gather x1, waiting for transfers between devices: 35.5 us -> 41 us  [shards(): pieces = lax.all_gather(spread, 'wide', axis=0, axis_index_groups=YC_GROUPS)]
    ppermute x2 -> x0, waiting for transfers between devices: 4.06 us -> none  [the longest x1 3.23 us: shards(): other = lax.ppermute(own, 'wide', CORE_SWAP)]
    all_to_all x1, blocking collectives: 21.7 us -> 25.3 us  [shards(): lax.all_to_all(copies, 'wide', 0, 0, axis_index_groups=YZ_GROUPS, tiled=T...]
    all_to_all x1, blocking collectives: 21.4 us -> 24.2 us  [shards(): lax.all_to_all(parts.reshape(owners * N_CORE, act, -1), ('wide', 'narrow'...]
    unnamed x16 -> x20, local copies, waits for them, and re-layouts: 4.37 us -> 6.6 us
  transfers between devices with their start and end apart: 6 -> 4, of which waited for: 5 -> 3; matrix products, arithmetic and copies ran while one was open for 2% -> 2% of each run, Pallas kernels for 2% -> 3%
where the time goes in v2:
time: 148 us; the launch traced here: 147 us
  blocking collectives  49.5 us (33%)
  waiting for transfers between devices  46.9 us (32%)
  starting transfers between devices  18.5 us (12%)
  between operations  14.1 us (10%)
  local copies, waits for them, and re-layouts  9.87 us (7%)
  Pallas kernels  7.94 us (5%)
    all_gather x1, waiting for transfers between devices, shards(): pieces = lax.all_gather(spread, 'wide', axis=0, axis_index_groups=YC_GROUPS)  41 us
    all_to_all x1, blocking collectives, shards(): lax.all_to_all(copies, 'wide', 0, 0, axis_index_groups=YZ_GROUPS, tiled=T...  25.3 us
    all_to_all x1, blocking collectives, shards(): lax.all_to_all(parts.reshape(owners * N_CORE, act, -1), ('wide', 'narrow'...  24.2 us
    all_to_all x1, starting transfers between devices, shards(): spread = lax.all_to_all(piece, 'narrow', 0, 0, tiled=True)  10.4 us
    unnamed x20, local copies, waits for them, and re-layouts  6.6 us
    all_to_all x1, waiting for transfers between devices, shards(): spread = lax.all_to_all(piece, 'narrow', 0, 0, tiled=True)  5.1 us
    all_to_all x1, starting transfers between devices, shards(): regrouped = lax.all_to_all(by_owner, 'narrow', 0, 0, tiled=True)  4.38 us
    pallas_call x1, Pallas kernels, shards(): call(tower_body, jax.ShapeDtypeStruct((samples, owners * w_first.shape[0]...  4.05 us
  transfers between devices with their start and end apart: 4, of which 3 were waited for; matrix products, arithmetic and copies ran while one was open for 2% of the time, Pallas kernels for 3%

profile of v2, /device:TPU:1, one launch (start us, length us, event | category | flops | bytes accessed | tf_op | source)
XLA Modules:
  0.0 146.9 jit_solution(10999923882530220009)
XLA Ops:
  7.2 0.1 pad_add_fusion.at_ref
  7.2 0.9 copy-done.2
  8.2 0.8 copy-done.3
  9.0 1.3 shard_map.104
  10.3 10.4 %all-to-all-start = ((bf16[16,48,128]{2,1,0:T(8,128)(2,1)}), bf16[16,48,128]{2,1,0:T(8,128)(2,1)S(1)}, u32[]{:S(2)}, u32[]{:S(2)}) async-start(bf16[16,48,128]{2,1,0:T(8,128)(2,1)} %shard_map.104), calls=%async_computation | async-start | bytes 393216 | tf_op jit(solution)/shard_map/all_to_all | solution.py:199
  20.7 0.0 all-gather.3.cloned.1.call-start
  20.7 3.3 %copy.15 = bf16[8,2,16,8,512]{4,3,1,0,2:T(8,128)(2,1)} copy(bf16[8,2,16,8,512]{4,3,2,1,0:T(8,128)(2,1)} %bitcast.18) | data formatting | bytes 4194304 | tf_op jit(solution)/shard_map/reshape | solution.py:200
  24.0 5.1 %all-to-all-done = bf16[16,48,128]{2,1,0:T(8,128)(2,1)S(1)} async-done(((bf16[16,48,128]{2,1,0:T(8,128)(2,1)}), bf16[16,48,128]{2,1,0:T(8,128)(2,1)S(1)}, u32[]{:S(2)}, u32[]{:S(2)}) %all-to-all-start) | async-done | bytes 196640 | tf_op jit(solution)/shard_map/all_to_all | solution.py:199
  29.1 0.7 copy-done.9
  29.8 0.0 all-gather.3.cloned.1.call-update
  29.8 0.0 copy-start.8
  29.8 4.4 %all-to-all-start.1 = ((bf16[16,8,16,512]{3,2,1,0:T(8,128)(2,1)}), bf16[16,8,16,512]{3,2,1,0:T(8,128)(2,1)S(1)}, u32[]{:S(2)}, u32[]{:S(2)}) async-start(bf16[16,8,16,512]{3,2,1,0:T(8,128)(2,1)} %bitcast.17), calls=%async_computation.1 | async-start | bytes 4194304 | tf_op jit(solution)/shard_map/all_to_all | solution.py:203
  34.2 41.0 %all-gather.3.cloned.1.call-done = bf16[256,48,128]{2,1,0:T(8,128)(2,1)} async-done(((bf16[16,48,128]{2,1,0:T(8,128)(2,1)}), bf16[256,48,128]{2,1,0:T(8,128)(2,1)}) %all-gather.3.cloned.1.call-update) | async-done | bytes 3145744 | tf_op jit(solution)/shard_map/all_gather | solution.py:202
  75.2 0.0 copy-done.8
  75.2 1.9 %copy-done.5 = bf16[256,48,128]{2,1,0:T(8,128)(2,1)S(1)} copy-done((bf16[256,48,128]{2,1,0:T(8,128)(2,1)S(1)}, bf16[256,48,128]{2,1,0:T(8,128)(2,1)}, u32[]{:S(2)}) %copy-start.5) | copy-done | bytes 3145752
  77.1 1.2 copy-done.6
  78.3 1.0 copy-done.7
  79.3 4.1 %shard_map.105.grad_ref = bf16[512,1024]{1,0:T(8,128)(2,1)S(1)} custom-call(bf16[16,16,48,128]{3,2,1,0:T(8,128)(2,1)S(1)} %bitcast.15, bf16[512,1024]{1,0:T(8,128)(2,1)S(1)} %copy-done.6, bf16[512,512]{1,0:T(8,128)(2,1)S(1)} %copy-done.7, f32[1,1024]{1,0:T(1,128)S(1)} %bitcast.16), custom_call_target="tpu_custom_call" | custom-call | flops 2684354560 | bytes 8388608 | tf_op jit(solution)/shard_map/pallas_call | solution.py:205
  83.4 0.0 all-to-all-done.1.counts_ref
  83.4 0.7 shard_map.106
  84.2 0.0 copy-start
  84.2 0.0 copy-start.1
  84.2 0.0 copy-start.4
  84.2 24.2 %all_to_all.20 = bf16[32,16,512]{2,1,0:T(8,128)(2,1)S(1)} all-to-all(bf16[32,16,512]{2,1,0:T(8,128)(2,1)S(1)} %bitcast.13), channel_id=1, replica_groups={{0,16,1,17,2,18,3,19,4,20,5,21,6,22,7,23,8,24,9,25,10,26,11,27,12,28,13..., dimensions={0} | all-to-all | bytes 1048576 | tf_op jit(solution)/shard_map/all_to_all | solution.py:226
  108.5 0.2 shard_map.107
  108.6 25.3 %all_to_all.21.parts_ref = bf16[16,64,128]{2,1,0:T(8,128)(2,1)S(1)} all-to-all(bf16[16,64,128]{2,1,0:T(8,128)(2,1)S(1)} %shard_map.107), channel_id=1, replica_groups={{0,32,64,96,128,160,192,224,256,288,320,352,384,416,448,480},{16,48,80,..., dimensions={0} | all-to-all | bytes 524288 | tf_op jit(solution)/shard_map/all_to_all | solution.py:243
  133.9 3.6 %collective-permute-start = (f32[64,128]{1,0:T(8,128)S(1)}, f32[64,128]{1,0:T(8,128)S(1)}, u32[]{:S(2)}, u32[]{:S(2)}) collective-permute-start(f32[64,128]{1,0:T(8,128)S(1)} %shard_map.108.mine_ref), channel_id=1, source_target_pairs={{0,16},{16,0},{32,48},{48,32},{64,80},{80,64},{96,112},{112,96},{1... | collective-permute-start | bytes 98312 | tf_op jit(solution)/shard_map/ppermute | solution.py:245
  137.6 0.8 collective-permute-done.other_ref
  138.4 0.0 copy-done
  138.4 0.0 copy-done.1
  138.4 0.0 copy-done.4
  138.4 1.6 %shard_map.109 = (f32[8,64,128]{2,1,0:T(8,128)}, f32[8,64,128]{2,1,0:T(8,128)}) custom-call(s32[1]{0:T(128)} %bitcast.core_ref, s32[8,16]{1,0:T(8,128)S(1)} %copy-done.4, f32[64,128]{1,0:T(8,128)S(1)} %shard_map.108.mine_ref, f32[64,128]{1,0:T(8,128)S(1)} %collective-permute-done.other_ref, f32[8,64,128]{2,1,0:T(8,128)S(1)} %copy-done, ...), custom_call_target="tpu_custom_call" | custom-call | bytes 2097152 | tf_op jit(solution)/shard_map/pallas_call | solution.py:247
  (7 shorter events, 0.1 us)
Async XLA Ops:
  7.2 0.9 copy-start.2
  8.1 0.8 copy-start.3
  10.3 18.8 %all-to-all-start = ((bf16[16,48,128]{2,1,0:T(8,128)(2,1)}), bf16[16,48,128]{2,1,0:T(8,128)(2,1)S(1)}, u32[]{:S(2)}, u32[]{:S(2)}) async-start(bf16[16,48,128]{2,1,0:T(8,128)(2,1)} %shard_map.104), calls=%async_computation | async-start | bytes 393216 | tf_op jit(solution)/shard_map/all_to_all | solution.py:199
  20.7 54.5 %all-gather.3.cloned.1.call-start = ((), (), s32[]{:S(2)}) async-start(), calls=%async_computation.4 | async-start | bytes 3342336 | tf_op jit(solution)/shard_map/all_gather | solution.py:202
  29.1 0.7 copy-start.9
  29.8 45.4 %copy-start.8 = (f32[1024]{0:T(1024)S(1)}, f32[1024]{0:T(1024)}, u32[]{:S(2)}) copy-start(f32[1024]{0:T(1024)} %param.12) | copy-start | bytes 12292
  29.8 53.6 %all-to-all-start.1 = ((bf16[16,8,16,512]{3,2,1,0:T(8,128)(2,1)}), bf16[16,8,16,512]{3,2,1,0:T(8,128)(2,1)S(1)}, u32[]{:S(2)}, u32[]{:S(2)}) async-start(bf16[16,8,16,512]{3,2,1,0:T(8,128)(2,1)} %bitcast.17), calls=%async_computation.1 | async-start | bytes 4194304 | tf_op jit(solution)/shard_map/all_to_all | solution.py:203
  75.2 1.9 %copy-start.5 = (bf16[256,48,128]{2,1,0:T(8,128)(2,1)S(1)}, bf16[256,48,128]{2,1,0:T(8,128)(2,1)}, u32[]{:S(2)}) copy-start(bf16[256,48,128]{2,1,0:T(8,128)(2,1)} %all-gather.3.cloned.1.call-done) | copy-start | bytes 9437188
  77.1 1.2 copy-start.6
  78.3 1.0 copy-start.7
  84.2 54.3 %copy-start = (f32[8,64,128]{2,1,0:T(8,128)S(1)}, f32[8,64,128]{2,1,0:T(8,128)}, u32[]{:S(2)}) copy-start(f32[8,64,128]{2,1,0:T(8,128)} %table_ref.1) | copy-start | bytes 786436
  84.2 54.3 %copy-start.1 = (f32[8,64,128]{2,1,0:T(8,128)S(1)}, f32[8,64,128]{2,1,0:T(8,128)}, u32[]{:S(2)}) copy-start(f32[8,64,128]{2,1,0:T(8,128)} %accum_ref.1) | copy-start | bytes 786436
  84.2 54.2 %copy-start.4 = (s32[8,16]{1,0:T(8,128)S(1)}, s32[8,16]{1,0:T(8,128)}, u32[]{:S(2)}) copy-start(s32[8,16]{1,0:T(8,128)} %ids_ref.1) | copy-start | bytes 1540
  133.9 4.5 %collective-permute-start = (f32[64,128]{1,0:T(8,128)S(1)}, f32[64,128]{1,0:T(8,128)S(1)}, u32[]{:S(2)}, u32[]{:S(2)}) collective-permute-start(f32[64,128]{1,0:T(8,128)S(1)} %shard_map.108.mine_ref), channel_id=1, source_target_pairs={{0,16},{16,0},{32,48},{48,32},{64,80},{80,64},{96,112},{112,96},{1... | collective-permute-start | bytes 98312 | tf_op jit(solution)/shard_map/ppermute | solution.py:245
Sparse Core Ops, SparseCore 0:
  29.9 45.2 all-gather.2

commit v3 on v2

--- a/solution.py
+++ b/solution.py
@@ -24,11 +24,14 @@
     return (y * N_HI + hi) * N_CORE + core
 
 
-YC_GROUPS = [
-    [wide_at(y, h, c) for y in range(N_Y) for c in range(N_CORE)] for h in range(N_HI)
-]
 YZ_GROUPS = [[wide_at(y, h, c) for y in range(N_Y) for h in range(N_HI)] for c in range(N_CORE)]
 CORE_SWAP = [(w, w ^ 1) for w in range(N_Y * N_HI * N_CORE)]
+RING = [
+    (wide_at(y, h, c), wide_at((y + 1 - 2 * c) % N_Y, h, c))
+    for y in range(N_Y)
+    for h in range(N_HI)
+    for c in range(N_CORE)
+]
 
 
 def chip_pairs(owners):
@@ -76,27 +79,36 @@
         out_ref[n] = held[...]
 
 
-def tower_body(pieces_ref, pooled_ref, cot_ref, bias_ref, grad_ref, first, second, deltas, sems):
+def tower_body(at_ref, *refs):
+    pieces, (pooled_ref, cot_ref, bias_ref, grad_ref, first, second, deltas, sems) = refs[:9], refs[9:]
+    core, y = at_ref[0], at_ref[1]
     owners, rows, inner = first.shape
     half = rows // N_CORE
+    whole, ahead, swapped = pieces[0], pieces[1:5], pieces[5:9]
+    blocks = [(whole.at[0], 0, core), (whole.at[1], 0, 1 - core)]
+    for k in range(1, 4):
+        for part in range(N_CORE):
+            blocks.append((ahead[k - 1].at[part], (2 * core - 1) * k, core if part == 0 else 1 - core))
+            blocks.append((swapped[k - 1].at[part], (1 - 2 * core) * k, 1 - core if part == 0 else core))
+    blocks.append((ahead[3], 4, core))
+    blocks.append((swapped[3], 4, 1 - core))
     copies = []
-    for y in range(N_Y):
-        for c in range(N_CORE):
-            p = y * N_CORE + c
-            copies.append(
-                pltpu.make_async_copy(
-                    pieces_ref.at[p, :, pl.ds(0, half), :],
-                    first.at[:, pl.ds(c * half, half), pl.ds(y * 128, 128)],
-                    sems.at[0, p],
-                )
+    for p, (ref, shift, side) in enumerate(blocks):
+        source = jnp.bitwise_and(y + shift + N_Y, N_Y - 1)
+        top = pl.multiple_of(side * half, 32)
+        low = pl.multiple_of(side * half + jnp.bitwise_and(source, 1) * 16, 16)
+        units = pl.multiple_of(source * 128, 128)
+        tops = pl.multiple_of(jnp.right_shift(source, 1) * 128, 128)
+        copies.append(
+            pltpu.make_async_copy(
+                ref.at[:, pl.ds(0, half), :], first.at[:, pl.ds(top, half), pl.ds(units, 128)], sems.at[0, p]
             )
-            copies.append(
-                pltpu.make_async_copy(
-                    pieces_ref.at[p, :, pl.ds(half, 16), :],
-                    second.at[:, pl.ds(c * half + (y % 2) * 16, 16), pl.ds((y // 2) * 128, 128)],
-                    sems.at[1, p],
-                )
+        )
+        copies.append(
+            pltpu.make_async_copy(
+                ref.at[:, pl.ds(half, 16), :], second.at[:, pl.ds(low, 16), pl.ds(tops, 128)], sems.at[1, p]
             )
+        )
     for copy in copies:
         copy.start()
     for copy in copies:
@@ -188,6 +200,7 @@
     core_at = core.reshape(1)
     half = w_first.shape[0] // N_CORE
 
+    place = jnp.stack([core, y])
     piece = call(
         piece_body,
         jax.ShapeDtypeStruct((owners, half + 16, 128), bf16),
@@ -195,17 +208,23 @@
         [pltpu.VMEM((half + 16, 128), bf16), pltpu.SemaphoreType.DMA((2,))],
         nbytes=MIB // 4,
         limit=2,
-    )(jnp.stack([core, y]), w_first, w_second)
+    )(place, w_first, w_second)
     spread = lax.all_to_all(piece, "narrow", 0, 0, tiled=True)
     by_owner = jnp.transpose(counts.reshape(tables, act, owners, samples), (2, 0, 1, 3))
     by_owner, spread = lax.optimization_barrier((by_owner, spread))
-    pieces = lax.all_gather(spread, "wide", axis=0, axis_index_groups=YC_GROUPS)
     regrouped = lax.all_to_all(by_owner, "narrow", 0, 0, tiled=True)
+
+    ring = [jnp.stack([spread, lax.ppermute(spread, "wide", CORE_SWAP)])]
+    swapped = []
+    for k in range(1, 5):
+        sent = ring[-1] if k < 4 else ring[-1][0]
+        ring.append(lax.ppermute(sent, "wide", RING))
+        swapped.append(lax.ppermute(ring[-1], "wide", CORE_SWAP))
 
     grad_in = call(
         tower_body,
         jax.ShapeDtypeStruct((samples, owners * w_first.shape[0]), bf16),
-        [HBM] + [VMEM] * 3,
+        [SMEM] + [HBM] * 9 + [VMEM] * 3,
         [
             pltpu.VMEM((owners, w_first.shape[0], inner), bf16),
             pltpu.VMEM((owners, w_second.shape[0], top), bf16),
@@ -214,7 +233,7 @@
         ],
         flops=2 * samples * inner * (2 * inner + top),
         nbytes=8 * MIB,
-    )(pieces, pooled, cotangent, b_first.reshape(1, -1))
+    )(place, *ring, *swapped, pooled, cotangent, b_first.reshape(1, -1))
 
     parts = call(
         partial_body,

time: 148 us -> 144 us (0.973)
  starting transfers between devices: 18.5 us -> 55.7 us
  waiting for transfers between devices: 46.9 us -> 18.2 us
  between operations: 14.1 us -> 0.83 us
  local copies, waits for them, and re-layouts: 9.87 us -> 7.29 us
  blocking collectives: 49.5 us -> 52 us
    all_gather x1 -> x0, waiting for transfers between devices: 41 us -> none  [shards(): pieces = lax.all_gather(spread, 'wide', axis=0, axis_index_groups=YC_GROUPS)]
    ppermute x0 -> x9, starting transfers between devices: none -> 37.1 us  [the longest x4 20.7 us: shards(): ring.append(lax.ppermute(sent, 'wide', RING))]
    ppermute x0 -> x9, waiting for transfers between devices: none -> 12.2 us  [the longest x4 10.1 us: shards(): ring.append(lax.ppermute(sent, 'wide', RING))]
    unnamed x20 -> x16, local copies, waits for them, and re-layouts: 6.6 us -> 4.03 us
    all_to_all x1, blocking collectives: 25.3 us -> 27.8 us  [shards(): lax.all_to_all(copies, 'wide', 0, 0, axis_index_groups=YZ_GROUPS, tiled=T...]
  transfers between devices with their start and end apart: 4 -> 12, of which waited for: 3 -> 8; matrix products, arithmetic and copies ran while one was open for 2% -> 2% of each run, Pallas kernels for 3% -> 3%
where the time goes in v3:
time: 144 us; the launch traced here: 143 us
  starting transfers between devices  55.7 us (39%)
  blocking collectives  52 us (36%)
  waiting for transfers between devices  18.2 us (13%)
  Pallas kernels  8.6 us (6%)
  local copies, waits for them, and re-layouts  7.29 us (5%)
    all_to_all x1, blocking collectives, shards(): lax.all_to_all(copies, 'wide', 0, 0, axis_index_groups=YZ_GROUPS, tiled=T...  27.8 us
    all_to_all x1, blocking collectives, shards(): lax.all_to_all(parts.reshape(owners * N_CORE, act, -1), ('wide', 'narrow'...  24.2 us
    ppermute x4, starting transfers between devices, shards(): ring.append(lax.ppermute(sent, 'wide', RING))  20.7 us
    ppermute x4, starting transfers between devices, shards(): swapped.append(lax.ppermute(ring[-1], 'wide', CORE_SWAP))  13 us
    all_to_all x1, starting transfers between devices, shards(): spread = lax.all_to_all(piece, 'narrow', 0, 0, tiled=True)  10.4 us
    ppermute x4, waiting for transfers between devices, shards(): ring.append(lax.ppermute(sent, 'wide', RING))  10.1 us
    all_to_all x1, waiting for transfers between devices, shards(): spread = lax.all_to_all(piece, 'narrow', 0, 0, tiled=True)  5.17 us
    pallas_call x1, Pallas kernels, shards(): call(tower_body, jax.ShapeDtypeStruct((samples, owners * w_first.shape[0]...  4.71 us
  transfers between devices with their start and end apart: 12, of which 8 were waited for; matrix products, arithmetic and copies ran while one was open for 2% of the time, Pallas kernels for 3%

profile of v3, /device:TPU:1, one launch (start us, length us, event | category | flops | bytes accessed | tf_op | source)
XLA Modules:
  0.0 142.7 jit_solution(3662596076096841840)
XLA Ops:
  0.7 0.9 copy-done.2
  1.6 0.8 copy-done.3
  2.5 1.3 shard_map.104
  3.7 10.4 %all-to-all-start = ((bf16[16,48,128]{2,1,0:T(8,128)(2,1)}), bf16[16,48,128]{2,1,0:T(8,128)(2,1)S(1)}, u32[]{:S(2)}, u32[]{:S(2)}) async-start(bf16[16,48,128]{2,1,0:T(8,128)(2,1)} %shard_map.104), calls=%async_computation | async-start | bytes 393216 | tf_op jit(solution)/shard_map/all_to_all | solution.py:212
  14.1 3.2 %copy.14 = bf16[8,2,16,8,512]{4,3,1,0,2:T(8,128)(2,1)} copy(bf16[8,2,16,8,512]{4,3,2,1,0:T(8,128)(2,1)} %bitcast.20) | data formatting | bytes 4194304 | tf_op jit(solution)/shard_map/reshape | solution.py:213
  17.4 5.2 %all-to-all-done = bf16[16,48,128]{2,1,0:T(8,128)(2,1)S(1)} async-done(((bf16[16,48,128]{2,1,0:T(8,128)(2,1)}), bf16[16,48,128]{2,1,0:T(8,128)(2,1)S(1)}, u32[]{:S(2)}, u32[]{:S(2)}) %all-to-all-start) | async-done | bytes 196640 | tf_op jit(solution)/shard_map/all_to_all | solution.py:212
  22.6 4.5 %all-to-all-start.1 = ((bf16[16,8,16,512]{3,2,1,0:T(8,128)(2,1)}), bf16[16,8,16,512]{3,2,1,0:T(8,128)(2,1)S(1)}, u32[]{:S(2)}, u32[]{:S(2)}) async-start(bf16[16,8,16,512]{3,2,1,0:T(8,128)(2,1)} %bitcast.19), calls=%async_computation.1 | async-start | bytes 4194304 | tf_op jit(solution)/shard_map/all_to_all | solution.py:215
  27.1 3.4 %collective-permute-start = (bf16[16,48,128]{2,1,0:T(8,128)(2,1)S(1)}, bf16[16,48,128]{2,1,0:T(8,128)(2,1)S(1)}, u32[]{:S(2)}, u32[]{:S(2)}) collective-permute-start(bf16[16,48,128]{2,1,0:T(8,128)(2,1)S(1)} %all-to-all-done), channel_id=1, source_target_pairs={{0,16},{16,0},{32,48},{48,32},{64,80},{80,64},{96,112},{112,96},{1... | collective-permute-start | bytes 589832 | tf_op jit(solution)/shard_map/ppermute | solution.py:217
  30.5 1.0 collective-permute-done
  31.6 5.1 %collective-permute-start.1 = (bf16[2,16,48,128]{3,2,1,0:T(8,128)(2,1)S(1)}, bf16[2,16,48,128]{3,2,1,0:T(8,128)(2,1)S(1)}, u32[]{:S(2)}, u32[]{:S(2)}) collective-permute-start(bf16[2,16,48,128]{3,2,1,0:T(8,128)(2,1)S(1)} %pad_maximum_fusion.refs_0_), channel_id=1, source_target_pairs={{0,64},{16,464},{32,96},{48,496},{64,128},{80,16},{96,160},{112,48... | collective-permute-start | bytes 1179656 | tf_op jit(solution)/shard_map/ppermute | solution.py:221
  36.7 4.7 %collective-permute-done.1.refs_1_ = bf16[2,16,48,128]{3,2,1,0:T(8,128)(2,1)S(1)} collective-permute-done((bf16[2,16,48,128]{3,2,1,0:T(8,128)(2,1)S(1)}, bf16[2,16,48,128]{3,2,1,0:T(8,128)(2,1)S(1)}, u32[]{:S(2)}, u32[]{:S(2)}) %collective-permute-start.1) | collective-permute-done | bytes 393248 | tf_op jit(solution)/shard_map/ppermute | solution.py:221
  41.4 5.3 %collective-permute-start.2 = (bf16[2,16,48,128]{3,2,1,0:T(8,128)(2,1)S(1)}, bf16[2,16,48,128]{3,2,1,0:T(8,128)(2,1)S(1)}, u32[]{:S(2)}, u32[]{:S(2)}) collective-permute-start(bf16[2,16,48,128]{3,2,1,0:T(8,128)(2,1)S(1)} %collective-permute-done.1.refs_1_), channel_id=1, source_target_pairs={{0,64},{16,464},{32,96},{48,496},{64,128},{80,16},{96,160},{112,48... | collective-permute-start | bytes 1179656 | tf_op jit(solution)/shard_map/ppermute | solution.py:221
  46.7 4.7 %collective-permute-done.2.refs_2_ = bf16[2,16,48,128]{3,2,1,0:T(8,128)(2,1)S(1)} collective-permute-done((bf16[2,16,48,128]{3,2,1,0:T(8,128)(2,1)S(1)}, bf16[2,16,48,128]{3,2,1,0:T(8,128)(2,1)S(1)}, u32[]{:S(2)}, u32[]{:S(2)}) %collective-permute-start.2) | collective-permute-done | bytes 393248 | tf_op jit(solution)/shard_map/ppermute | solution.py:221
  51.4 5.3 %collective-permute-start.3 = (bf16[2,16,48,128]{3,2,1,0:T(8,128)(2,1)S(1)}, bf16[2,16,48,128]{3,2,1,0:T(8,128)(2,1)S(1)}, u32[]{:S(2)}, u32[]{:S(2)}) collective-permute-start(bf16[2,16,48,128]{3,2,1,0:T(8,128)(2,1)S(1)} %collective-permute-done.2.refs_2_), channel_id=1, source_target_pairs={{0,64},{16,464},{32,96},{48,496},{64,128},{80,16},{96,160},{112,48... | collective-permute-start | bytes 1179656 | tf_op jit(solution)/shard_map/ppermute | solution.py:221
  56.7 1.9 %collective-permute-start.5 = (bf16[2,16,48,128]{3,2,1,0:T(8,128)(2,1)S(1)}, bf16[2,16,48,128]{3,2,1,0:T(8,128)(2,1)S(1)}, u32[]{:S(2)}, u32[]{:S(2)}) collective-permute-start(bf16[2,16,48,128]{3,2,1,0:T(8,128)(2,1)S(1)} %collective-permute-done.1.refs_1_), channel_id=1, source_target_pairs={{0,16},{16,0},{32,48},{48,32},{64,80},{80,64},{96,112},{112,96},{1... | collective-permute-start | bytes 1179656 | tf_op jit(solution)/shard_map/ppermute | solution.py:222
  58.7 2.4 %collective-permute-start.6 = (bf16[2,16,48,128]{3,2,1,0:T(8,128)(2,1)S(1)}, bf16[2,16,48,128]{3,2,1,0:T(8,128)(2,1)S(1)}, u32[]{:S(2)}, u32[]{:S(2)}) collective-permute-start(bf16[2,16,48,128]{3,2,1,0:T(8,128)(2,1)S(1)} %collective-permute-done.2.refs_2_), channel_id=1, source_target_pairs={{0,16},{16,0},{32,48},{48,32},{64,80},{80,64},{96,112},{112,96},{1... | collective-permute-start | bytes 1179656 | tf_op jit(solution)/shard_map/ppermute | solution.py:222
  61.1 0.4 collective-permute-done.3.refs_3_
  61.4 5.0 %collective-permute-start.4 = (bf16[16,48,128]{2,1,0:T(8,128)(2,1)S(1)}, bf16[16,48,128]{2,1,0:T(8,128)(2,1)S(1)}, u32[]{:S(2)}, u32[]{:S(2)}) collective-permute-start(bf16[16,48,128]{2,1,0:T(8,128)(2,1)S(1)} %slice_bitcast_fusion), channel_id=1, source_target_pairs={{0,64},{16,464},{32,96},{48,496},{64,128},{80,16},{96,160},{112,48... | collective-permute-start | bytes 589832 | tf_op jit(solution)/shard_map/ppermute | solution.py:221
  66.5 2.2 %collective-permute-start.7 = (bf16[2,16,48,128]{3,2,1,0:T(8,128)(2,1)S(1)}, bf16[2,16,48,128]{3,2,1,0:T(8,128)(2,1)S(1)}, u32[]{:S(2)}, u32[]{:S(2)}) collective-permute-start(bf16[2,16,48,128]{3,2,1,0:T(8,128)(2,1)S(1)} %collective-permute-done.3.refs_3_), channel_id=1, source_target_pairs={{0,16},{16,0},{32,48},{48,32},{64,80},{80,64},{96,112},{112,96},{1... | collective-permute-start | bytes 1179656 | tf_op jit(solution)/shard_map/ppermute | solution.py:222
  68.7 0.4 collective-permute-done.4.refs_4_
  69.1 6.4 %collective-permute-start.8 = (bf16[16,48,128]{2,1,0:T(8,128)(2,1)S(1)}, bf16[16,48,128]{2,1,0:T(8,128)(2,1)S(1)}, u32[]{:S(2)}, u32[]{:S(2)}) collective-permute-start(bf16[16,48,128]{2,1,0:T(8,128)(2,1)S(1)} %collective-permute-done.4.refs_4_), channel_id=1, source_target_pairs={{0,16},{16,0},{32,48},{48,32},{64,80},{80,64},{96,112},{112,96},{1... | collective-permute-start | bytes 589832 | tf_op jit(solution)/shard_map/ppermute | solution.py:222
  75.6 1.0 collective-permute-done.8.refs_8_
  76.6 1.2 copy-done.5
  77.8 1.0 copy-done.6
  78.8 4.7 %shard_map.105.grad_ref = bf16[512,1024]{1,0:T(8,128)(2,1)S(1)} custom-call(s32[2]{0:T(128)S(1)} %pad_add_fusion.at_ref, bf16[2,16,48,128]{3,2,1,0:T(8,128)(2,1)S(1)} %pad_maximum_fusion.refs_0_, bf16[2,16,48,128]{3,2,1,0:T(8,128)(2,1)S(1)} %collective-permute-done.1.refs_1_, bf16[2,16,48,128]{3,2,1,0:T(8,128)(2,1)S(1)} %collective-permute-done.2.refs_2_, ...), custom_call_target="tpu_custom_call" | custom-call | flops 2684354560 | bytes 8388608 | tf_op jit(solution)/shard_map/pallas_call | solution.py:224
  83.6 0.7 shard_map.106
  84.4 24.2 %all_to_all.20 = bf16[32,16,512]{2,1,0:T(8,128)(2,1)S(1)} all-to-all(bf16[32,16,512]{2,1,0:T(8,128)(2,1)S(1)} %bitcast.16), channel_id=1, replica_groups={{0,16,1,17,2,18,3,19,4,20,5,21,6,22,7,23,8,24,9,25,10,26,11,27,12,28,13..., dimensions={0} | all-to-all | bytes 1048576 | tf_op jit(solution)/shard_map/all_to_all | solution.py:245
  108.6 0.2 shard_map.107
  108.8 27.8 %all_to_all.21.parts_ref = bf16[16,64,128]{2,1,0:T(8,128)(2,1)S(1)} all-to-all(bf16[16,64,128]{2,1,0:T(8,128)(2,1)S(1)} %shard_map.107), channel_id=1, replica_groups={{0,32,64,96,128,160,192,224,256,288,320,352,384,416,448,480},{16,48,80,..., dimensions={0} | all-to-all | bytes 524288 | tf_op jit(solution)/shard_map/all_to_all | solution.py:262
  136.6 3.6 %collective-permute-start.9 = (f32[64,128]{1,0:T(8,128)S(1)}, f32[64,128]{1,0:T(8,128)S(1)}, u32[]{:S(2)}, u32[]{:S(2)}) collective-permute-start(f32[64,128]{1,0:T(8,128)S(1)} %shard_map.108.mine_ref), channel_id=1, source_target_pairs={{0,16},{16,0},{32,48},{48,32},{64,80},{80,64},{96,112},{112,96},{1... | collective-permute-start | bytes 98312 | tf_op jit(solution)/shard_map/ppermute | solution.py:264
  140.2 0.8 collective-permute-done.9.other_ref
  141.1 1.6 %shard_map.109 = (f32[8,64,128]{2,1,0:T(8,128)}, f32[8,64,128]{2,1,0:T(8,128)}) custom-call(s32[1]{0:T(128)} %bitcast.core_ref, s32[8,16]{1,0:T(8,128)S(1)} %copy-done.4, f32[64,128]{1,0:T(8,128)S(1)} %shard_map.108.mine_ref, f32[64,128]{1,0:T(8,128)S(1)} %collective-permute-done.9.other_ref, f32[8,64,128]{2,1,0:T(8,128)S(1)} %copy-done, ...), custom_call_target="tpu_custom_call" | custom-call | bytes 2097152 | tf_op jit(solution)/shard_map/pallas_call | solution.py:266
  (20 shorter events, 0.2 us)
Async XLA Ops:
  0.7 0.9 copy-start.2
  1.6 0.8 copy-start.3
  3.7 18.8 %all-to-all-start = ((bf16[16,48,128]{2,1,0:T(8,128)(2,1)}), bf16[16,48,128]{2,1,0:T(8,128)(2,1)S(1)}, u32[]{:S(2)}, u32[]{:S(2)}) async-start(bf16[16,48,128]{2,1,0:T(8,128)(2,1)} %shard_map.104), calls=%async_computation | async-start | bytes 393216 | tf_op jit(solution)/shard_map/all_to_all | solution.py:212
  22.6 54.0 %copy-start.7 = (f32[1024]{0:T(1024)S(1)}, f32[1024]{0:T(1024)}, u32[]{:S(2)}) copy-start(f32[1024]{0:T(1024)} %param.12) | copy-start | bytes 12292
  22.6 61.0 %all-to-all-start.1 = ((bf16[16,8,16,512]{3,2,1,0:T(8,128)(2,1)}), bf16[16,8,16,512]{3,2,1,0:T(8,128)(2,1)S(1)}, u32[]{:S(2)}, u32[]{:S(2)}) async-start(bf16[16,8,16,512]{3,2,1,0:T(8,128)(2,1)} %bitcast.19), calls=%async_computation.1 | async-start | bytes 4194304 | tf_op jit(solution)/shard_map/all_to_all | solution.py:215
  27.1 4.5 %collective-permute-start = (bf16[16,48,128]{2,1,0:T(8,128)(2,1)S(1)}, bf16[16,48,128]{2,1,0:T(8,128)(2,1)S(1)}, u32[]{:S(2)}, u32[]{:S(2)}) collective-permute-start(bf16[16,48,128]{2,1,0:T(8,128)(2,1)S(1)} %all-to-all-done), channel_id=1, source_target_pairs={{0,16},{16,0},{32,48},{48,32},{64,80},{80,64},{96,112},{112,96},{1... | collective-permute-start | bytes 589832 | tf_op jit(solution)/shard_map/ppermute | solution.py:217
  31.6 9.8 %collective-permute-start.1 = (bf16[2,16,48,128]{3,2,1,0:T(8,128)(2,1)S(1)}, bf16[2,16,48,128]{3,2,1,0:T(8,128)(2,1)S(1)}, u32[]{:S(2)}, u32[]{:S(2)}) collective-permute-start(bf16[2,16,48,128]{3,2,1,0:T(8,128)(2,1)S(1)} %pad_maximum_fusion.refs_0_), channel_id=1, source_target_pairs={{0,64},{16,464},{32,96},{48,496},{64,128},{80,16},{96,160},{112,48... | collective-permute-start | bytes 1179656 | tf_op jit(solution)/shard_map/ppermute | solution.py:221
  41.4 10.0 %collective-permute-start.2 = (bf16[2,16,48,128]{3,2,1,0:T(8,128)(2,1)S(1)}, bf16[2,16,48,128]{3,2,1,0:T(8,128)(2,1)S(1)}, u32[]{:S(2)}, u32[]{:S(2)}) collective-permute-start(bf16[2,16,48,128]{3,2,1,0:T(8,128)(2,1)S(1)} %collective-permute-done.1.refs_1_), channel_id=1, source_target_pairs={{0,64},{16,464},{32,96},{48,496},{64,128},{80,16},{96,160},{112,48... | collective-permute-start | bytes 1179656 | tf_op jit(solution)/shard_map/ppermute | solution.py:221
  51.4 10.0 %collective-permute-start.3 = (bf16[2,16,48,128]{3,2,1,0:T(8,128)(2,1)S(1)}, bf16[2,16,48,128]{3,2,1,0:T(8,128)(2,1)S(1)}, u32[]{:S(2)}, u32[]{:S(2)}) collective-permute-start(bf16[2,16,48,128]{3,2,1,0:T(8,128)(2,1)S(1)} %collective-permute-done.2.refs_2_), channel_id=1, source_target_pairs={{0,64},{16,464},{32,96},{48,496},{64,128},{80,16},{96,160},{112,48... | collective-permute-start | bytes 1179656 | tf_op jit(solution)/shard_map/ppermute | solution.py:221
  56.7 18.8 %collective-permute-start.5 = (bf16[2,16,48,128]{3,2,1,0:T(8,128)(2,1)S(1)}, bf16[2,16,48,128]{3,2,1,0:T(8,128)(2,1)S(1)}, u32[]{:S(2)}, u32[]{:S(2)}) collective-permute-start(bf16[2,16,48,128]{3,2,1,0:T(8,128)(2,1)S(1)} %collective-permute-done.1.refs_1_), channel_id=1, source_target_pairs={{0,16},{16,0},{32,48},{48,32},{64,80},{80,64},{96,112},{112,96},{1... | collective-permute-start | bytes 1179656 | tf_op jit(solution)/shard_map/ppermute | solution.py:222
  58.7 16.9 %collective-permute-start.6 = (bf16[2,16,48,128]{3,2,1,0:T(8,128)(2,1)S(1)}, bf16[2,16,48,128]{3,2,1,0:T(8,128)(2,1)S(1)}, u32[]{:S(2)}, u32[]{:S(2)}) collective-permute-start(bf16[2,16,48,128]{3,2,1,0:T(8,128)(2,1)S(1)} %collective-permute-done.2.refs_2_), channel_id=1, source_target_pairs={{0,16},{16,0},{32,48},{48,32},{64,80},{80,64},{96,112},{112,96},{1... | collective-permute-start | bytes 1179656 | tf_op jit(solution)/shard_map/ppermute | solution.py:222
  61.4 7.6 %collective-permute-start.4 = (bf16[16,48,128]{2,1,0:T(8,128)(2,1)S(1)}, bf16[16,48,128]{2,1,0:T(8,128)(2,1)S(1)}, u32[]{:S(2)}, u32[]{:S(2)}) collective-permute-start(bf16[16,48,128]{2,1,0:T(8,128)(2,1)S(1)} %slice_bitcast_fusion), channel_id=1, source_target_pairs={{0,64},{16,464},{32,96},{48,496},{64,128},{80,16},{96,160},{112,48... | collective-permute-start | bytes 589832 | tf_op jit(solution)/shard_map/ppermute | solution.py:221
  66.5 9.1 %collective-permute-start.7 = (bf16[2,16,48,128]{3,2,1,0:T(8,128)(2,1)S(1)}, bf16[2,16,48,128]{3,2,1,0:T(8,128)(2,1)S(1)}, u32[]{:S(2)}, u32[]{:S(2)}) collective-permute-start(bf16[2,16,48,128]{3,2,1,0:T(8,128)(2,1)S(1)} %collective-permute-done.3.refs_3_), channel_id=1, source_target_pairs={{0,16},{16,0},{32,48},{48,32},{64,80},{80,64},{96,112},{112,96},{1... | collective-permute-start | bytes 1179656 | tf_op jit(solution)/shard_map/ppermute | solution.py:222
  69.1 7.5 %collective-permute-start.8 = (bf16[16,48,128]{2,1,0:T(8,128)(2,1)S(1)}, bf16[16,48,128]{2,1,0:T(8,128)(2,1)S(1)}, u32[]{:S(2)}, u32[]{:S(2)}) collective-permute-start(bf16[16,48,128]{2,1,0:T(8,128)(2,1)S(1)} %collective-permute-done.4.refs_4_), channel_id=1, source_target_pairs={{0,16},{16,0},{32,48},{48,32},{64,80},{80,64},{96,112},{112,96},{1... | collective-permute-start | bytes 589832 | tf_op jit(solution)/shard_map/ppermute | solution.py:222
  76.6 1.2 copy-start.5
  77.8 1.0 copy-start.6
  84.3 56.7 %copy-start = (f32[8,64,128]{2,1,0:T(8,128)S(1)}, f32[8,64,128]{2,1,0:T(8,128)}, u32[]{:S(2)}) copy-start(f32[8,64,128]{2,1,0:T(8,128)} %table_ref.1) | copy-start | bytes 786436
  84.3 56.7 %copy-start.1 = (f32[8,64,128]{2,1,0:T(8,128)S(1)}, f32[8,64,128]{2,1,0:T(8,128)}, u32[]{:S(2)}) copy-start(f32[8,64,128]{2,1,0:T(8,128)} %accum_ref.1) | copy-start | bytes 786436
  84.3 56.7 %copy-start.4 = (s32[8,16]{1,0:T(8,128)S(1)}, s32[8,16]{1,0:T(8,128)}, u32[]{:S(2)}) copy-start(s32[8,16]{1,0:T(8,128)} %ids_ref.1) | copy-start | bytes 1540
  136.6 4.5 %collective-permute-start.9 = (f32[64,128]{1,0:T(8,128)S(1)}, f32[64,128]{1,0:T(8,128)S(1)}, u32[]{:S(2)}, u32[]{:S(2)}) collective-permute-start(f32[64,128]{1,0:T(8,128)S(1)} %shard_map.108.mine_ref), channel_id=1, source_target_pairs={{0,16},{16,0},{32,48},{48,32},{64,80},{80,64},{96,112},{112,96},{1... | collective-permute-start | bytes 98312 | tf_op jit(solution)/shard_map/ppermute | solution.py:264

commit v4 on v3

--- a/solution.py
+++ b/solution.py
@@ -26,12 +26,19 @@
 
 YZ_GROUPS = [[wide_at(y, h, c) for y in range(N_Y) for h in range(N_HI)] for c in range(N_CORE)]
 CORE_SWAP = [(w, w ^ 1) for w in range(N_Y * N_HI * N_CORE)]
-RING = [
-    (wide_at(y, h, c), wide_at((y + 1 - 2 * c) % N_Y, h, c))
-    for y in range(N_Y)
-    for h in range(N_HI)
-    for c in range(N_CORE)
-]
+
+
+def y_shift(by):
+    return [
+        (wide_at(y, h, c), wide_at((y + by - 2 * by * c) % N_Y, h, c))
+        for y in range(N_Y)
+        for h in range(N_HI)
+        for c in range(N_CORE)
+    ]
+
+
+def in_hbm(x):
+    return pltpu.with_memory_space_constraint(x, pltpu.HBM)
 
 
 def chip_pairs(owners):
@@ -80,7 +87,8 @@
 
 
 def tower_body(at_ref, *refs):
-    pieces, (pooled_ref, cot_ref, bias_ref, grad_ref, first, second, deltas, sems) = refs[:9], refs[9:]
+    pieces = refs[:9]
+    pooled_hbm, cot_hbm, bias_ref, grad_ref, first, second, deltas, pooled_ref, cot_ref, sems = refs[9:]
     core, y = at_ref[0], at_ref[1]
     owners, rows, inner = first.shape
     half = rows // N_CORE
@@ -92,7 +100,10 @@
             blocks.append((swapped[k - 1].at[part], (1 - 2 * core) * k, 1 - core if part == 0 else core))
     blocks.append((ahead[3], 4, core))
     blocks.append((swapped[3], 4, 1 - core))
-    copies = []
+    copies = [
+        pltpu.make_async_copy(pooled_hbm, pooled_ref, sems.at[0, len(blocks)]),
+        pltpu.make_async_copy(cot_hbm, cot_ref, sems.at[1, len(blocks)]),
+    ]
     for p, (ref, shift, side) in enumerate(blocks):
         source = jnp.bitwise_and(y + shift + N_Y, N_Y - 1)
         top = pl.multiple_of(side * half, 32)
@@ -208,32 +219,35 @@
         [pltpu.VMEM((half + 16, 128), bf16), pltpu.SemaphoreType.DMA((2,))],
         nbytes=MIB // 4,
         limit=2,
-    )(place, w_first, w_second)
+    )(place, in_hbm(w_first), in_hbm(w_second))
     spread = lax.all_to_all(piece, "narrow", 0, 0, tiled=True)
     by_owner = jnp.transpose(counts.reshape(tables, act, owners, samples), (2, 0, 1, 3))
     by_owner, spread = lax.optimization_barrier((by_owner, spread))
     regrouped = lax.all_to_all(by_owner, "narrow", 0, 0, tiled=True)
 
-    ring = [jnp.stack([spread, lax.ppermute(spread, "wide", CORE_SWAP)])]
-    swapped = []
-    for k in range(1, 5):
-        sent = ring[-1] if k < 4 else ring[-1][0]
-        ring.append(lax.ppermute(sent, "wide", RING))
-        swapped.append(lax.ppermute(ring[-1], "wide", CORE_SWAP))
+    whole = jnp.stack([spread, lax.ppermute(spread, "wide", CORE_SWAP)])
+    ahead2 = lax.ppermute(whole, "wide", y_shift(2))
+    ahead1 = lax.ppermute(whole, "wide", y_shift(1))
+    ahead3 = lax.ppermute(ahead2, "wide", y_shift(1))
+    ahead4 = lax.ppermute(ahead2[0], "wide", y_shift(2))
+    ring = [ahead1, ahead2, ahead3, ahead4]
+    swapped = [lax.ppermute(block, "wide", CORE_SWAP) for block in ring]
 
     grad_in = call(
         tower_body,
         jax.ShapeDtypeStruct((samples, owners * w_first.shape[0]), bf16),
-        [SMEM] + [HBM] * 9 + [VMEM] * 3,
+        [SMEM] + [HBM] * 11 + [VMEM],
         [
             pltpu.VMEM((owners, w_first.shape[0], inner), bf16),
             pltpu.VMEM((owners, w_second.shape[0], top), bf16),
             pltpu.VMEM((samples, inner), bf16),
-            pltpu.SemaphoreType.DMA((2, N_Y * N_CORE)),
+            pltpu.VMEM(pooled.shape, bf16),
+            pltpu.VMEM(cotangent.shape, bf16),
+            pltpu.SemaphoreType.DMA((2, N_Y * N_CORE + 1)),
         ],
         flops=2 * samples * inner * (2 * inner + top),
         nbytes=8 * MIB,
-    )(place, *ring, *swapped, pooled, cotangent, b_first.reshape(1, -1))
+    )(place, whole, *ring, *swapped, in_hbm(pooled), in_hbm(cotangent), b_first.reshape(1, -1))
 
     parts = call(
         partial_body,

time: 144 us -> 133 us (0.924)
  starting transfers between devices: 55.7 us -> 49.8 us
  waiting for transfers between devices: 18.2 us -> 14 us
  local copies, waits for them, and re-layouts: 7.29 us -> 3.3 us
  blocking collectives: 52 us -> 54.1 us
    ppermute x9, starting transfers between devices: 37.1 us -> 31.3 us  [the longest x4 10.9 us: shards(): swapped = [lax.ppermute(block, 'wide', CORE_SWAP) for block in ring]]
    ppermute x9, waiting for transfers between devices: 12.2 us -> 8.05 us  [the longest x1 5.93 us: shards(): ahead2 = lax.ppermute(whole, 'wide', y_shift(2))]
    unnamed x16 -> x8, local copies, waits for them, and re-layouts: 4.03 us -> 0.02 us
    all_to_all x1, blocking collectives: 24.2 us -> 26 us  [shards(): lax.all_to_all(parts.reshape(owners * N_CORE, act, -1), ('wide', 'narrow'...]
  transfers between devices with their start and end apart: 12 -> 12, of which waited for: 8 -> 5; matrix products, arithmetic and copies ran while one was open for 2% -> 3% of each run, Pallas kernels for 3% -> 4%
where the time goes in v4:
time: 133 us; the launch traced here: 132 us
  blocking collectives  54.1 us (41%)
  starting transfers between devices  49.8 us (37%)
  waiting for transfers between devices  14 us (11%)
  Pallas kernels  9.74 us (7%)
  local copies, waits for them, and re-layouts  3.3 us (2%)
    all_to_all x1, blocking collectives, shards(): lax.all_to_all(copies, 'wide', 0, 0, axis_index_groups=YZ_GROUPS, tiled=T...  28 us
    all_to_all x1, blocking collectives, shards(): lax.all_to_all(parts.reshape(owners * N_CORE, act, -1), ('wide', 'narrow'...  26 us
    ppermute x4, starting transfers between devices, shards(): swapped = [lax.ppermute(block, 'wide', CORE_SWAP) for block in ring]  10.9 us
    all_to_all x1, starting transfers between devices, shards(): spread = lax.all_to_all(piece, 'narrow', 0, 0, tiled=True)  10.4 us
    ppermute x1, waiting for transfers between devices, shards(): ahead2 = lax.ppermute(whole, 'wide', y_shift(2))  5.93 us
    ppermute x1, starting transfers between devices, shards(): ahead2 = lax.ppermute(whole, 'wide', y_shift(2))  5.89 us
    pallas_call x1, Pallas kernels, shards(): call(tower_body, jax.ShapeDtypeStruct((samples, owners * w_first.shape[0]...  5.17 us
    all_to_all x1, waiting for transfers between devices, shards(): spread = lax.all_to_all(piece, 'narrow', 0, 0, tiled=True)  5.16 us
  transfers between devices with their start and end apart: 12, of which 5 were waited for; matrix products, arithmetic and copies ran while one was open for 3% of the time, Pallas kernels for 4%

profile of v4, /device:TPU:1, one launch (start us, length us, event | category | flops | bytes accessed | tf_op | source)
XLA Modules:
  0.0 131.9 jit_solution(12271597841086969205)
XLA Ops:
  0.6 0.1 pad_add_fusion.at_ref
  0.7 2.0 %shard_map.104 = bf16[16,48,128]{2,1,0:T(8,128)(2,1)} custom-call(s32[2]{0:T(128)S(1)} %pad_add_fusion.at_ref, bf16[64,1024]{1,0:T(8,128)(2,1)} %first_ref.1, bf16[64,512]{1,0:T(8,128)(2,1)} %second_ref.1), custom_call_target="tpu_custom_call" | custom-call | bytes 262144 | tf_op jit(solution)/shard_map/pallas_call | solution.py:215
  2.7 10.4 %all-to-all-start = ((bf16[16,48,128]{2,1,0:T(8,128)(2,1)}), bf16[16,48,128]{2,1,0:T(8,128)(2,1)S(1)}, u32[]{:S(2)}, u32[]{:S(2)}) async-start(bf16[16,48,128]{2,1,0:T(8,128)(2,1)} %shard_map.104), calls=%async_computation | async-start | bytes 393216 | tf_op jit(solution)/shard_map/all_to_all | solution.py:223
  13.1 3.3 %copy.14 = bf16[8,2,16,8,512]{4,3,1,0,2:T(8,128)(2,1)} copy(bf16[8,2,16,8,512]{4,3,2,1,0:T(8,128)(2,1)} %bitcast.20) | data formatting | bytes 4194304 | tf_op jit(solution)/shard_map/reshape | solution.py:224
  16.3 5.2 %all-to-all-done = bf16[16,48,128]{2,1,0:T(8,128)(2,1)S(1)} async-done(((bf16[16,48,128]{2,1,0:T(8,128)(2,1)}), bf16[16,48,128]{2,1,0:T(8,128)(2,1)S(1)}, u32[]{:S(2)}, u32[]{:S(2)}) %all-to-all-start) | async-done | bytes 196640 | tf_op jit(solution)/shard_map/all_to_all | solution.py:223
  21.5 4.5 %all-to-all-start.1 = ((bf16[16,8,16,512]{3,2,1,0:T(8,128)(2,1)}), bf16[16,8,16,512]{3,2,1,0:T(8,128)(2,1)S(1)}, u32[]{:S(2)}, u32[]{:S(2)}) async-start(bf16[16,8,16,512]{3,2,1,0:T(8,128)(2,1)} %bitcast.19), calls=%async_computation.1 | async-start | bytes 4194304 | tf_op jit(solution)/shard_map/all_to_all | solution.py:226
  26.0 3.4 %collective-permute-start = (bf16[16,48,128]{2,1,0:T(8,128)(2,1)S(1)}, bf16[16,48,128]{2,1,0:T(8,128)(2,1)S(1)}, u32[]{:S(2)}, u32[]{:S(2)}) collective-permute-start(bf16[16,48,128]{2,1,0:T(8,128)(2,1)S(1)} %all-to-all-done), channel_id=1, source_target_pairs={{0,16},{16,0},{32,48},{48,32},{64,80},{80,64},{96,112},{112,96},{1... | collective-permute-start | bytes 589832 | tf_op jit(solution)/shard_map/ppermute | solution.py:228
  29.4 1.0 collective-permute-done
  30.5 5.9 %collective-permute-start.2 = (bf16[2,16,48,128]{3,2,1,0:T(8,128)(2,1)S(1)}, bf16[2,16,48,128]{3,2,1,0:T(8,128)(2,1)S(1)}, u32[]{:S(2)}, u32[]{:S(2)}) collective-permute-start(bf16[2,16,48,128]{3,2,1,0:T(8,128)(2,1)S(1)} %pad_maximum_fusion.refs_0_), channel_id=1, source_target_pairs={{0,128},{16,400},{32,160},{48,432},{64,192},{80,464},{96,224},{112... | collective-permute-start | bytes 1179656 | tf_op jit(solution)/shard_map/ppermute | solution.py:229
  36.4 3.0 %collective-permute-start.1 = (bf16[2,16,48,128]{3,2,1,0:T(8,128)(2,1)S(1)}, bf16[2,16,48,128]{3,2,1,0:T(8,128)(2,1)S(1)}, u32[]{:S(2)}, u32[]{:S(2)}) collective-permute-start(bf16[2,16,48,128]{3,2,1,0:T(8,128)(2,1)S(1)} %pad_maximum_fusion.refs_0_), channel_id=1, source_target_pairs={{0,64},{16,464},{32,96},{48,496},{64,128},{80,16},{96,160},{112,48... | collective-permute-start | bytes 1179656 | tf_op jit(solution)/shard_map/ppermute | solution.py:230
  39.4 5.9 %collective-permute-done.2.refs_2_ = bf16[2,16,48,128]{3,2,1,0:T(8,128)(2,1)S(1)} collective-permute-done((bf16[2,16,48,128]{3,2,1,0:T(8,128)(2,1)S(1)}, bf16[2,16,48,128]{3,2,1,0:T(8,128)(2,1)S(1)}, u32[]{:S(2)}, u32[]{:S(2)}) %collective-permute-start.2) | collective-permute-done | bytes 393248 | tf_op jit(solution)/shard_map/ppermute | solution.py:229
  45.3 4.4 %collective-permute-start.3 = (bf16[2,16,48,128]{3,2,1,0:T(8,128)(2,1)S(1)}, bf16[2,16,48,128]{3,2,1,0:T(8,128)(2,1)S(1)}, u32[]{:S(2)}, u32[]{:S(2)}) collective-permute-start(bf16[2,16,48,128]{3,2,1,0:T(8,128)(2,1)S(1)} %collective-permute-done.2.refs_2_), channel_id=1, source_target_pairs={{0,64},{16,464},{32,96},{48,496},{64,128},{80,16},{96,160},{112,48... | collective-permute-start | bytes 1179656 | tf_op jit(solution)/shard_map/ppermute | solution.py:231
  49.7 3.8 %collective-permute-start.4 = (bf16[16,48,128]{2,1,0:T(8,128)(2,1)S(1)}, bf16[16,48,128]{2,1,0:T(8,128)(2,1)S(1)}, u32[]{:S(2)}, u32[]{:S(2)}) collective-permute-start(bf16[16,48,128]{2,1,0:T(8,128)(2,1)S(1)} %slice_bitcast_fusion), channel_id=1, source_target_pairs={{0,128},{16,400},{32,160},{48,432},{64,192},{80,464},{96,224},{112... | collective-permute-start | bytes 589832 | tf_op jit(solution)/shard_map/ppermute | solution.py:232
  53.5 2.1 %collective-permute-start.6 = (bf16[2,16,48,128]{3,2,1,0:T(8,128)(2,1)S(1)}, bf16[2,16,48,128]{3,2,1,0:T(8,128)(2,1)S(1)}, u32[]{:S(2)}, u32[]{:S(2)}) collective-permute-start(bf16[2,16,48,128]{3,2,1,0:T(8,128)(2,1)S(1)} %collective-permute-done.2.refs_2_), channel_id=1, source_target_pairs={{0,16},{16,0},{32,48},{48,32},{64,80},{80,64},{96,112},{112,96},{1... | collective-permute-start | bytes 1179656 | tf_op jit(solution)/shard_map/ppermute | solution.py:234
  55.6 2.2 %collective-permute-start.5 = (bf16[2,16,48,128]{3,2,1,0:T(8,128)(2,1)S(1)}, bf16[2,16,48,128]{3,2,1,0:T(8,128)(2,1)S(1)}, u32[]{:S(2)}, u32[]{:S(2)}) collective-permute-start(bf16[2,16,48,128]{3,2,1,0:T(8,128)(2,1)S(1)} %collective-permute-done.1.refs_1_), channel_id=1, source_target_pairs={{0,16},{16,0},{32,48},{48,32},{64,80},{80,64},{96,112},{112,96},{1... | collective-permute-start | bytes 1179656 | tf_op jit(solution)/shard_map/ppermute | solution.py:234
  57.9 2.1 %collective-permute-start.7 = (bf16[2,16,48,128]{3,2,1,0:T(8,128)(2,1)S(1)}, bf16[2,16,48,128]{3,2,1,0:T(8,128)(2,1)S(1)}, u32[]{:S(2)}, u32[]{:S(2)}) collective-permute-start(bf16[2,16,48,128]{3,2,1,0:T(8,128)(2,1)S(1)} %collective-permute-done.3.refs_3_), channel_id=1, source_target_pairs={{0,16},{16,0},{32,48},{48,32},{64,80},{80,64},{96,112},{112,96},{1... | collective-permute-start | bytes 1179656 | tf_op jit(solution)/shard_map/ppermute | solution.py:234
  60.0 0.0 collective-permute-done.4.refs_4_
  60.0 4.5 %collective-permute-start.8 = (bf16[16,48,128]{2,1,0:T(8,128)(2,1)S(1)}, bf16[16,48,128]{2,1,0:T(8,128)(2,1)S(1)}, u32[]{:S(2)}, u32[]{:S(2)}) collective-permute-start(bf16[16,48,128]{2,1,0:T(8,128)(2,1)S(1)} %collective-permute-done.4.refs_4_), channel_id=1, source_target_pairs={{0,16},{16,0},{32,48},{48,32},{64,80},{80,64},{96,112},{112,96},{1... | collective-permute-start | bytes 589832 | tf_op jit(solution)/shard_map/ppermute | solution.py:234
  64.4 1.0 collective-permute-done.8.refs_8_
  65.5 0.0 collective-permute-done.7.refs_7_
  65.5 5.2 %shard_map.105.grad_ref = bf16[512,1024]{1,0:T(8,128)(2,1)S(1)} custom-call(s32[2]{0:T(128)S(1)} %pad_add_fusion.at_ref, bf16[2,16,48,128]{3,2,1,0:T(8,128)(2,1)S(1)} %pad_maximum_fusion.refs_0_, bf16[2,16,48,128]{3,2,1,0:T(8,128)(2,1)S(1)} %collective-permute-done.1.refs_1_, bf16[2,16,48,128]{3,2,1,0:T(8,128)(2,1)S(1)} %collective-permute-done.2.refs_2_, ...), custom_call_target="tpu_custom_call" | custom-call | flops 2684354560 | bytes 8388608 | tf_op jit(solution)/shard_map/pallas_call | solution.py:236
  70.7 0.0 all-to-all-done.1.counts_ref
  70.7 0.7 shard_map.106
  71.4 0.0 copy-start
  71.4 0.0 copy-start.1
  71.5 0.0 copy-start.2
  71.5 26.0 %all_to_all.20 = bf16[32,16,512]{2,1,0:T(8,128)(2,1)S(1)} all-to-all(bf16[32,16,512]{2,1,0:T(8,128)(2,1)S(1)} %bitcast.16), channel_id=1, replica_groups={{0,16,1,17,2,18,3,19,4,20,5,21,6,22,7,23,8,24,9,25,10,26,11,27,12,28,13..., dimensions={0} | all-to-all | bytes 1048576 | tf_op jit(solution)/shard_map/all_to_all | solution.py:259
  97.5 0.2 shard_map.107
  97.7 28.0 %all_to_all.21.parts_ref = bf16[16,64,128]{2,1,0:T(8,128)(2,1)S(1)} all-to-all(bf16[16,64,128]{2,1,0:T(8,128)(2,1)S(1)} %shard_map.107), channel_id=1, replica_groups={{0,32,64,96,128,160,192,224,256,288,320,352,384,416,448,480},{16,48,80,..., dimensions={0} | all-to-all | bytes 524288 | tf_op jit(solution)/shard_map/all_to_all | solution.py:276
  125.8 3.6 %collective-permute-start.9 = (f32[64,128]{1,0:T(8,128)S(1)}, f32[64,128]{1,0:T(8,128)S(1)}, u32[]{:S(2)}, u32[]{:S(2)}) collective-permute-start(f32[64,128]{1,0:T(8,128)S(1)} %shard_map.108.mine_ref), channel_id=1, source_target_pairs={{0,16},{16,0},{32,48},{48,32},{64,80},{80,64},{96,112},{112,96},{1... | collective-permute-start | bytes 98312 | tf_op jit(solution)/shard_map/ppermute | solution.py:278
  129.4 0.8 collective-permute-done.9.other_ref
  130.3 1.6 %shard_map.109 = (f32[8,64,128]{2,1,0:T(8,128)}, f32[8,64,128]{2,1,0:T(8,128)}) custom-call(s32[1]{0:T(128)} %bitcast.core_ref, s32[8,16]{1,0:T(8,128)S(1)} %copy-done.2, f32[64,128]{1,0:T(8,128)S(1)} %shard_map.108.mine_ref, f32[64,128]{1,0:T(8,128)S(1)} %collective-permute-done.9.other_ref, f32[8,64,128]{2,1,0:T(8,128)S(1)} %copy-done, ...), custom_call_target="tpu_custom_call" | custom-call | bytes 2097152 | tf_op jit(solution)/shard_map/pallas_call | solution.py:280
  (12 shorter events, 0.1 us)
Async XLA Ops:
  2.7 18.8 %all-to-all-start = ((bf16[16,48,128]{2,1,0:T(8,128)(2,1)}), bf16[16,48,128]{2,1,0:T(8,128)(2,1)S(1)}, u32[]{:S(2)}, u32[]{:S(2)}) async-start(bf16[16,48,128]{2,1,0:T(8,128)(2,1)} %shard_map.104), calls=%async_computation | async-start | bytes 393216 | tf_op jit(solution)/shard_map/all_to_all | solution.py:223
  21.5 44.0 %copy-start.3 = (f32[1024]{0:T(1024)S(1)}, f32[1024]{0:T(1024)}, u32[]{:S(2)}) copy-start(f32[1024]{0:T(1024)} %param.12) | copy-start | bytes 12292
  21.5 49.2 %all-to-all-start.1 = ((bf16[16,8,16,512]{3,2,1,0:T(8,128)(2,1)}), bf16[16,8,16,512]{3,2,1,0:T(8,128)(2,1)S(1)}, u32[]{:S(2)}, u32[]{:S(2)}) async-start(bf16[16,8,16,512]{3,2,1,0:T(8,128)(2,1)} %bitcast.19), calls=%async_computation.1 | async-start | bytes 4194304 | tf_op jit(solution)/shard_map/all_to_all | solution.py:226
  26.0 4.5 %collective-permute-start = (bf16[16,48,128]{2,1,0:T(8,128)(2,1)S(1)}, bf16[16,48,128]{2,1,0:T(8,128)(2,1)S(1)}, u32[]{:S(2)}, u32[]{:S(2)}) collective-permute-start(bf16[16,48,128]{2,1,0:T(8,128)(2,1)S(1)} %all-to-all-done), channel_id=1, source_target_pairs={{0,16},{16,0},{32,48},{48,32},{64,80},{80,64},{96,112},{112,96},{1... | collective-permute-start | bytes 589832 | tf_op jit(solution)/shard_map/ppermute | solution.py:228
  30.5 14.8 %collective-permute-start.2 = (bf16[2,16,48,128]{3,2,1,0:T(8,128)(2,1)S(1)}, bf16[2,16,48,128]{3,2,1,0:T(8,128)(2,1)S(1)}, u32[]{:S(2)}, u32[]{:S(2)}) collective-permute-start(bf16[2,16,48,128]{3,2,1,0:T(8,128)(2,1)S(1)} %pad_maximum_fusion.refs_0_), channel_id=1, source_target_pairs={{0,128},{16,400},{32,160},{48,432},{64,192},{80,464},{96,224},{112... | collective-permute-start | bytes 1179656 | tf_op jit(solution)/shard_map/ppermute | solution.py:229
  36.4 19.2 %collective-permute-start.1 = (bf16[2,16,48,128]{3,2,1,0:T(8,128)(2,1)S(1)}, bf16[2,16,48,128]{3,2,1,0:T(8,128)(2,1)S(1)}, u32[]{:S(2)}, u32[]{:S(2)}) collective-permute-start(bf16[2,16,48,128]{3,2,1,0:T(8,128)(2,1)S(1)} %pad_maximum_fusion.refs_0_), channel_id=1, source_target_pairs={{0,64},{16,464},{32,96},{48,496},{64,128},{80,16},{96,160},{112,48... | collective-permute-start | bytes 1179656 | tf_op jit(solution)/shard_map/ppermute | solution.py:230
  45.3 12.5 %collective-permute-start.3 = (bf16[2,16,48,128]{3,2,1,0:T(8,128)(2,1)S(1)}, bf16[2,16,48,128]{3,2,1,0:T(8,128)(2,1)S(1)}, u32[]{:S(2)}, u32[]{:S(2)}) collective-permute-start(bf16[2,16,48,128]{3,2,1,0:T(8,128)(2,1)S(1)} %collective-permute-done.2.refs_2_), channel_id=1, source_target_pairs={{0,64},{16,464},{32,96},{48,496},{64,128},{80,16},{96,160},{112,48... | collective-permute-start | bytes 1179656 | tf_op jit(solution)/shard_map/ppermute | solution.py:231
  49.7 10.2 %collective-permute-start.4 = (bf16[16,48,128]{2,1,0:T(8,128)(2,1)S(1)}, bf16[16,48,128]{2,1,0:T(8,128)(2,1)S(1)}, u32[]{:S(2)}, u32[]{:S(2)}) collective-permute-start(bf16[16,48,128]{2,1,0:T(8,128)(2,1)S(1)} %slice_bitcast_fusion), channel_id=1, source_target_pairs={{0,128},{16,400},{32,160},{48,432},{64,192},{80,464},{96,224},{112... | collective-permute-start | bytes 589832 | tf_op jit(solution)/shard_map/ppermute | solution.py:232
  53.5 12.0 %collective-permute-start.6 = (bf16[2,16,48,128]{3,2,1,0:T(8,128)(2,1)S(1)}, bf16[2,16,48,128]{3,2,1,0:T(8,128)(2,1)S(1)}, u32[]{:S(2)}, u32[]{:S(2)}) collective-permute-start(bf16[2,16,48,128]{3,2,1,0:T(8,128)(2,1)S(1)} %collective-permute-done.2.refs_2_), channel_id=1, source_target_pairs={{0,16},{16,0},{32,48},{48,32},{64,80},{80,64},{96,112},{112,96},{1... | collective-permute-start | bytes 1179656 | tf_op jit(solution)/shard_map/ppermute | solution.py:234
  55.6 9.9 %collective-permute-start.5 = (bf16[2,16,48,128]{3,2,1,0:T(8,128)(2,1)S(1)}, bf16[2,16,48,128]{3,2,1,0:T(8,128)(2,1)S(1)}, u32[]{:S(2)}, u32[]{:S(2)}) collective-permute-start(bf16[2,16,48,128]{3,2,1,0:T(8,128)(2,1)S(1)} %collective-permute-done.1.refs_1_), channel_id=1, source_target_pairs={{0,16},{16,0},{32,48},{48,32},{64,80},{80,64},{96,112},{112,96},{1... | collective-permute-start | bytes 1179656 | tf_op jit(solution)/shard_map/ppermute | solution.py:234
  57.9 7.6 %collective-permute-start.7 = (bf16[2,16,48,128]{3,2,1,0:T(8,128)(2,1)S(1)}, bf16[2,16,48,128]{3,2,1,0:T(8,128)(2,1)S(1)}, u32[]{:S(2)}, u32[]{:S(2)}) collective-permute-start(bf16[2,16,48,128]{3,2,1,0:T(8,128)(2,1)S(1)} %collective-permute-done.3.refs_3_), channel_id=1, source_target_pairs={{0,16},{16,0},{32,48},{48,32},{64,80},{80,64},{96,112},{112,96},{1... | collective-permute-start | bytes 1179656 | tf_op jit(solution)/shard_map/ppermute | solution.py:234
  60.0 5.5 %collective-permute-start.8 = (bf16[16,48,128]{2,1,0:T(8,128)(2,1)S(1)}, bf16[16,48,128]{2,1,0:T(8,128)(2,1)S(1)}, u32[]{:S(2)}, u32[]{:S(2)}) collective-permute-start(bf16[16,48,128]{2,1,0:T(8,128)(2,1)S(1)} %collective-permute-done.4.refs_4_), channel_id=1, source_target_pairs={{0,16},{16,0},{32,48},{48,32},{64,80},{80,64},{96,112},{112,96},{1... | collective-permute-start | bytes 589832 | tf_op jit(solution)/shard_map/ppermute | solution.py:234
  71.4 58.8 %copy-start = (f32[8,64,128]{2,1,0:T(8,128)S(1)}, f32[8,64,128]{2,1,0:T(8,128)}, u32[]{:S(2)}) copy-start(f32[8,64,128]{2,1,0:T(8,128)} %table_ref.1) | copy-start | bytes 786436
  71.4 58.8 %copy-start.1 = (f32[8,64,128]{2,1,0:T(8,128)S(1)}, f32[8,64,128]{2,1,0:T(8,128)}, u32[]{:S(2)}) copy-start(f32[8,64,128]{2,1,0:T(8,128)} %accum_ref.1) | copy-start | bytes 786436
  71.5 58.8 %copy-start.2 = (s32[8,16]{1,0:T(8,128)S(1)}, s32[8,16]{1,0:T(8,128)}, u32[]{:S(2)}) copy-start(s32[8,16]{1,0:T(8,128)} %ids_ref.1) | copy-start | bytes 1540
  125.8 4.5 %collective-permute-start.9 = (f32[64,128]{1,0:T(8,128)S(1)}, f32[64,128]{1,0:T(8,128)S(1)}, u32[]{:S(2)}, u32[]{:S(2)}) collective-permute-start(f32[64,128]{1,0:T(8,128)S(1)} %shard_map.108.mine_ref), channel_id=1, source_target_pairs={{0,16},{16,0},{32,48},{48,32},{64,80},{80,64},{96,112},{112,96},{1... | collective-permute-start | bytes 98312 | tf_op jit(solution)/shard_map/ppermute | solution.py:278

commit v5 on v4

v5 whole, which is shorter than its diff:
```python
import functools
import math

import jax
import jax.numpy as jnp
from jax import lax
from jax.experimental import pallas as pl
from jax.experimental.pallas import tpu as pltpu
from jax.sharding import PartitionSpec as P

clip_factor = 0.5
learn_rate = 0.05
epsilon = 1e-08

N_Y, N_HI, N_CORE = 8, 2, 2
bf16, f32 = jnp.bfloat16, jnp.float32
VMEM = pl.BlockSpec(memory_space=pltpu.VMEM)
SMEM = pl.BlockSpec(memory_space=pltpu.SMEM)
HBM = pl.BlockSpec(memory_space=pltpu.HBM)
MIB = 1 << 20


def wide_at(y, hi, core):
    return (y * N_HI + hi) * N_CORE + core


CORE_SWAP = [(w, w ^ 1) for w in range(N_Y * N_HI * N_CORE)]


def y_shift(by):
    return [
        (wide_at(y, h, c), wide_at((y + by - 2 * by * c) % N_Y, h, c))
        for y in range(N_Y)
        for h in range(N_HI)
        for c in range(N_CORE)
    ]


def in_hbm(x):
    return pltpu.with_memory_space_constraint(x, pltpu.HBM)


def quads(owners):
    return [
        [wide_at(y, h, c) * owners + n for c in range(N_CORE) for h in range(N_HI) for n in range(owners)]
        for y in range(N_Y)
    ]


WIDE_ORDER = [
    [wide_at(y, h, c) for c in range(N_CORE) for h in range(N_HI) for y in range(N_Y)]
]
N_X = 4


def offset_of(y, core):
    return 2 * (1 - core) if y < 4 else 1 + 2 * core, y % N_X


def shard_moves(owners):
    n_z = owners // N_X
    moves = []
    for y in range(N_Y):
        for h in range(N_HI):
            for c in range(N_CORE):
                dz, dx = offset_of(y, c)
                for z in range(n_z):
                    for x in range(N_X):
                        to = (z + dz) % n_z * N_X + (x + dx) % N_X
                        base = wide_at(y, h, c) * owners
                        moves.append((base + z * N_X + x, base + to))
    return moves


def call(body, out_shape, in_specs, scratch=(), flops=0, nbytes=0, limit=16):
    return pl.pallas_call(
        body,
        out_shape=out_shape,
        in_specs=in_specs,
        out_specs=jax.tree.map(lambda _: VMEM, out_shape),
        scratch_shapes=list(scratch),
        compiler_params=pltpu.CompilerParams(vmem_limit_bytes=limit * MIB),
        cost_estimate=pl.CostEstimate(flops=flops, bytes_accessed=nbytes, transcendentals=0),
    )


def join_body(first_ref, second_ref, out_ref, sems):
    inner = first_ref.shape[1]
    copies = [
        pltpu.make_async_copy(first_ref, out_ref.at[:, pl.ds(0, inner)], sems.at[0]),
        pltpu.make_async_copy(second_ref, out_ref.at[:, pl.ds(inner, second_ref.shape[1])], sems.at[1]),
    ]
    for copy in copies:
        copy.start()
    for copy in copies:
        copy.wait()


def tower_body(at_ref, *refs):
    whole, ahead, swapped = refs[0], refs[1:5], refs[5:9]
    pooled_hbm, cot_hbm, bias_ref, grad_ref, first, second, deltas, pooled_ref, cot_ref, sems = refs[9:]
    core, y, z, x = at_ref[0], at_ref[1], at_ref[2], at_ref[3]
    owners, rows, inner = first.shape
    top = second.shape[2]
    blocks = [(whole.at[0], 0, core), (whole.at[1], 0, 1 - core)]
    for k in range(1, 4):
        for part in range(N_CORE):
            blocks.append((ahead[k - 1].at[part], (2 * core - 1) * k, core if part == 0 else 1 - core))
            blocks.append((swapped[k - 1].at[part], (1 - 2 * core) * k, 1 - core if part == 0 else core))
    blocks.append((ahead[3], 4, core))
    blocks.append((swapped[3], 4, 1 - core))
    copies = [
        pltpu.make_async_copy(pooled_hbm, pooled_ref, sems.at[0, len(blocks)]),
        pltpu.make_async_copy(cot_hbm, cot_ref, sems.at[1, len(blocks)]),
    ]
    for p, (ref, shift, side) in enumerate(blocks):
        source = jnp.bitwise_and(y + shift + N_Y, N_Y - 1)
        dz = jnp.where(source < 4, 2 * (1 - side), 1 + 2 * side)
        from_z = jnp.bitwise_and(z - dz + 4, owners // N_X - 1)
        from_x = jnp.bitwise_and(x - source + N_Y, N_X - 1)
        owner = from_z * N_X + from_x
        copies.append(pltpu.make_async_copy(ref.at[:, pl.ds(0, inner)], first.at[owner], sems.at[0, p]))
        copies.append(pltpu.make_async_copy(ref.at[:, pl.ds(inner, top)], second.at[owner], sems.at[1, p]))
    for copy in copies:
        copy.start()
    for copy in copies:
        copy.wait()
    step = 256
    across = (((1,), (1,)), ((), ()))
    per = step // rows
    for k in range(inner // step):
        cols = slice(k * step, (k + 1) * step)
        columns = first[:, :, cols].reshape(owners * rows, step)
        units = second[k * per : (k + 1) * per].reshape(step, second.shape[2])
        hidden = jnp.dot(pooled_ref[...], columns, preferred_element_type=f32) + bias_ref[:, cols]
        back = lax.dot_general(cot_ref[...], units, across, preferred_element_type=f32)
        gate = jax.nn.sigmoid(hidden)
        deltas[:, cols] = (back * (gate * (1.0 + hidden * (1.0 - gate)))).astype(bf16)
    for k in range(owners * rows // step):
        features = first[k * per : (k + 1) * per].reshape(step, inner)
        grad_ref[:, k * step : (k + 1) * step] = lax.dot_general(
            deltas[...], features, across, preferred_element_type=f32
        ).astype(bf16)


def partial_body(counts_ref, grad_ref, out_ref):
    owners, tables, act, bags = counts_ref.shape
    emb = grad_ref.shape[1] // tables
    per = tables // out_ref.shape[0]
    for t in range(tables):
        lookups = counts_ref[:, t, :, :].reshape(owners * act, bags)
        part = jnp.dot(lookups, grad_ref[:, t * emb : (t + 1) * emb], preferred_element_type=f32)
        at = (t % per) * emb
        out_ref[t // per, :, :, at : at + emb] = part.reshape(owners, act, emb).astype(bf16)


def clip_body(scale, limit, parts_ref, out_ref, rows):
    groups, owners, act, width = parts_ref.shape
    emb = rows.shape[1]
    for g in range(groups):
        total = parts_ref[g, 0].astype(f32)
        for n in range(1, owners):
            total = total + parts_ref[g, n].astype(f32)
        total = total * scale
        for t in range(width // emb):
            grads = total[:, t * emb : (t + 1) * emb]
            norms = jnp.sqrt(jnp.sum(grads * grads, axis=-1, keepdims=True))
            clipped = grads * (limit / jnp.maximum(norms, limit))
            at = slice(t * act, (t + 1) * act)
            rows[at, :] = clipped if g == 0 else rows[at, :] + clipped
    both = rows[...].astype(bf16)
    for n in range(out_ref.shape[0]):
        out_ref[n] = both


def update_body(ids_ref, shares_ref, table_ref, accum_ref, new_table_ref, new_accum_ref, dense, rows):
    tables, act = ids_ref.shape
    quarters = N_HI * N_CORE
    per = tables // quarters
    dense[...] = jnp.zeros_like(dense)
    for q in range(quarters):
        total = shares_ref[q * N_Y].astype(f32)
        for y in range(1, N_Y):
            total = total + shares_ref[q * N_Y + y].astype(f32)
        rows[...] = total
        for t in range(per):
            table = q * per + t
            for a in range(act):
                row = ids_ref[table, a]
                dense[table, pl.ds(row, 1), :] = rows[pl.ds(t * act + a, 1), :]
    for t in range(tables):
        summed = dense[t]
        new_acc = accum_ref[t] + summed * summed
        new_accum_ref[t] = new_acc
        new_table_ref[t] = table_ref[t] - learn_rate * summed / (jnp.sqrt(new_acc) + epsilon)


def shards(pooled, cotangent, w_first, b_first, w_second, counts, row_ids, table, accum):
    tables, act, bags = counts.shape
    emb = table.shape[2]
    samples = pooled.shape[0]
    inner, top = w_first.shape[1], w_second.shape[1]
    owners = lax.axis_size("narrow")
    scale = 1.0 / math.sqrt(bags)
    limit = clip_factor * math.sqrt(emb)
    wide = lax.axis_index("wide").astype(jnp.int32)
    core = jnp.bitwise_and(wide, N_CORE - 1)
    y = jnp.right_shift(wide, 2)
    narrow = lax.axis_index("narrow").astype(jnp.int32)
    place = jnp.stack([core, y, jnp.right_shift(narrow, 2), jnp.bitwise_and(narrow, N_X - 1)])

    shard = call(
        join_body,
        jax.ShapeDtypeStruct((w_first.shape[0], inner + top), bf16),
        [HBM, HBM],
        [pltpu.SemaphoreType.DMA((2,))],
        nbytes=MIB // 2,
        limit=2,
    )(in_hbm(w_first), in_hbm(w_second))
    moved = lax.ppermute(shard, ("wide", "narrow"), shard_moves(owners))
    by_owner = jnp.transpose(counts.reshape(tables, act, owners, samples), (2, 0, 1, 3))
    by_owner, moved = lax.optimization_barrier((by_owner, moved))
    regrouped = lax.all_to_all(by_owner, "narrow", 0, 0, tiled=True)
    whole = jnp.stack([moved, lax.ppermute(moved, "wide", CORE_SWAP)])
    ahead2 = lax.ppermute(whole, "wide", y_shift(2))
    ahead1 = lax.ppermute(whole, "wide", y_shift(1))
    ahead3 = lax.ppermute(ahead2, "wide", y_shift(1))
    ahead4 = lax.ppermute(ahead2[0], "wide", y_shift(2))
    ring = [ahead1, ahead2, ahead3, ahead4]
    swapped = [lax.ppermute(block, "wide", CORE_SWAP) for block in ring]

    grad_in = call(
        tower_body,
        jax.ShapeDtypeStruct((samples, owners * w_first.shape[0]), bf16),
        [SMEM] + [HBM] * 11 + [VMEM],
        [
            pltpu.VMEM((owners, w_first.shape[0], inner), bf16),
            pltpu.VMEM((owners, w_second.shape[0], top), bf16),
            pltpu.VMEM((samples, inner), bf16),
            pltpu.VMEM(pooled.shape, bf16),
            pltpu.VMEM(cotangent.shape, bf16),
            pltpu.SemaphoreType.DMA((2, N_Y * N_CORE + 1)),
        ],
        flops=2 * samples * inner * (2 * inner + top),
        nbytes=8 * MIB,
    )(place, *map(in_hbm, (whole, *ring, *swapped, pooled, cotangent)), b_first.reshape(1, -1))

    quarters = N_HI * N_CORE
    parts = call(
        partial_body,
        jax.ShapeDtypeStruct((quarters, owners, act, tables // quarters * emb), bf16),
        [VMEM] * 2,
        flops=2 * owners * act * samples * tables * emb,
        nbytes=4 * MIB,
    )(regrouped, grad_in)
    arrived = lax.all_to_all(
        parts.reshape(owners * quarters, act, -1),
        ("wide", "narrow"),
        0,
        0,
        axis_index_groups=quads(owners),
        tiled=True,
    )
    rows = tables * act // quarters
    copies = call(
        functools.partial(clip_body, scale, limit),
        jax.ShapeDtypeStruct((N_Y * quarters, rows, emb), bf16),
        [VMEM],
        [pltpu.VMEM((rows, emb), f32)],
        nbytes=MIB,
    )(arrived.reshape(parts.shape))
    shares = lax.all_to_all(copies, "wide", 0, 0, axis_index_groups=WIDE_ORDER, tiled=True)
    updated = jax.ShapeDtypeStruct(table.shape, f32)
    return call(
        update_body,
        (updated, updated),
        [SMEM] + [VMEM] * 3,
        [pltpu.VMEM(table.shape, f32), pltpu.VMEM((rows, emb), f32)],
        nbytes=2 * MIB,
    )(row_ids, shares, table, accum)


def solution(mesh):
    in_specs = (
        P(("wide", "narrow"), None),
        P(("wide", "narrow"), None),
        P("narrow", None),
        P(),
        P("narrow", None),
        P(None, "narrow", "wide"),
        P(None, "narrow"),
        P(None, "narrow", None),
        P(None, "narrow", None),
    )
    out_specs = (P(None, "narrow", None), P(None, "narrow", None))
    return jax.shard_map(shards, mesh=mesh, in_specs=in_specs, out_specs=out_specs, check_vma=False)
```

time: 133 us -> 127 us (0.955)
  waiting for transfers between devices: 14 us -> 9.06 us
    all_to_all x1 -> x0, starting transfers between devices: 10.4 us -> none  [shards(): spread = lax.all_to_all(piece, 'narrow', 0, 0, tiled=True)]
    all_to_all x1, starting transfers between devices: 4.5 us -> 10.5 us  [shards(): regrouped = lax.all_to_all(by_owner, 'narrow', 0, 0, tiled=True)]
    all_to_all x1 -> x0, waiting for transfers between devices: 5.16 us -> none  [shards(): spread = lax.all_to_all(piece, 'narrow', 0, 0, tiled=True)]
    ppermute x1, starting transfers between devices: 5.89 us -> 8.3 us  [shards(): ahead2 = lax.ppermute(whole, 'wide', y_shift(2))]
    ppermute x2, starting transfers between devices: 7.07 us -> 9.25 us  [the longest x1 8.58 us: shards(): whole = jnp.stack([moved, lax.ppermute(moved, 'wide', CORE_SWAP)])]
    pallas_call x4 -> x3, Pallas kernels: 4.4 us -> 3.27 us  [the longest x1 1.6 us: shards(): call(update_body, (updated, updated), [SMEM] + [VMEM] * 3, [pltpu.VMEM(ta...]
  transfers between devices with their start and end apart: 12 -> 11, of which waited for: 5 -> 3; matrix products, arithmetic and copies ran while one was open for 3% -> 3% of each run, Pallas kernels for 4% -> 5%
where the time goes in v5:
time: 127 us; the launch traced here: 126 us
  blocking collectives  54.3 us (43%)
  starting transfers between devices  49.1 us (39%)
  Pallas kernels  9.48 us (7%)
  waiting for transfers between devices  9.06 us (7%)
  local copies, waits for them, and re-layouts  3.31 us (3%)
    all_to_all x1, blocking collectives, shards(): lax.all_to_all(copies, 'wide', 0, 0, axis_index_groups=WIDE_ORDER, tiled=...  27.6 us
    all_to_all x1, blocking collectives, shards(): lax.all_to_all(parts.reshape(owners * quarters, act, -1), ('wide', 'narro...  26.6 us
    ppermute x4, starting transfers between devices, shards(): swapped = [lax.ppermute(block, 'wide', CORE_SWAP) for block in ring]  11 us
    all_to_all x1, starting transfers between devices, shards(): regrouped = lax.all_to_all(by_owner, 'narrow', 0, 0, tiled=True)  10.5 us
    ppermute x1, starting transfers between devices, shards(): whole = jnp.stack([moved, lax.ppermute(moved, 'wide', CORE_SWAP)])  8.58 us
    ppermute x1, starting transfers between devices, shards(): ahead2 = lax.ppermute(whole, 'wide', y_shift(2))  8.3 us
    ppermute x1, waiting for transfers between devices, shards(): ahead2 = lax.ppermute(whole, 'wide', y_shift(2))  6.54 us
    pallas_call x1, Pallas kernels, shards(): call(tower_body, jax.ShapeDtypeStruct((samples, owners * w_first.shape[0]...  6.04 us
  transfers between devices with their start and end apart: 11, of which 3 were waited for; matrix products, arithmetic and copies ran while one was open for 3% of the time, Pallas kernels for 5%

profile of v5, /device:TPU:1, one launch (start us, length us, event | category | flops | bytes accessed | tf_op | source)
XLA Modules:
  0.0 126.3 jit_solution(2045635998189986036)
XLA Ops:
  0.6 0.9 shard_map.104
  1.6 0.7 collective-permute-start
  2.2 3.3 %copy.14 = bf16[8,2,16,8,512]{4,3,1,0,2:T(8,128)(2,1)} copy(bf16[8,2,16,8,512]{4,3,2,1,0:T(8,128)(2,1)} %bitcast.22) | data formatting | bytes 4194304 | tf_op jit(solution)/shard_map/reshape | solution.py:221
  5.5 10.5 %all-to-all-start = ((bf16[16,8,16,512]{3,2,1,0:T(8,128)(2,1)}), bf16[16,8,16,512]{3,2,1,0:T(8,128)(2,1)S(1)}, u32[]{:S(2)}, u32[]{:S(2)}) async-start(bf16[16,8,16,512]{3,2,1,0:T(8,128)(2,1)} %bitcast.21), calls=%async_computation | async-start | bytes 4194304 | tf_op jit(solution)/shard_map/all_to_all | solution.py:223
  16.0 8.6 %collective-permute-start.1 = (bf16[64,1536]{1,0:T(8,128)(2,1)S(1)}, bf16[64,1536]{1,0:T(8,128)(2,1)S(1)}, u32[]{:S(2)}, u32[]{:S(2)}) collective-permute-start(bf16[64,1536]{1,0:T(8,128)(2,1)S(1)} %collective-permute-done), channel_id=1, source_target_pairs={{0,16},{16,0},{32,48},{48,32},{64,80},{80,64},{96,112},{112,96},{1... | collective-permute-start | bytes 589832 | tf_op jit(solution)/shard_map/ppermute | solution.py:224
  24.6 1.0 collective-permute-done.1
  25.7 8.3 %collective-permute-start.3 = (bf16[2,64,1536]{2,1,0:T(8,128)(2,1)S(1)}, bf16[2,64,1536]{2,1,0:T(8,128)(2,1)S(1)}, u32[]{:S(2)}, u32[]{:S(2)}) collective-permute-start(bf16[2,64,1536]{2,1,0:T(8,128)(2,1)S(1)} %pad_maximum_fusion.refs_0_), channel_id=1, source_target_pairs={{0,128},{16,400},{32,160},{48,432},{64,192},{80,464},{96,224},{112... | collective-permute-start | bytes 1179656 | tf_op jit(solution)/shard_map/ppermute | solution.py:225
  34.0 1.9 %collective-permute-start.2 = (bf16[2,64,1536]{2,1,0:T(8,128)(2,1)S(1)}, bf16[2,64,1536]{2,1,0:T(8,128)(2,1)S(1)}, u32[]{:S(2)}, u32[]{:S(2)}) collective-permute-start(bf16[2,64,1536]{2,1,0:T(8,128)(2,1)S(1)} %pad_maximum_fusion.refs_0_), channel_id=1, source_target_pairs={{0,64},{16,464},{32,96},{48,496},{64,128},{80,16},{96,160},{112,48... | collective-permute-start | bytes 1179656 | tf_op jit(solution)/shard_map/ppermute | solution.py:226
  35.9 6.5 %collective-permute-done.3.refs_2_ = bf16[2,64,1536]{2,1,0:T(8,128)(2,1)S(1)} collective-permute-done((bf16[2,64,1536]{2,1,0:T(8,128)(2,1)S(1)}, bf16[2,64,1536]{2,1,0:T(8,128)(2,1)S(1)}, u32[]{:S(2)}, u32[]{:S(2)}) %collective-permute-start.3) | collective-permute-done | bytes 393248 | tf_op jit(solution)/shard_map/ppermute | solution.py:225
  42.5 4.6 %collective-permute-start.4 = (bf16[2,64,1536]{2,1,0:T(8,128)(2,1)S(1)}, bf16[2,64,1536]{2,1,0:T(8,128)(2,1)}, u32[]{:S(2)}, u32[]{:S(2)}) collective-permute-start(bf16[2,64,1536]{2,1,0:T(8,128)(2,1)S(1)} %collective-permute-done.3.refs_2_), channel_id=1, source_target_pairs={{0,64},{16,464},{32,96},{48,496},{64,128},{80,16},{96,160},{112,48... | collective-permute-start | bytes 1179656 | tf_op jit(solution)/shard_map/ppermute | solution.py:227
  47.1 3.6 %collective-permute-start.5 = (bf16[64,1536]{1,0:T(8,128)(2,1)S(1)}, bf16[64,1536]{1,0:T(8,128)(2,1)S(1)}, u32[]{:S(2)}, u32[]{:S(2)}) collective-permute-start(bf16[64,1536]{1,0:T(8,128)(2,1)S(1)} %slice_bitcast_fusion), channel_id=1, source_target_pairs={{0,128},{16,400},{32,160},{48,432},{64,192},{80,464},{96,224},{112... | collective-permute-start | bytes 589832 | tf_op jit(solution)/shard_map/ppermute | solution.py:228
  50.7 1.9 %collective-permute-start.7 = (bf16[2,64,1536]{2,1,0:T(8,128)(2,1)S(1)}, bf16[2,64,1536]{2,1,0:T(8,128)(2,1)}, u32[]{:S(2)}, u32[]{:S(2)}) collective-permute-start(bf16[2,64,1536]{2,1,0:T(8,128)(2,1)S(1)} %collective-permute-done.3.refs_2_), channel_id=1, source_target_pairs={{0,16},{16,0},{32,48},{48,32},{64,80},{80,64},{96,112},{112,96},{1... | collective-permute-start | bytes 1179656 | tf_op jit(solution)/shard_map/ppermute | solution.py:230
  52.6 0.0 collective-permute-done.2.refs_1_
  52.6 2.4 %collective-permute-start.6 = (bf16[2,64,1536]{2,1,0:T(8,128)(2,1)S(1)}, bf16[2,64,1536]{2,1,0:T(8,128)(2,1)}, u32[]{:S(2)}, u32[]{:S(2)}) collective-permute-start(bf16[2,64,1536]{2,1,0:T(8,128)(2,1)S(1)} %collective-permute-done.2.refs_1_), channel_id=1, source_target_pairs={{0,16},{16,0},{32,48},{48,32},{64,80},{80,64},{96,112},{112,96},{1... | collective-permute-start | bytes 1179656 | tf_op jit(solution)/shard_map/ppermute | solution.py:230
  55.0 4.8 %collective-permute-start.8 = (bf16[2,64,1536]{2,1,0:T(8,128)(2,1)}, bf16[2,64,1536]{2,1,0:T(8,128)(2,1)}, u32[]{:S(2)}, u32[]{:S(2)}) collective-permute-start(bf16[2,64,1536]{2,1,0:T(8,128)(2,1)} %collective-permute-done.4.refs_3_), channel_id=1, source_target_pairs={{0,16},{16,0},{32,48},{48,32},{64,80},{80,64},{96,112},{112,96},{1... | collective-permute-start | bytes 1179656 | tf_op jit(solution)/shard_map/ppermute | solution.py:230
  59.8 0.0 collective-permute-done.5.refs_4_
  59.8 0.0 copy-start.7
  59.8 1.9 %collective-permute-start.9 = (bf16[64,1536]{1,0:T(8,128)(2,1)S(1)}, bf16[64,1536]{1,0:T(8,128)(2,1)}, u32[]{:S(2)}, u32[]{:S(2)}) collective-permute-start(bf16[64,1536]{1,0:T(8,128)(2,1)S(1)} %collective-permute-done.5.refs_4_), channel_id=1, source_target_pairs={{0,16},{16,0},{32,48},{48,32},{64,80},{80,64},{96,112},{112,96},{1... | collective-permute-start | bytes 589832 | tf_op jit(solution)/shard_map/ppermute | solution.py:230
  61.8 0.1 pad_add_fusion.at_ref
  61.8 1.5 %collective-permute-done.9.refs_8_ = bf16[64,1536]{1,0:T(8,128)(2,1)} collective-permute-done((bf16[64,1536]{1,0:T(8,128)(2,1)S(1)}, bf16[64,1536]{1,0:T(8,128)(2,1)}, u32[]{:S(2)}, u32[]{:S(2)}) %collective-permute-start.9) | collective-permute-done | bytes 196640 | tf_op jit(solution)/shard_map/ppermute | solution.py:230
  63.3 0.0 collective-permute-done.7.refs_6_
  63.3 0.0 collective-permute-done.6.refs_5_
  63.3 0.0 collective-permute-done.8.refs_7_
  63.4 6.0 %shard_map.105.grad_ref = bf16[512,1024]{1,0:T(8,128)(2,1)S(1)} custom-call(s32[4]{0:T(128)S(1)} %pad_add_fusion.at_ref, bf16[2,64,1536]{2,1,0:T(8,128)(2,1)} %copy-done.4, bf16[2,64,1536]{2,1,0:T(8,128)(2,1)} %copy-done.6, bf16[2,64,1536]{2,1,0:T(8,128)(2,1)} %copy-done.5, bf16[2,64,1536]{2,1,0:T(8,128)(2,1)} %collective-permute-done.4.refs_3_, ...), custom_call_target="tpu_custom_call" | custom-call | flops 2684354560 | bytes 8388608 | tf_op jit(solution)/shard_map/pallas_call | solution.py:232
  69.4 0.7 shard_map.106
  70.2 0.0 copy-start
  70.2 0.0 copy-start.1
  70.2 0.0 copy-start.2
  70.2 26.6 %all_to_all.15 = bf16[64,16,256]{2,1,0:T(8,128)(2,1)S(1)} all-to-all(bf16[64,16,256]{2,1,0:T(8,128)(2,1)S(1)} %bitcast.18), channel_id=1, replica_groups={{0,1,2,3,4,5,6,7,8,9,10,11,12,13,14,15,32,33,34,35,36,37,38,39,40,41,42..., dimensions={0} | all-to-all | bytes 1048576 | tf_op jit(solution)/shard_map/all_to_all | solution.py:256
  96.8 0.2 shard_map.107
  97.0 27.6 %all_to_all.16.shares_ref = bf16[32,32,128]{2,1,0:T(8,128)(2,1)S(1)} all-to-all(bf16[32,32,128]{2,1,0:T(8,128)(2,1)S(1)} %shard_map.107), channel_id=1, replica_groups={{0,64,128,192,256,320,384,448,32,96,160,224,288,352,416,480,16,80,144,2..., dimensions={0} | all-to-all | bytes 524288 | tf_op jit(solution)/shard_map/all_to_all | solution.py:272
  124.7 1.6 %shard_map.108 = (f32[8,64,128]{2,1,0:T(8,128)}, f32[8,64,128]{2,1,0:T(8,128)}) custom-call(s32[8,16]{1,0:T(8,128)S(1)} %copy-done.2, bf16[32,32,128]{2,1,0:T(8,128)(2,1)S(1)} %all_to_all.16.shares_ref, f32[8,64,128]{2,1,0:T(8,128)S(1)} %copy-done, f32[8,64,128]{2,1,0:T(8,128)S(1)} %copy-done.1), custom_call_target="tpu_custom_call" | custom-call | bytes 2097152 | tf_op jit(solution)/shard_map/pallas_call | solution.py:274
  (17 shorter events, 0.1 us)
Async XLA Ops:
  1.6 3.9 %collective-permute-start = (bf16[64,1536]{1,0:T(8,128)(2,1)S(1)}, bf16[64,1536]{1,0:T(8,128)(2,1)S(1)}, u32[]{:S(2)}, u32[]{:S(2)}) collective-permute-start(bf16[64,1536]{1,0:T(8,128)(2,1)S(1)} %shard_map.104), channel_id=1, source_target_pairs={{0,8},{1,9},{2,10},{3,11},{4,12},{5,13},{6,14},{7,15},{8,0},{9,1},... | collective-permute-start | bytes 589832 | tf_op jit(solution)/shard_map/ppermute | solution.py:220
  5.5 57.8 %copy-start.3 = (f32[1024]{0:T(1024)S(1)}, f32[1024]{0:T(1024)}, u32[]{:S(2)}) copy-start(f32[1024]{0:T(1024)} %param.12) | copy-start | bytes 12292
  5.5 63.9 %all-to-all-start = ((bf16[16,8,16,512]{3,2,1,0:T(8,128)(2,1)}), bf16[16,8,16,512]{3,2,1,0:T(8,128)(2,1)S(1)}, u32[]{:S(2)}, u32[]{:S(2)}) async-start(bf16[16,8,16,512]{3,2,1,0:T(8,128)(2,1)} %bitcast.21), calls=%async_computation | async-start | bytes 4194304 | tf_op jit(solution)/shard_map/all_to_all | solution.py:223
  16.0 9.6 %collective-permute-start.1 = (bf16[64,1536]{1,0:T(8,128)(2,1)S(1)}, bf16[64,1536]{1,0:T(8,128)(2,1)S(1)}, u32[]{:S(2)}, u32[]{:S(2)}) collective-permute-start(bf16[64,1536]{1,0:T(8,128)(2,1)S(1)} %collective-permute-done), channel_id=1, source_target_pairs={{0,16},{16,0},{32,48},{48,32},{64,80},{80,64},{96,112},{112,96},{1... | collective-permute-start | bytes 589832 | tf_op jit(solution)/shard_map/ppermute | solution.py:224
  25.7 37.6 %copy-start.4 = (bf16[2,64,1536]{2,1,0:T(8,128)(2,1)}, bf16[2,64,1536]{2,1,0:T(8,128)(2,1)S(1)}, u32[]{:S(2)}) copy-start(bf16[2,64,1536]{2,1,0:T(8,128)(2,1)S(1)} %pad_maximum_fusion.refs_0_) | copy-start | bytes 1179652
  25.7 16.8 %collective-permute-start.3 = (bf16[2,64,1536]{2,1,0:T(8,128)(2,1)S(1)}, bf16[2,64,1536]{2,1,0:T(8,128)(2,1)S(1)}, u32[]{:S(2)}, u32[]{:S(2)}) collective-permute-start(bf16[2,64,1536]{2,1,0:T(8,128)(2,1)S(1)} %pad_maximum_fusion.refs_0_), channel_id=1, source_target_pairs={{0,128},{16,400},{32,160},{48,432},{64,192},{80,464},{96,224},{112... | collective-permute-start | bytes 1179656 | tf_op jit(solution)/shard_map/ppermute | solution.py:225
  34.0 18.6 %collective-permute-start.2 = (bf16[2,64,1536]{2,1,0:T(8,128)(2,1)S(1)}, bf16[2,64,1536]{2,1,0:T(8,128)(2,1)S(1)}, u32[]{:S(2)}, u32[]{:S(2)}) collective-permute-start(bf16[2,64,1536]{2,1,0:T(8,128)(2,1)S(1)} %pad_maximum_fusion.refs_0_), channel_id=1, source_target_pairs={{0,64},{16,464},{32,96},{48,496},{64,128},{80,16},{96,160},{112,48... | collective-permute-start | bytes 1179656 | tf_op jit(solution)/shard_map/ppermute | solution.py:226
  42.5 20.8 %copy-start.5 = (bf16[2,64,1536]{2,1,0:T(8,128)(2,1)}, bf16[2,64,1536]{2,1,0:T(8,128)(2,1)S(1)}, u32[]{:S(2)}) copy-start(bf16[2,64,1536]{2,1,0:T(8,128)(2,1)S(1)} %collective-permute-done.3.refs_2_) | copy-start | bytes 1179652
  42.5 12.5 %collective-permute-start.4 = (bf16[2,64,1536]{2,1,0:T(8,128)(2,1)S(1)}, bf16[2,64,1536]{2,1,0:T(8,128)(2,1)}, u32[]{:S(2)}, u32[]{:S(2)}) collective-permute-start(bf16[2,64,1536]{2,1,0:T(8,128)(2,1)S(1)} %collective-permute-done.3.refs_2_), channel_id=1, source_target_pairs={{0,64},{16,464},{32,96},{48,496},{64,128},{80,16},{96,160},{112,48... | collective-permute-start | bytes 1179656 | tf_op jit(solution)/shard_map/ppermute | solution.py:227
  47.1 12.7 %collective-permute-start.5 = (bf16[64,1536]{1,0:T(8,128)(2,1)S(1)}, bf16[64,1536]{1,0:T(8,128)(2,1)S(1)}, u32[]{:S(2)}, u32[]{:S(2)}) collective-permute-start(bf16[64,1536]{1,0:T(8,128)(2,1)S(1)} %slice_bitcast_fusion), channel_id=1, source_target_pairs={{0,128},{16,400},{32,160},{48,432},{64,192},{80,464},{96,224},{112... | collective-permute-start | bytes 589832 | tf_op jit(solution)/shard_map/ppermute | solution.py:228
  50.7 12.6 %collective-permute-start.7 = (bf16[2,64,1536]{2,1,0:T(8,128)(2,1)S(1)}, bf16[2,64,1536]{2,1,0:T(8,128)(2,1)}, u32[]{:S(2)}, u32[]{:S(2)}) collective-permute-start(bf16[2,64,1536]{2,1,0:T(8,128)(2,1)S(1)} %collective-permute-done.3.refs_2_), channel_id=1, source_target_pairs={{0,16},{16,0},{32,48},{48,32},{64,80},{80,64},{96,112},{112,96},{1... | collective-permute-start | bytes 1179656 | tf_op jit(solution)/shard_map/ppermute | solution.py:230
  52.6 10.7 %copy-start.6 = (bf16[2,64,1536]{2,1,0:T(8,128)(2,1)}, bf16[2,64,1536]{2,1,0:T(8,128)(2,1)S(1)}, u32[]{:S(2)}) copy-start(bf16[2,64,1536]{2,1,0:T(8,128)(2,1)S(1)} %collective-permute-done.2.refs_1_) | copy-start | bytes 1179652
  52.6 10.7 %collective-permute-start.6 = (bf16[2,64,1536]{2,1,0:T(8,128)(2,1)S(1)}, bf16[2,64,1536]{2,1,0:T(8,128)(2,1)}, u32[]{:S(2)}, u32[]{:S(2)}) collective-permute-start(bf16[2,64,1536]{2,1,0:T(8,128)(2,1)S(1)} %collective-permute-done.2.refs_1_), channel_id=1, source_target_pairs={{0,16},{16,0},{32,48},{48,32},{64,80},{80,64},{96,112},{112,96},{1... | collective-permute-start | bytes 1179656 | tf_op jit(solution)/shard_map/ppermute | solution.py:230
  55.0 8.3 %collective-permute-start.8 = (bf16[2,64,1536]{2,1,0:T(8,128)(2,1)}, bf16[2,64,1536]{2,1,0:T(8,128)(2,1)}, u32[]{:S(2)}, u32[]{:S(2)}) collective-permute-start(bf16[2,64,1536]{2,1,0:T(8,128)(2,1)} %collective-permute-done.4.refs_3_), channel_id=1, source_target_pairs={{0,16},{16,0},{32,48},{48,32},{64,80},{80,64},{96,112},{112,96},{1... | collective-permute-start | bytes 1179656 | tf_op jit(solution)/shard_map/ppermute | solution.py:230
  59.8 3.5 %copy-start.7 = (bf16[64,1536]{1,0:T(8,128)(2,1)}, bf16[64,1536]{1,0:T(8,128)(2,1)S(1)}, u32[]{:S(2)}) copy-start(bf16[64,1536]{1,0:T(8,128)(2,1)S(1)} %collective-permute-done.5.refs_4_) | copy-start | bytes 589828
  59.8 3.5 %collective-permute-start.9 = (bf16[64,1536]{1,0:T(8,128)(2,1)S(1)}, bf16[64,1536]{1,0:T(8,128)(2,1)}, u32[]{:S(2)}, u32[]{:S(2)}) collective-permute-start(bf16[64,1536]{1,0:T(8,128)(2,1)S(1)} %collective-permute-done.5.refs_4_), channel_id=1, source_target_pairs={{0,16},{16,0},{32,48},{48,32},{64,80},{80,64},{96,112},{112,96},{1... | collective-permute-start | bytes 589832 | tf_op jit(solution)/shard_map/ppermute | solution.py:230
  70.2 54.5 %copy-start = (f32[8,64,128]{2,1,0:T(8,128)S(1)}, f32[8,64,128]{2,1,0:T(8,128)}, u32[]{:S(2)}) copy-start(f32[8,64,128]{2,1,0:T(8,128)} %table_ref.1) | copy-start | bytes 786436
  70.2 54.5 %copy-start.1 = (f32[8,64,128]{2,1,0:T(8,128)S(1)}, f32[8,64,128]{2,1,0:T(8,128)}, u32[]{:S(2)}) copy-start(f32[8,64,128]{2,1,0:T(8,128)} %accum_ref.1) | copy-start | bytes 786436
  70.2 54.5 %copy-start.2 = (s32[8,16]{1,0:T(8,128)S(1)}, s32[8,16]{1,0:T(8,128)}, u32[]{:S(2)}) copy-start(s32[8,16]{1,0:T(8,128)} %ids_ref.1) | copy-start | bytes 1540

commit v6 on v5

--- a/solution.py
+++ b/solution.py
@@ -40,16 +40,15 @@
     return pltpu.with_memory_space_constraint(x, pltpu.HBM)
 
 
-def quads(owners):
+def chip_pairs(owners):
     return [
-        [wide_at(y, h, c) * owners + n for c in range(N_CORE) for h in range(N_HI) for n in range(owners)]
+        [wide_at(y, h, c) * owners + n for c in range(N_CORE) for n in range(owners)]
         for y in range(N_Y)
+        for h in range(N_HI)
     ]
 
 
-WIDE_ORDER = [
-    [wide_at(y, h, c) for c in range(N_CORE) for h in range(N_HI) for y in range(N_Y)]
-]
+HY_GROUPS = [[wide_at(y, h, c) for h in range(N_HI) for y in range(N_Y)] for c in range(N_CORE)]
 N_X = 4
 
 
@@ -173,21 +172,24 @@
         out_ref[n] = both
 
 
-def update_body(ids_ref, shares_ref, table_ref, accum_ref, new_table_ref, new_accum_ref, dense, rows):
+def share_body(parts_ref, out_ref):
+    total = parts_ref[0].astype(f32)
+    for n in range(1, parts_ref.shape[0]):
+        total = total + parts_ref[n].astype(f32)
+    out_ref[...] = total
+
+
+def update_body(at_ref, ids_ref, mine_ref, other_ref, table_ref, accum_ref, new_table_ref, new_accum_ref, dense):
     tables, act = ids_ref.shape
-    quarters = N_HI * N_CORE
-    per = tables // quarters
+    per_core = tables // N_CORE
+    core = at_ref[0]
     dense[...] = jnp.zeros_like(dense)
-    for q in range(quarters):
-        total = shares_ref[q * N_Y].astype(f32)
-        for y in range(1, N_Y):
-            total = total + shares_ref[q * N_Y + y].astype(f32)
-        rows[...] = total
-        for t in range(per):
-            table = q * per + t
+    for ref, side in ((mine_ref, core), (other_ref, 1 - core)):
+        for t in range(per_core):
             for a in range(act):
+                table = side * per_core + t
                 row = ids_ref[table, a]
-                dense[table, pl.ds(row, 1), :] = rows[pl.ds(t * act + a, 1), :]
+                dense[table, pl.ds(row, 1), :] = ref[pl.ds(t * act + a, 1), :]
     for t in range(tables):
         summed = dense[t]
         new_acc = accum_ref[t] + summed * summed
@@ -218,8 +220,8 @@
         limit=2,
     )(in_hbm(w_first), in_hbm(w_second))
     moved = lax.ppermute(shard, ("wide", "narrow"), shard_moves(owners))
+    counts, _ = lax.optimization_barrier((counts, shard))
     by_owner = jnp.transpose(counts.reshape(tables, act, owners, samples), (2, 0, 1, 3))
-    by_owner, moved = lax.optimization_barrier((by_owner, moved))
     regrouped = lax.all_to_all(by_owner, "narrow", 0, 0, tiled=True)
     whole = jnp.stack([moved, lax.ppermute(moved, "wide", CORE_SWAP)])
     ahead2 = lax.ppermute(whole, "wide", y_shift(2))
@@ -241,11 +243,11 @@
             pltpu.VMEM(cotangent.shape, bf16),
             pltpu.SemaphoreType.DMA((2, N_Y * N_CORE + 1)),
         ],
-        flops=2 * samples * inner * (2 * inner + top),
+        flops=35 * samples * inner * (2 * inner + top) // 2,
         nbytes=8 * MIB,
     )(place, *map(in_hbm, (whole, *ring, *swapped, pooled, cotangent)), b_first.reshape(1, -1))
 
-    quarters = N_HI * N_CORE
+    quarters = N_CORE
     parts = call(
         partial_body,
         jax.ShapeDtypeStruct((quarters, owners, act, tables // quarters * emb), bf16),
@@ -258,26 +260,28 @@
         ("wide", "narrow"),
         0,
         0,
-        axis_index_groups=quads(owners),
+        axis_index_groups=chip_pairs(owners),
         tiled=True,
     )
     rows = tables * act // quarters
     copies = call(
         functools.partial(clip_body, scale, limit),
-        jax.ShapeDtypeStruct((N_Y * quarters, rows, emb), bf16),
+        jax.ShapeDtypeStruct((N_Y * N_HI, rows, emb), bf16),
         [VMEM],
         [pltpu.VMEM((rows, emb), f32)],
         nbytes=MIB,
     )(arrived.reshape(parts.shape))
-    shares = lax.all_to_all(copies, "wide", 0, 0, axis_index_groups=WIDE_ORDER, tiled=True)
+    shares = lax.all_to_all(copies, "wide", 0, 0, axis_index_groups=HY_GROUPS, tiled=True)
+    mine = call(share_body, jax.ShapeDtypeStruct((rows, emb), f32), [VMEM], nbytes=MIB)(shares)
+    theirs = lax.ppermute(mine, "wide", CORE_SWAP)
     updated = jax.ShapeDtypeStruct(table.shape, f32)
     return call(
         update_body,
         (updated, updated),
-        [SMEM] + [VMEM] * 3,
-        [pltpu.VMEM(table.shape, f32), pltpu.VMEM((rows, emb), f32)],
+        [SMEM, SMEM] + [VMEM] * 4,
+        [pltpu.VMEM(table.shape, f32)],
         nbytes=2 * MIB,
-    )(row_ids, shares, table, accum)
+    )(place, row_ids, mine, theirs, table, accum)
 
 
 def solution(mesh):

time: 127 us -> 122 us (0.961)
  blocking collectives: 54.3 us -> 49.7 us
    ppermute x0 -> x1, starting transfers between devices: none -> 4.86 us  [shards(): theirs = lax.ppermute(mine, 'wide', CORE_SWAP)]
    ppermute x1, starting transfers between devices: 8.58 us -> 4.66 us  [shards(): whole = jnp.stack([moved, lax.ppermute(moved, 'wide', CORE_SWAP)])]
    all_to_all x1, blocking collectives: 26.6 us -> 23.8 us  [shards(): lax.all_to_all(parts.reshape(owners * quarters, act, -1), ('wide', 'narro...]
    all_to_all x1, blocking collectives: 27.6 us -> 25.9 us  [shards(): lax.all_to_all(copies, 'wide', 0, 0, axis_index_groups=HY_GROUPS, tiled=T...]
  transfers between devices with their start and end apart: 11 -> 12, of which waited for: 3 -> 4; matrix products, arithmetic and copies ran while one was open for 3% -> 3% of each run, Pallas kernels for 5% -> 5%
where the time goes in v6:
time: 122 us; the launch traced here: 121 us
  blocking collectives  49.7 us (41%)
  starting transfers between devices  48.4 us (40%)
  Pallas kernels  9.54 us (8%)
  waiting for transfers between devices  9.33 us (8%)
  local copies, waits for them, and re-layouts  3.31 us (3%)
    all_to_all x1, blocking collectives, shards(): lax.all_to_all(copies, 'wide', 0, 0, axis_index_groups=HY_GROUPS, tiled=T...  25.9 us
    all_to_all x1, blocking collectives, shards(): lax.all_to_all(parts.reshape(owners * quarters, act, -1), ('wide', 'narro...  23.8 us
    all_to_all x1, starting transfers between devices, shards(): regrouped = lax.all_to_all(by_owner, 'narrow', 0, 0, tiled=True)  10.5 us
    ppermute x4, starting transfers between devices, shards(): swapped = [lax.ppermute(block, 'wide', CORE_SWAP) for block in ring]  10 us
    ppermute x1, starting transfers between devices, shards(): ahead2 = lax.ppermute(whole, 'wide', y_shift(2))  7.07 us
    ppermute x1, waiting for transfers between devices, shards(): ahead2 = lax.ppermute(whole, 'wide', y_shift(2))  6.33 us
    pallas_call x1, Pallas kernels, shards(): call(tower_body, jax.ShapeDtypeStruct((samples, owners * w_first.shape[0]...  6.04 us
    ppermute x1, starting transfers between devices, shards(): theirs = lax.ppermute(mine, 'wide', CORE_SWAP)  4.86 us
  transfers between devices with their start and end apart: 12, of which 4 were waited for; matrix products, arithmetic and copies ran while one was open for 3% of the time, Pallas kernels for 5%

profile of v6, /device:TPU:1, one launch (start us, length us, event | category | flops | bytes accessed | tf_op | source)
XLA Modules:
  0.0 121.3 jit_solution(11077119328589495711)
XLA Ops:
  0.6 0.9 shard_map.104
  1.6 0.7 collective-permute-start
  2.2 3.3 %copy.14 = bf16[8,2,16,8,512]{4,3,1,0,2:T(8,128)(2,1)} copy(bf16[8,2,16,8,512]{4,3,2,1,0:T(8,128)(2,1)} %bitcast.22) | data formatting | bytes 4194304 | tf_op jit(solution)/shard_map/reshape | solution.py:224
  5.5 10.5 %all-to-all-start = ((bf16[16,8,16,512]{3,2,1,0:T(8,128)(2,1)}), bf16[16,8,16,512]{3,2,1,0:T(8,128)(2,1)S(1)}, u32[]{:S(2)}, u32[]{:S(2)}) async-start(bf16[16,8,16,512]{3,2,1,0:T(8,128)(2,1)} %bitcast.21), calls=%async_computation | async-start | bytes 4194304 | tf_op jit(solution)/shard_map/all_to_all | solution.py:225
  16.0 0.0 collective-permute-done
  16.0 4.7 %collective-permute-start.1 = (bf16[64,1536]{1,0:T(8,128)(2,1)S(1)}, bf16[64,1536]{1,0:T(8,128)(2,1)S(1)}, u32[]{:S(2)}, u32[]{:S(2)}) collective-permute-start(bf16[64,1536]{1,0:T(8,128)(2,1)S(1)} %collective-permute-done), channel_id=1, source_target_pairs={{0,16},{16,0},{32,48},{48,32},{64,80},{80,64},{96,112},{112,96},{1... | collective-permute-start | bytes 589832 | tf_op jit(solution)/shard_map/ppermute | solution.py:226
  20.7 1.0 collective-permute-done.1
  21.8 7.1 %collective-permute-start.3 = (bf16[2,64,1536]{2,1,0:T(8,128)(2,1)S(1)}, bf16[2,64,1536]{2,1,0:T(8,128)(2,1)S(1)}, u32[]{:S(2)}, u32[]{:S(2)}) collective-permute-start(bf16[2,64,1536]{2,1,0:T(8,128)(2,1)S(1)} %pad_maximum_fusion.refs_0_), channel_id=1, source_target_pairs={{0,128},{16,400},{32,160},{48,432},{64,192},{80,464},{96,224},{112... | collective-permute-start | bytes 1179656 | tf_op jit(solution)/shard_map/ppermute | solution.py:227
  28.9 2.4 %collective-permute-start.2 = (bf16[2,64,1536]{2,1,0:T(8,128)(2,1)S(1)}, bf16[2,64,1536]{2,1,0:T(8,128)(2,1)S(1)}, u32[]{:S(2)}, u32[]{:S(2)}) collective-permute-start(bf16[2,64,1536]{2,1,0:T(8,128)(2,1)S(1)} %pad_maximum_fusion.refs_0_), channel_id=1, source_target_pairs={{0,64},{16,464},{32,96},{48,496},{64,128},{80,16},{96,160},{112,48... | collective-permute-start | bytes 1179656 | tf_op jit(solution)/shard_map/ppermute | solution.py:228
  31.3 6.3 %collective-permute-done.3.refs_2_ = bf16[2,64,1536]{2,1,0:T(8,128)(2,1)S(1)} collective-permute-done((bf16[2,64,1536]{2,1,0:T(8,128)(2,1)S(1)}, bf16[2,64,1536]{2,1,0:T(8,128)(2,1)S(1)}, u32[]{:S(2)}, u32[]{:S(2)}) %collective-permute-start.3) | collective-permute-done | bytes 393248 | tf_op jit(solution)/shard_map/ppermute | solution.py:227
  37.6 4.1 %collective-permute-start.4 = (bf16[2,64,1536]{2,1,0:T(8,128)(2,1)S(1)}, bf16[2,64,1536]{2,1,0:T(8,128)(2,1)}, u32[]{:S(2)}, u32[]{:S(2)}) collective-permute-start(bf16[2,64,1536]{2,1,0:T(8,128)(2,1)S(1)} %collective-permute-done.3.refs_2_), channel_id=1, source_target_pairs={{0,64},{16,464},{32,96},{48,496},{64,128},{80,16},{96,160},{112,48... | collective-permute-start | bytes 1179656 | tf_op jit(solution)/shard_map/ppermute | solution.py:229
  41.8 4.0 %collective-permute-start.5 = (bf16[64,1536]{1,0:T(8,128)(2,1)S(1)}, bf16[64,1536]{1,0:T(8,128)(2,1)S(1)}, u32[]{:S(2)}, u32[]{:S(2)}) collective-permute-start(bf16[64,1536]{1,0:T(8,128)(2,1)S(1)} %slice_bitcast_fusion), channel_id=1, source_target_pairs={{0,128},{16,400},{32,160},{48,432},{64,192},{80,464},{96,224},{112... | collective-permute-start | bytes 589832 | tf_op jit(solution)/shard_map/ppermute | solution.py:230
  45.8 1.9 %collective-permute-start.7 = (bf16[2,64,1536]{2,1,0:T(8,128)(2,1)S(1)}, bf16[2,64,1536]{2,1,0:T(8,128)(2,1)}, u32[]{:S(2)}, u32[]{:S(2)}) collective-permute-start(bf16[2,64,1536]{2,1,0:T(8,128)(2,1)S(1)} %collective-permute-done.3.refs_2_), channel_id=1, source_target_pairs={{0,16},{16,0},{32,48},{48,32},{64,80},{80,64},{96,112},{112,96},{1... | collective-permute-start | bytes 1179656 | tf_op jit(solution)/shard_map/ppermute | solution.py:232
  47.8 2.4 %collective-permute-start.6 = (bf16[2,64,1536]{2,1,0:T(8,128)(2,1)S(1)}, bf16[2,64,1536]{2,1,0:T(8,128)(2,1)}, u32[]{:S(2)}, u32[]{:S(2)}) collective-permute-start(bf16[2,64,1536]{2,1,0:T(8,128)(2,1)S(1)} %collective-permute-done.2.refs_1_), channel_id=1, source_target_pairs={{0,16},{16,0},{32,48},{48,32},{64,80},{80,64},{96,112},{112,96},{1... | collective-permute-start | bytes 1179656 | tf_op jit(solution)/shard_map/ppermute | solution.py:232
  50.2 0.0 collective-permute-done.4.refs_3_
  50.2 1.9 %collective-permute-start.8 = (bf16[2,64,1536]{2,1,0:T(8,128)(2,1)}, bf16[2,64,1536]{2,1,0:T(8,128)(2,1)}, u32[]{:S(2)}, u32[]{:S(2)}) collective-permute-start(bf16[2,64,1536]{2,1,0:T(8,128)(2,1)} %collective-permute-done.4.refs_3_), channel_id=1, source_target_pairs={{0,16},{16,0},{32,48},{48,32},{64,80},{80,64},{96,112},{112,96},{1... | collective-permute-start | bytes 1179656 | tf_op jit(solution)/shard_map/ppermute | solution.py:232
  52.1 0.0 collective-permute-done.5.refs_4_
  52.1 0.0 copy-start.7
  52.1 3.8 %collective-permute-start.9 = (bf16[64,1536]{1,0:T(8,128)(2,1)S(1)}, bf16[64,1536]{1,0:T(8,128)(2,1)}, u32[]{:S(2)}, u32[]{:S(2)}) collective-permute-start(bf16[64,1536]{1,0:T(8,128)(2,1)S(1)} %collective-permute-done.5.refs_4_), channel_id=1, source_target_pairs={{0,16},{16,0},{32,48},{48,32},{64,80},{80,64},{96,112},{112,96},{1... | collective-permute-start | bytes 589832 | tf_op jit(solution)/shard_map/ppermute | solution.py:232
  55.9 0.1 pad_add_fusion.at_ref
  56.0 1.1 collective-permute-done.9.refs_8_
  57.2 6.0 %shard_map.105.grad_ref = bf16[512,1024]{1,0:T(8,128)(2,1)S(1)} custom-call(s32[4]{0:T(128)S(1)} %pad_add_fusion.at_ref, bf16[2,64,1536]{2,1,0:T(8,128)(2,1)} %copy-done.4, bf16[2,64,1536]{2,1,0:T(8,128)(2,1)} %copy-done.6, bf16[2,64,1536]{2,1,0:T(8,128)(2,1)} %copy-done.5, bf16[2,64,1536]{2,1,0:T(8,128)(2,1)} %collective-permute-done.4.refs_3_, ...), custom_call_target="tpu_custom_call" | custom-call | flops 23488102400 | bytes 8388608 | tf_op jit(solution)/shard_map/pallas_call | solution.py:234
  63.2 0.7 shard_map.106
  63.9 0.0 copy-start
  64.0 0.0 copy-start.1
  64.0 0.0 copy-start.2
  64.0 23.8 %all_to_all.15 = bf16[32,16,512]{2,1,0:T(8,128)(2,1)S(1)} all-to-all(bf16[32,16,512]{2,1,0:T(8,128)(2,1)S(1)} %bitcast.18), channel_id=1, replica_groups={{0,1,2,3,4,5,6,7,8,9,10,11,12,13,14,15,16,17,18,19,20,21,22,23,24,25,26..., dimensions={0} | all-to-all | bytes 1048576 | tf_op jit(solution)/shard_map/all_to_all | solution.py:258
  87.7 0.2 shard_map.107
  87.9 25.9 %all_to_all.16.parts_ref = bf16[16,64,128]{2,1,0:T(8,128)(2,1)S(1)} all-to-all(bf16[16,64,128]{2,1,0:T(8,128)(2,1)S(1)} %shard_map.107), channel_id=1, replica_groups={{0,64,128,192,256,320,384,448,32,96,160,224,288,352,416,480},{16,80,144..., dimensions={0} | all-to-all | bytes 524288 | tf_op jit(solution)/shard_map/all_to_all | solution.py:274
  113.9 4.9 %collective-permute-start.10 = (f32[64,128]{1,0:T(8,128)S(1)}, f32[64,128]{1,0:T(8,128)S(1)}, u32[]{:S(2)}, u32[]{:S(2)}) collective-permute-start(f32[64,128]{1,0:T(8,128)S(1)} %shard_map.108.mine_ref), channel_id=1, source_target_pairs={{0,16},{16,0},{32,48},{48,32},{64,80},{80,64},{96,112},{112,96},{1... | collective-permute-start | bytes 98312 | tf_op jit(solution)/shard_map/ppermute | solution.py:276
  118.8 0.8 collective-permute-done.10.other_ref
  119.6 1.6 %shard_map.109 = (f32[8,64,128]{2,1,0:T(8,128)}, f32[8,64,128]{2,1,0:T(8,128)}) custom-call(s32[4]{0:T(128)S(1)} %pad_add_fusion.at_ref, s32[8,16]{1,0:T(8,128)S(1)} %copy-done.2, f32[64,128]{1,0:T(8,128)S(1)} %shard_map.108.mine_ref, f32[64,128]{1,0:T(8,128)S(1)} %collective-permute-done.10.other_ref, f32[8,64,128]{2,1,0:T(8,128)S(1)} %copy-done, ...), custom_call_target="tpu_custom_call" | custom-call | bytes 2097152 | tf_op jit(solution)/shard_map/pallas_call | solution.py:278
  (20 shorter events, 0.1 us)
Async XLA Ops:
  1.6 14.5 %collective-permute-start = (bf16[64,1536]{1,0:T(8,128)(2,1)S(1)}, bf16[64,1536]{1,0:T(8,128)(2,1)S(1)}, u32[]{:S(2)}, u32[]{:S(2)}) collective-permute-start(bf16[64,1536]{1,0:T(8,128)(2,1)S(1)} %shard_map.104), channel_id=1, source_target_pairs={{0,8},{1,9},{2,10},{3,11},{4,12},{5,13},{6,14},{7,15},{8,0},{9,1},... | collective-permute-start | bytes 589832 | tf_op jit(solution)/shard_map/ppermute | solution.py:222
  5.5 51.7 %copy-start.3 = (f32[1024]{0:T(1024)S(1)}, f32[1024]{0:T(1024)}, u32[]{:S(2)}) copy-start(f32[1024]{0:T(1024)} %param.12) | copy-start | bytes 12292
  5.5 57.7 %all-to-all-start = ((bf16[16,8,16,512]{3,2,1,0:T(8,128)(2,1)}), bf16[16,8,16,512]{3,2,1,0:T(8,128)(2,1)S(1)}, u32[]{:S(2)}, u32[]{:S(2)}) async-start(bf16[16,8,16,512]{3,2,1,0:T(8,128)(2,1)} %bitcast.21), calls=%async_computation | async-start | bytes 4194304 | tf_op jit(solution)/shard_map/all_to_all | solution.py:225
  16.0 5.7 %collective-permute-start.1 = (bf16[64,1536]{1,0:T(8,128)(2,1)S(1)}, bf16[64,1536]{1,0:T(8,128)(2,1)S(1)}, u32[]{:S(2)}, u32[]{:S(2)}) collective-permute-start(bf16[64,1536]{1,0:T(8,128)(2,1)S(1)} %collective-permute-done), channel_id=1, source_target_pairs={{0,16},{16,0},{32,48},{48,32},{64,80},{80,64},{96,112},{112,96},{1... | collective-permute-start | bytes 589832 | tf_op jit(solution)/shard_map/ppermute | solution.py:226
  21.8 35.4 %copy-start.4 = (bf16[2,64,1536]{2,1,0:T(8,128)(2,1)}, bf16[2,64,1536]{2,1,0:T(8,128)(2,1)S(1)}, u32[]{:S(2)}) copy-start(bf16[2,64,1536]{2,1,0:T(8,128)(2,1)S(1)} %pad_maximum_fusion.refs_0_) | copy-start | bytes 1179652
  21.8 15.8 %collective-permute-start.3 = (bf16[2,64,1536]{2,1,0:T(8,128)(2,1)S(1)}, bf16[2,64,1536]{2,1,0:T(8,128)(2,1)S(1)}, u32[]{:S(2)}, u32[]{:S(2)}) collective-permute-start(bf16[2,64,1536]{2,1,0:T(8,128)(2,1)S(1)} %pad_maximum_fusion.refs_0_), channel_id=1, source_target_pairs={{0,128},{16,400},{32,160},{48,432},{64,192},{80,464},{96,224},{112... | collective-permute-start | bytes 1179656 | tf_op jit(solution)/shard_map/ppermute | solution.py:227
  28.9 18.9 %collective-permute-start.2 = (bf16[2,64,1536]{2,1,0:T(8,128)(2,1)S(1)}, bf16[2,64,1536]{2,1,0:T(8,128)(2,1)S(1)}, u32[]{:S(2)}, u32[]{:S(2)}) collective-permute-start(bf16[2,64,1536]{2,1,0:T(8,128)(2,1)S(1)} %pad_maximum_fusion.refs_0_), channel_id=1, source_target_pairs={{0,64},{16,464},{32,96},{48,496},{64,128},{80,16},{96,160},{112,48... | collective-permute-start | bytes 1179656 | tf_op jit(solution)/shard_map/ppermute | solution.py:228
  37.6 19.5 %copy-start.5 = (bf16[2,64,1536]{2,1,0:T(8,128)(2,1)}, bf16[2,64,1536]{2,1,0:T(8,128)(2,1)S(1)}, u32[]{:S(2)}) copy-start(bf16[2,64,1536]{2,1,0:T(8,128)(2,1)S(1)} %collective-permute-done.3.refs_2_) | copy-start | bytes 1179652
  37.6 12.5 %collective-permute-start.4 = (bf16[2,64,1536]{2,1,0:T(8,128)(2,1)S(1)}, bf16[2,64,1536]{2,1,0:T(8,128)(2,1)}, u32[]{:S(2)}, u32[]{:S(2)}) collective-permute-start(bf16[2,64,1536]{2,1,0:T(8,128)(2,1)S(1)} %collective-permute-done.3.refs_2_), channel_id=1, source_target_pairs={{0,64},{16,464},{32,96},{48,496},{64,128},{80,16},{96,160},{112,48... | collective-permute-start | bytes 1179656 | tf_op jit(solution)/shard_map/ppermute | solution.py:229
  41.8 10.3 %collective-permute-start.5 = (bf16[64,1536]{1,0:T(8,128)(2,1)S(1)}, bf16[64,1536]{1,0:T(8,128)(2,1)S(1)}, u32[]{:S(2)}, u32[]{:S(2)}) collective-permute-start(bf16[64,1536]{1,0:T(8,128)(2,1)S(1)} %slice_bitcast_fusion), channel_id=1, source_target_pairs={{0,128},{16,400},{32,160},{48,432},{64,192},{80,464},{96,224},{112... | collective-permute-start | bytes 589832 | tf_op jit(solution)/shard_map/ppermute | solution.py:230
  45.8 11.3 %collective-permute-start.7 = (bf16[2,64,1536]{2,1,0:T(8,128)(2,1)S(1)}, bf16[2,64,1536]{2,1,0:T(8,128)(2,1)}, u32[]{:S(2)}, u32[]{:S(2)}) collective-permute-start(bf16[2,64,1536]{2,1,0:T(8,128)(2,1)S(1)} %collective-permute-done.3.refs_2_), channel_id=1, source_target_pairs={{0,16},{16,0},{32,48},{48,32},{64,80},{80,64},{96,112},{112,96},{1... | collective-permute-start | bytes 1179656 | tf_op jit(solution)/shard_map/ppermute | solution.py:232
  47.7 9.4 %copy-start.6 = (bf16[2,64,1536]{2,1,0:T(8,128)(2,1)}, bf16[2,64,1536]{2,1,0:T(8,128)(2,1)S(1)}, u32[]{:S(2)}) copy-start(bf16[2,64,1536]{2,1,0:T(8,128)(2,1)S(1)} %collective-permute-done.2.refs_1_) | copy-start | bytes 1179652
  47.8 9.4 %collective-permute-start.6 = (bf16[2,64,1536]{2,1,0:T(8,128)(2,1)S(1)}, bf16[2,64,1536]{2,1,0:T(8,128)(2,1)}, u32[]{:S(2)}, u32[]{:S(2)}) collective-permute-start(bf16[2,64,1536]{2,1,0:T(8,128)(2,1)S(1)} %collective-permute-done.2.refs_1_), channel_id=1, source_target_pairs={{0,16},{16,0},{32,48},{48,32},{64,80},{80,64},{96,112},{112,96},{1... | collective-permute-start | bytes 1179656 | tf_op jit(solution)/shard_map/ppermute | solution.py:232
  50.2 6.9 %collective-permute-start.8 = (bf16[2,64,1536]{2,1,0:T(8,128)(2,1)}, bf16[2,64,1536]{2,1,0:T(8,128)(2,1)}, u32[]{:S(2)}, u32[]{:S(2)}) collective-permute-start(bf16[2,64,1536]{2,1,0:T(8,128)(2,1)} %collective-permute-done.4.refs_3_), channel_id=1, source_target_pairs={{0,16},{16,0},{32,48},{48,32},{64,80},{80,64},{96,112},{112,96},{1... | collective-permute-start | bytes 1179656 | tf_op jit(solution)/shard_map/ppermute | solution.py:232
  52.1 5.0 %copy-start.7 = (bf16[64,1536]{1,0:T(8,128)(2,1)}, bf16[64,1536]{1,0:T(8,128)(2,1)S(1)}, u32[]{:S(2)}) copy-start(bf16[64,1536]{1,0:T(8,128)(2,1)S(1)} %collective-permute-done.5.refs_4_) | copy-start | bytes 589828
  52.1 5.0 %collective-permute-start.9 = (bf16[64,1536]{1,0:T(8,128)(2,1)S(1)}, bf16[64,1536]{1,0:T(8,128)(2,1)}, u32[]{:S(2)}, u32[]{:S(2)}) collective-permute-start(bf16[64,1536]{1,0:T(8,128)(2,1)S(1)} %collective-permute-done.5.refs_4_), channel_id=1, source_target_pairs={{0,16},{16,0},{32,48},{48,32},{64,80},{80,64},{96,112},{112,96},{1... | collective-permute-start | bytes 589832 | tf_op jit(solution)/shard_map/ppermute | solution.py:232
  63.9 55.7 %copy-start = (f32[8,64,128]{2,1,0:T(8,128)S(1)}, f32[8,64,128]{2,1,0:T(8,128)}, u32[]{:S(2)}) copy-start(f32[8,64,128]{2,1,0:T(8,128)} %table_ref.1) | copy-start | bytes 786436
  64.0 55.7 %copy-start.1 = (f32[8,64,128]{2,1,0:T(8,128)S(1)}, f32[8,64,128]{2,1,0:T(8,128)}, u32[]{:S(2)}) copy-start(f32[8,64,128]{2,1,0:T(8,128)} %accum_ref.1) | copy-start | bytes 786436
  64.0 55.7 %copy-start.2 = (s32[8,16]{1,0:T(8,128)S(1)}, s32[8,16]{1,0:T(8,128)}, u32[]{:S(2)}) copy-start(s32[8,16]{1,0:T(8,128)} %ids_ref.1) | copy-start | bytes 1540
  113.9 5.7 %collective-permute-start.10 = (f32[64,128]{1,0:T(8,128)S(1)}, f32[64,128]{1,0:T(8,128)S(1)}, u32[]{:S(2)}, u32[]{:S(2)}) collective-permute-start(f32[64,128]{1,0:T(8,128)S(1)} %shard_map.108.mine_ref), channel_id=1, source_target_pairs={{0,16},{16,0},{32,48},{48,32},{64,80},{80,64},{96,112},{112,96},{1... | collective-permute-start | bytes 98312 | tf_op jit(solution)/shard_map/ppermute | solution.py:276

commit v7 on v6

--- a/solution.py
+++ b/solution.py
@@ -71,12 +71,12 @@
     return moves
 
 
-def call(body, out_shape, in_specs, scratch=(), flops=0, nbytes=0, limit=16):
+def call(body, out_shape, in_specs, scratch=(), flops=0, nbytes=0, limit=16, out=VMEM):
     return pl.pallas_call(
         body,
         out_shape=out_shape,
         in_specs=in_specs,
-        out_specs=jax.tree.map(lambda _: VMEM, out_shape),
+        out_specs=jax.tree.map(lambda _: out, out_shape),
         scratch_shapes=list(scratch),
         compiler_params=pltpu.CompilerParams(vmem_limit_bytes=limit * MIB),
         cost_estimate=pl.CostEstimate(flops=flops, bytes_accessed=nbytes, transcendentals=0),
@@ -92,6 +92,22 @@
     for copy in copies:
         copy.start()
     for copy in copies:
+        copy.wait()
+
+
+def regroup_body(counts_ref, out_ref, held, sems):
+    owners, bags = held.shape[0], held.shape[3]
+    reads = [
+        pltpu.make_async_copy(counts_ref.at[:, :, pl.ds(n * bags, bags)], held.at[n], sems.at[0, n])
+        for n in range(owners)
+    ]
+    writes = [pltpu.make_async_copy(held.at[n], out_ref.at[n], sems.at[1, n]) for n in range(owners)]
+    for copy in reads:
+        copy.start()
+    for read, write in zip(reads, writes):
+        read.wait()
+        write.start()
+    for copy in writes:
         copy.wait()
 
 
@@ -221,7 +237,15 @@
     )(in_hbm(w_first), in_hbm(w_second))
     moved = lax.ppermute(shard, ("wide", "narrow"), shard_moves(owners))
     counts, _ = lax.optimization_barrier((counts, shard))
-    by_owner = jnp.transpose(counts.reshape(tables, act, owners, samples), (2, 0, 1, 3))
+    by_owner = call(
+        regroup_body,
+        pltpu.HBM((owners, tables, act, samples), bf16),
+        [HBM],
+        [pltpu.VMEM((owners, tables, act, samples), bf16), pltpu.SemaphoreType.DMA((2, owners))],
+        nbytes=4 * MIB,
+        limit=8,
+        out=HBM,
+    )(in_hbm(counts))
     regrouped = lax.all_to_all(by_owner, "narrow", 0, 0, tiled=True)
     whole = jnp.stack([moved, lax.ppermute(moved, "wide", CORE_SWAP)])
     ahead2 = lax.ppermute(whole, "wide", y_shift(2))
@@ -243,7 +267,7 @@
             pltpu.VMEM(cotangent.shape, bf16),
             pltpu.SemaphoreType.DMA((2, N_Y * N_CORE + 1)),
         ],
-        flops=35 * samples * inner * (2 * inner + top) // 2,
+        flops=34 * samples * inner * (2 * inner + top) // 2,
         nbytes=8 * MIB,
     )(place, *map(in_hbm, (whole, *ring, *swapped, pooled, cotangent)), b_first.reshape(1, -1))
 

time: 122 us -> 121 us (level)
  local copies, waits for them, and re-layouts: 3.31 us -> 0.06 us
  Pallas kernels: 9.54 us -> 12.2 us
    reshape x1 -> x0, local copies, waits for them, and re-layouts: 3.25 us -> none  [shards(): counts.reshape(tables, act, owners, samples)]
    pallas_call x0 -> x1, Pallas kernels: none -> 2.62 us  [shards(): call(regroup_body, pltpu.HBM((owners, tables, act, samples), bf16), [HBM]...]
  transfers between devices with their start and end apart: 12 -> 12, of which waited for: 4 -> 4; matrix products, arithmetic and copies ran while one was open for 3% -> 0% of each run, Pallas kernels for 5% -> 7%
where the time goes in v7:
time: 121 us
  blocking collectives  49.7 us (41%)
  starting transfers between devices  48.2 us (40%)
  Pallas kernels  12.2 us (10%)
  waiting for transfers between devices  9.33 us (8%)
    all_to_all x1, blocking collectives, shards(): lax.all_to_all(copies, 'wide', 0, 0, axis_index_groups=HY_GROUPS, tiled=T...  25.9 us
    all_to_all x1, blocking collectives, shards(): lax.all_to_all(parts.reshape(owners * quarters, act, -1), ('wide', 'narro...  23.8 us
    all_to_all x1, starting transfers between devices, shards(): regrouped = lax.all_to_all(by_owner, 'narrow', 0, 0, tiled=True)  10.4 us
    ppermute x4, starting transfers between devices, shards(): swapped = [lax.ppermute(block, 'wide', CORE_SWAP) for block in ring]  10 us
    ppermute x1, starting transfers between devices, shards(): ahead2 = lax.ppermute(whole, 'wide', y_shift(2))  7.07 us
    ppermute x1, waiting for transfers between devices, shards(): ahead2 = lax.ppermute(whole, 'wide', y_shift(2))  6.33 us
    pallas_call x1, Pallas kernels, shards(): call(tower_body, jax.ShapeDtypeStruct((samples, owners * w_first.shape[0]...  6.04 us
    ppermute x1, starting transfers between devices, shards(): theirs = lax.ppermute(mine, 'wide', CORE_SWAP)  4.86 us
  transfers between devices with their start and end apart: 12, of which 4 were waited for; matrix products, arithmetic and copies ran while one was open for 0% of the time, Pallas kernels for 7%

profile of v7, /device:TPU:1, one launch (start us, length us, event | category | flops | bytes accessed | tf_op | source)
XLA Modules:
  0.0 120.5 jit_solution(3717998522048513618)
XLA Ops:
  0.6 0.9 shard_map.104
  1.6 0.7 collective-permute-start
  2.2 2.6 %shard_map.105 = bf16[16,8,16,512]{3,2,1,0:T(8,128)(2,1)} custom-call(bf16[8,16,8192]{2,1,0:T(8,128)(2,1)} %counts_ref), custom_call_target="tpu_custom_call" | custom-call | bytes 4194304 | tf_op jit(solution)/shard_map/pallas_call | solution.py:240
  4.9 0.0 copy-start.3
  4.9 10.4 %all-to-all-start = ((bf16[16,8,16,512]{3,2,1,0:T(8,128)(2,1)}), bf16[16,8,16,512]{3,2,1,0:T(8,128)(2,1)S(1)}, u32[]{:S(2)}, u32[]{:S(2)}) async-start(bf16[16,8,16,512]{3,2,1,0:T(8,128)(2,1)} %shard_map.105), calls=%async_computation | async-start | bytes 4194304 | tf_op jit(solution)/shard_map/all_to_all | solution.py:249
  15.3 0.0 collective-permute-done
  15.3 4.7 %collective-permute-start.1 = (bf16[64,1536]{1,0:T(8,128)(2,1)S(1)}, bf16[64,1536]{1,0:T(8,128)(2,1)S(1)}, u32[]{:S(2)}, u32[]{:S(2)}) collective-permute-start(bf16[64,1536]{1,0:T(8,128)(2,1)S(1)} %collective-permute-done), channel_id=1, source_target_pairs={{0,16},{16,0},{32,48},{48,32},{64,80},{80,64},{96,112},{112,96},{1... | collective-permute-start | bytes 589832 | tf_op jit(solution)/shard_map/ppermute | solution.py:250
  20.0 1.0 collective-permute-done.1
  21.1 7.1 %collective-permute-start.3 = (bf16[2,64,1536]{2,1,0:T(8,128)(2,1)S(1)}, bf16[2,64,1536]{2,1,0:T(8,128)(2,1)S(1)}, u32[]{:S(2)}, u32[]{:S(2)}) collective-permute-start(bf16[2,64,1536]{2,1,0:T(8,128)(2,1)S(1)} %pad_maximum_fusion.refs_0_), channel_id=1, source_target_pairs={{0,128},{16,400},{32,160},{48,432},{64,192},{80,464},{96,224},{112... | collective-permute-start | bytes 1179656 | tf_op jit(solution)/shard_map/ppermute | solution.py:251
  28.1 2.4 %collective-permute-start.2 = (bf16[2,64,1536]{2,1,0:T(8,128)(2,1)S(1)}, bf16[2,64,1536]{2,1,0:T(8,128)(2,1)S(1)}, u32[]{:S(2)}, u32[]{:S(2)}) collective-permute-start(bf16[2,64,1536]{2,1,0:T(8,128)(2,1)S(1)} %pad_maximum_fusion.refs_0_), channel_id=1, source_target_pairs={{0,64},{16,464},{32,96},{48,496},{64,128},{80,16},{96,160},{112,48... | collective-permute-start | bytes 1179656 | tf_op jit(solution)/shard_map/ppermute | solution.py:252
  30.6 6.3 %collective-permute-done.3.refs_2_ = bf16[2,64,1536]{2,1,0:T(8,128)(2,1)S(1)} collective-permute-done((bf16[2,64,1536]{2,1,0:T(8,128)(2,1)S(1)}, bf16[2,64,1536]{2,1,0:T(8,128)(2,1)S(1)}, u32[]{:S(2)}, u32[]{:S(2)}) %collective-permute-start.3) | collective-permute-done | bytes 393248 | tf_op jit(solution)/shard_map/ppermute | solution.py:251
  36.9 4.1 %collective-permute-start.4 = (bf16[2,64,1536]{2,1,0:T(8,128)(2,1)S(1)}, bf16[2,64,1536]{2,1,0:T(8,128)(2,1)}, u32[]{:S(2)}, u32[]{:S(2)}) collective-permute-start(bf16[2,64,1536]{2,1,0:T(8,128)(2,1)S(1)} %collective-permute-done.3.refs_2_), channel_id=1, source_target_pairs={{0,64},{16,464},{32,96},{48,496},{64,128},{80,16},{96,160},{112,48... | collective-permute-start | bytes 1179656 | tf_op jit(solution)/shard_map/ppermute | solution.py:253
  41.1 4.0 %collective-permute-start.5 = (bf16[64,1536]{1,0:T(8,128)(2,1)S(1)}, bf16[64,1536]{1,0:T(8,128)(2,1)S(1)}, u32[]{:S(2)}, u32[]{:S(2)}) collective-permute-start(bf16[64,1536]{1,0:T(8,128)(2,1)S(1)} %slice_bitcast_fusion), channel_id=1, source_target_pairs={{0,128},{16,400},{32,160},{48,432},{64,192},{80,464},{96,224},{112... | collective-permute-start | bytes 589832 | tf_op jit(solution)/shard_map/ppermute | solution.py:254
  45.1 1.9 %collective-permute-start.7 = (bf16[2,64,1536]{2,1,0:T(8,128)(2,1)S(1)}, bf16[2,64,1536]{2,1,0:T(8,128)(2,1)}, u32[]{:S(2)}, u32[]{:S(2)}) collective-permute-start(bf16[2,64,1536]{2,1,0:T(8,128)(2,1)S(1)} %collective-permute-done.3.refs_2_), channel_id=1, source_target_pairs={{0,16},{16,0},{32,48},{48,32},{64,80},{80,64},{96,112},{112,96},{1... | collective-permute-start | bytes 1179656 | tf_op jit(solution)/shard_map/ppermute | solution.py:256
  47.0 2.4 %collective-permute-start.6 = (bf16[2,64,1536]{2,1,0:T(8,128)(2,1)S(1)}, bf16[2,64,1536]{2,1,0:T(8,128)(2,1)}, u32[]{:S(2)}, u32[]{:S(2)}) collective-permute-start(bf16[2,64,1536]{2,1,0:T(8,128)(2,1)S(1)} %collective-permute-done.2.refs_1_), channel_id=1, source_target_pairs={{0,16},{16,0},{32,48},{48,32},{64,80},{80,64},{96,112},{112,96},{1... | collective-permute-start | bytes 1179656 | tf_op jit(solution)/shard_map/ppermute | solution.py:256
  49.4 0.0 collective-permute-done.4.refs_3_
  49.5 1.9 %collective-permute-start.8 = (bf16[2,64,1536]{2,1,0:T(8,128)(2,1)}, bf16[2,64,1536]{2,1,0:T(8,128)(2,1)}, u32[]{:S(2)}, u32[]{:S(2)}) collective-permute-start(bf16[2,64,1536]{2,1,0:T(8,128)(2,1)} %collective-permute-done.4.refs_3_), channel_id=1, source_target_pairs={{0,16},{16,0},{32,48},{48,32},{64,80},{80,64},{96,112},{112,96},{1... | collective-permute-start | bytes 1179656 | tf_op jit(solution)/shard_map/ppermute | solution.py:256
  51.4 0.0 copy-start.7
  51.4 3.8 %collective-permute-start.9 = (bf16[64,1536]{1,0:T(8,128)(2,1)S(1)}, bf16[64,1536]{1,0:T(8,128)(2,1)}, u32[]{:S(2)}, u32[]{:S(2)}) collective-permute-start(bf16[64,1536]{1,0:T(8,128)(2,1)S(1)} %collective-permute-done.5.refs_4_), channel_id=1, source_target_pairs={{0,16},{16,0},{32,48},{48,32},{64,80},{80,64},{96,112},{112,96},{1... | collective-permute-start | bytes 589832 | tf_op jit(solution)/shard_map/ppermute | solution.py:256
  55.2 0.1 pad_add_fusion.at_ref
  55.3 1.1 collective-permute-done.9.refs_8_
  56.4 6.0 %shard_map.106.grad_ref = bf16[512,1024]{1,0:T(8,128)(2,1)S(1)} custom-call(s32[4]{0:T(128)S(1)} %pad_add_fusion.at_ref, bf16[2,64,1536]{2,1,0:T(8,128)(2,1)} %copy-done.4, bf16[2,64,1536]{2,1,0:T(8,128)(2,1)} %copy-done.6, bf16[2,64,1536]{2,1,0:T(8,128)(2,1)} %copy-done.5, bf16[2,64,1536]{2,1,0:T(8,128)(2,1)} %collective-permute-done.4.refs_3_, ...), custom_call_target="tpu_custom_call" | custom-call | flops 22817013760 | bytes 8388608 | tf_op jit(solution)/shard_map/pallas_call | solution.py:258
  62.5 0.7 shard_map.107
  63.2 0.0 copy-start
  63.2 0.0 copy-start.1
  63.2 0.0 copy-start.2
  63.3 23.8 %all_to_all.15 = bf16[32,16,512]{2,1,0:T(8,128)(2,1)S(1)} all-to-all(bf16[32,16,512]{2,1,0:T(8,128)(2,1)S(1)} %bitcast.11), channel_id=1, replica_groups={{0,1,2,3,4,5,6,7,8,9,10,11,12,13,14,15,16,17,18,19,20,21,22,23,24,25,26..., dimensions={0} | all-to-all | bytes 1048576 | tf_op jit(solution)/shard_map/all_to_all | solution.py:282
  87.0 0.2 shard_map.108
  87.2 25.9 %all_to_all.16.parts_ref = bf16[16,64,128]{2,1,0:T(8,128)(2,1)S(1)} all-to-all(bf16[16,64,128]{2,1,0:T(8,128)(2,1)S(1)} %shard_map.108), channel_id=1, replica_groups={{0,64,128,192,256,320,384,448,32,96,160,224,288,352,416,480},{16,80,144..., dimensions={0} | all-to-all | bytes 524288 | tf_op jit(solution)/shard_map/all_to_all | solution.py:298
  113.2 4.9 %collective-permute-start.10 = (f32[64,128]{1,0:T(8,128)S(1)}, f32[64,128]{1,0:T(8,128)S(1)}, u32[]{:S(2)}, u32[]{:S(2)}) collective-permute-start(f32[64,128]{1,0:T(8,128)S(1)} %shard_map.109.mine_ref), channel_id=1, source_target_pairs={{0,16},{16,0},{32,48},{48,32},{64,80},{80,64},{96,112},{112,96},{1... | collective-permute-start | bytes 98312 | tf_op jit(solution)/shard_map/ppermute | solution.py:300
  118.1 0.8 collective-permute-done.10.other_ref
  118.9 1.6 %shard_map.110 = (f32[8,64,128]{2,1,0:T(8,128)}, f32[8,64,128]{2,1,0:T(8,128)}) custom-call(s32[4]{0:T(128)S(1)} %pad_add_fusion.at_ref, s32[8,16]{1,0:T(8,128)S(1)} %copy-done.2, f32[64,128]{1,0:T(8,128)S(1)} %shard_map.109.mine_ref, f32[64,128]{1,0:T(8,128)S(1)} %collective-permute-done.10.other_ref, f32[8,64,128]{2,1,0:T(8,128)S(1)} %copy-done, ...), custom_call_target="tpu_custom_call" | custom-call | bytes 2097152 | tf_op jit(solution)/shard_map/pallas_call | solution.py:302
  (20 shorter events, 0.1 us)
Async XLA Ops:
  1.6 13.7 %collective-permute-start = (bf16[64,1536]{1,0:T(8,128)(2,1)S(1)}, bf16[64,1536]{1,0:T(8,128)(2,1)S(1)}, u32[]{:S(2)}, u32[]{:S(2)}) collective-permute-start(bf16[64,1536]{1,0:T(8,128)(2,1)S(1)} %shard_map.104), channel_id=1, source_target_pairs={{0,8},{1,9},{2,10},{3,11},{4,12},{5,13},{6,14},{7,15},{8,0},{9,1},... | collective-permute-start | bytes 589832 | tf_op jit(solution)/shard_map/ppermute | solution.py:238
  4.9 51.6 %copy-start.3 = (f32[1024]{0:T(1024)S(1)}, f32[1024]{0:T(1024)}, u32[]{:S(2)}) copy-start(f32[1024]{0:T(1024)} %param.12) | copy-start | bytes 12292
  4.9 57.6 %all-to-all-start = ((bf16[16,8,16,512]{3,2,1,0:T(8,128)(2,1)}), bf16[16,8,16,512]{3,2,1,0:T(8,128)(2,1)S(1)}, u32[]{:S(2)}, u32[]{:S(2)}) async-start(bf16[16,8,16,512]{3,2,1,0:T(8,128)(2,1)} %shard_map.105), calls=%async_computation | async-start | bytes 4194304 | tf_op jit(solution)/shard_map/all_to_all | solution.py:249
  15.3 5.7 %collective-permute-start.1 = (bf16[64,1536]{1,0:T(8,128)(2,1)S(1)}, bf16[64,1536]{1,0:T(8,128)(2,1)S(1)}, u32[]{:S(2)}, u32[]{:S(2)}) collective-permute-start(bf16[64,1536]{1,0:T(8,128)(2,1)S(1)} %collective-permute-done), channel_id=1, source_target_pairs={{0,16},{16,0},{32,48},{48,32},{64,80},{80,64},{96,112},{112,96},{1... | collective-permute-start | bytes 589832 | tf_op jit(solution)/shard_map/ppermute | solution.py:250
  21.1 35.4 %copy-start.4 = (bf16[2,64,1536]{2,1,0:T(8,128)(2,1)}, bf16[2,64,1536]{2,1,0:T(8,128)(2,1)S(1)}, u32[]{:S(2)}) copy-start(bf16[2,64,1536]{2,1,0:T(8,128)(2,1)S(1)} %pad_maximum_fusion.refs_0_) | copy-start | bytes 1179652
  21.1 15.8 %collective-permute-start.3 = (bf16[2,64,1536]{2,1,0:T(8,128)(2,1)S(1)}, bf16[2,64,1536]{2,1,0:T(8,128)(2,1)S(1)}, u32[]{:S(2)}, u32[]{:S(2)}) collective-permute-start(bf16[2,64,1536]{2,1,0:T(8,128)(2,1)S(1)} %pad_maximum_fusion.refs_0_), channel_id=1, source_target_pairs={{0,128},{16,400},{32,160},{48,432},{64,192},{80,464},{96,224},{112... | collective-permute-start | bytes 1179656 | tf_op jit(solution)/shard_map/ppermute | solution.py:251
  28.1 18.9 %collective-permute-start.2 = (bf16[2,64,1536]{2,1,0:T(8,128)(2,1)S(1)}, bf16[2,64,1536]{2,1,0:T(8,128)(2,1)S(1)}, u32[]{:S(2)}, u32[]{:S(2)}) collective-permute-start(bf16[2,64,1536]{2,1,0:T(8,128)(2,1)S(1)} %pad_maximum_fusion.refs_0_), channel_id=1, source_target_pairs={{0,64},{16,464},{32,96},{48,496},{64,128},{80,16},{96,160},{112,48... | collective-permute-start | bytes 1179656 | tf_op jit(solution)/shard_map/ppermute | solution.py:252
  36.9 19.5 %copy-start.5 = (bf16[2,64,1536]{2,1,0:T(8,128)(2,1)}, bf16[2,64,1536]{2,1,0:T(8,128)(2,1)S(1)}, u32[]{:S(2)}) copy-start(bf16[2,64,1536]{2,1,0:T(8,128)(2,1)S(1)} %collective-permute-done.3.refs_2_) | copy-start | bytes 1179652
  36.9 12.5 %collective-permute-start.4 = (bf16[2,64,1536]{2,1,0:T(8,128)(2,1)S(1)}, bf16[2,64,1536]{2,1,0:T(8,128)(2,1)}, u32[]{:S(2)}, u32[]{:S(2)}) collective-permute-start(bf16[2,64,1536]{2,1,0:T(8,128)(2,1)S(1)} %collective-permute-done.3.refs_2_), channel_id=1, source_target_pairs={{0,64},{16,464},{32,96},{48,496},{64,128},{80,16},{96,160},{112,48... | collective-permute-start | bytes 1179656 | tf_op jit(solution)/shard_map/ppermute | solution.py:253
  41.1 10.3 %collective-permute-start.5 = (bf16[64,1536]{1,0:T(8,128)(2,1)S(1)}, bf16[64,1536]{1,0:T(8,128)(2,1)S(1)}, u32[]{:S(2)}, u32[]{:S(2)}) collective-permute-start(bf16[64,1536]{1,0:T(8,128)(2,1)S(1)} %slice_bitcast_fusion), channel_id=1, source_target_pairs={{0,128},{16,400},{32,160},{48,432},{64,192},{80,464},{96,224},{112... | collective-permute-start | bytes 589832 | tf_op jit(solution)/shard_map/ppermute | solution.py:254
  45.1 11.3 %collective-permute-start.7 = (bf16[2,64,1536]{2,1,0:T(8,128)(2,1)S(1)}, bf16[2,64,1536]{2,1,0:T(8,128)(2,1)}, u32[]{:S(2)}, u32[]{:S(2)}) collective-permute-start(bf16[2,64,1536]{2,1,0:T(8,128)(2,1)S(1)} %collective-permute-done.3.refs_2_), channel_id=1, source_target_pairs={{0,16},{16,0},{32,48},{48,32},{64,80},{80,64},{96,112},{112,96},{1... | collective-permute-start | bytes 1179656 | tf_op jit(solution)/shard_map/ppermute | solution.py:256
  47.0 9.4 %copy-start.6 = (bf16[2,64,1536]{2,1,0:T(8,128)(2,1)}, bf16[2,64,1536]{2,1,0:T(8,128)(2,1)S(1)}, u32[]{:S(2)}) copy-start(bf16[2,64,1536]{2,1,0:T(8,128)(2,1)S(1)} %collective-permute-done.2.refs_1_) | copy-start | bytes 1179652
  47.0 9.4 %collective-permute-start.6 = (bf16[2,64,1536]{2,1,0:T(8,128)(2,1)S(1)}, bf16[2,64,1536]{2,1,0:T(8,128)(2,1)}, u32[]{:S(2)}, u32[]{:S(2)}) collective-permute-start(bf16[2,64,1536]{2,1,0:T(8,128)(2,1)S(1)} %collective-permute-done.2.refs_1_), channel_id=1, source_target_pairs={{0,16},{16,0},{32,48},{48,32},{64,80},{80,64},{96,112},{112,96},{1... | collective-permute-start | bytes 1179656 | tf_op jit(solution)/shard_map/ppermute | solution.py:256
  49.5 6.9 %collective-permute-start.8 = (bf16[2,64,1536]{2,1,0:T(8,128)(2,1)}, bf16[2,64,1536]{2,1,0:T(8,128)(2,1)}, u32[]{:S(2)}, u32[]{:S(2)}) collective-permute-start(bf16[2,64,1536]{2,1,0:T(8,128)(2,1)} %collective-permute-done.4.refs_3_), channel_id=1, source_target_pairs={{0,16},{16,0},{32,48},{48,32},{64,80},{80,64},{96,112},{112,96},{1... | collective-permute-start | bytes 1179656 | tf_op jit(solution)/shard_map/ppermute | solution.py:256
  51.4 5.0 %copy-start.7 = (bf16[64,1536]{1,0:T(8,128)(2,1)}, bf16[64,1536]{1,0:T(8,128)(2,1)S(1)}, u32[]{:S(2)}) copy-start(bf16[64,1536]{1,0:T(8,128)(2,1)S(1)} %collective-permute-done.5.refs_4_) | copy-start | bytes 589828
  51.4 5.0 %collective-permute-start.9 = (bf16[64,1536]{1,0:T(8,128)(2,1)S(1)}, bf16[64,1536]{1,0:T(8,128)(2,1)}, u32[]{:S(2)}, u32[]{:S(2)}) collective-permute-start(bf16[64,1536]{1,0:T(8,128)(2,1)S(1)} %collective-permute-done.5.refs_4_), channel_id=1, source_target_pairs={{0,16},{16,0},{32,48},{48,32},{64,80},{80,64},{96,112},{112,96},{1... | collective-permute-start | bytes 589832 | tf_op jit(solution)/shard_map/ppermute | solution.py:256
  63.2 55.7 %copy-start = (f32[8,64,128]{2,1,0:T(8,128)S(1)}, f32[8,64,128]{2,1,0:T(8,128)}, u32[]{:S(2)}) copy-start(f32[8,64,128]{2,1,0:T(8,128)} %table_ref.1) | copy-start | bytes 786436
  63.2 55.7 %copy-start.1 = (f32[8,64,128]{2,1,0:T(8,128)S(1)}, f32[8,64,128]{2,1,0:T(8,128)}, u32[]{:S(2)}) copy-start(f32[8,64,128]{2,1,0:T(8,128)} %accum_ref.1) | copy-start | bytes 786436
  63.2 55.7 %copy-start.2 = (s32[8,16]{1,0:T(8,128)S(1)}, s32[8,16]{1,0:T(8,128)}, u32[]{:S(2)}) copy-start(s32[8,16]{1,0:T(8,128)} %ids_ref.1) | copy-start | bytes 1540
  113.2 5.7 %collective-permute-start.10 = (f32[64,128]{1,0:T(8,128)S(1)}, f32[64,128]{1,0:T(8,128)S(1)}, u32[]{:S(2)}, u32[]{:S(2)}) collective-permute-start(f32[64,128]{1,0:T(8,128)S(1)} %shard_map.109.mine_ref), channel_id=1, source_target_pairs={{0,16},{16,0},{32,48},{48,32},{64,80},{80,64},{96,112},{112,96},{1... | collective-permute-start | bytes 98312 | tf_op jit(solution)/shard_map/ppermute | solution.py:300

commit v8 on v7

--- a/solution.py
+++ b/solution.py
@@ -48,7 +48,7 @@
     ]
 
 
-HY_GROUPS = [[wide_at(y, h, c) for h in range(N_HI) for y in range(N_Y)] for c in range(N_CORE)]
+HY_GROUPS = [[wide_at(y, h, c) for h in (1, 0) for y in range(N_Y - 1, -1, -1)] for c in range(N_CORE)]
 N_X = 4
 
 

time: 121 us -> 117 us (0.967)
  blocking collectives: 49.7 us -> 44.4 us
    all_to_all x1, blocking collectives: 25.9 us -> 20.6 us  [shards(): lax.all_to_all(copies, 'wide', 0, 0, axis_index_groups=HY_GROUPS, tiled=T...]
where the time goes in v8:
time: 117 us; the launch traced here: 116 us
  starting transfers between devices  49.2 us (42%)
  blocking collectives  44.4 us (38%)
  Pallas kernels  12.2 us (10%)
  waiting for transfers between devices  9.33 us (8%)
    all_to_all x1, blocking collectives, shards(): lax.all_to_all(parts.reshape(owners * quarters, act, -1), ('wide', 'narro...  23.8 us
    all_to_all x1, blocking collectives, shards(): lax.all_to_all(copies, 'wide', 0, 0, axis_index_groups=HY_GROUPS, tiled=T...  20.6 us
    all_to_all x1, starting transfers between devices, shards(): regrouped = lax.all_to_all(by_owner, 'narrow', 0, 0, tiled=True)  10.4 us
    ppermute x4, starting transfers between devices, shards(): swapped = [lax.ppermute(block, 'wide', CORE_SWAP) for block in ring]  10 us
    ppermute x1, starting transfers between devices, shards(): ahead2 = lax.ppermute(whole, 'wide', y_shift(2))  7.07 us
    ppermute x1, waiting for transfers between devices, shards(): ahead2 = lax.ppermute(whole, 'wide', y_shift(2))  6.33 us
    pallas_call x1, Pallas kernels, shards(): call(tower_body, jax.ShapeDtypeStruct((samples, owners * w_first.shape[0]...  6.04 us
    ppermute x1, starting transfers between devices, shards(): theirs = lax.ppermute(mine, 'wide', CORE_SWAP)  5.85 us
  transfers between devices with their start and end apart: 12, of which 4 were waited for; matrix products, arithmetic and copies ran while one was open for 0% of the time, Pallas kernels for 7%

profile of v8, /device:TPU:1, one launch (start us, length us, event | category | flops | bytes accessed | tf_op | source)
XLA Modules:
  0.0 116.2 jit_solution(799305776161684559)
XLA Ops:
  0.6 0.9 shard_map.104
  1.6 0.7 collective-permute-start
  2.2 2.6 %shard_map.105 = bf16[16,8,16,512]{3,2,1,0:T(8,128)(2,1)} custom-call(bf16[8,16,8192]{2,1,0:T(8,128)(2,1)} %counts_ref), custom_call_target="tpu_custom_call" | custom-call | bytes 4194304 | tf_op jit(solution)/shard_map/pallas_call | solution.py:240
  4.9 0.0 copy-start.3
  4.9 10.4 %all-to-all-start = ((bf16[16,8,16,512]{3,2,1,0:T(8,128)(2,1)}), bf16[16,8,16,512]{3,2,1,0:T(8,128)(2,1)S(1)}, u32[]{:S(2)}, u32[]{:S(2)}) async-start(bf16[16,8,16,512]{3,2,1,0:T(8,128)(2,1)} %shard_map.105), calls=%async_computation | async-start | bytes 4194304 | tf_op jit(solution)/shard_map/all_to_all | solution.py:249
  15.3 4.7 %collective-permute-start.1 = (bf16[64,1536]{1,0:T(8,128)(2,1)S(1)}, bf16[64,1536]{1,0:T(8,128)(2,1)S(1)}, u32[]{:S(2)}, u32[]{:S(2)}) collective-permute-start(bf16[64,1536]{1,0:T(8,128)(2,1)S(1)} %collective-permute-done), channel_id=1, source_target_pairs={{0,16},{16,0},{32,48},{48,32},{64,80},{80,64},{96,112},{112,96},{1... | collective-permute-start | bytes 589832 | tf_op jit(solution)/shard_map/ppermute | solution.py:250
  20.0 1.0 collective-permute-done.1
  21.1 7.1 %collective-permute-start.3 = (bf16[2,64,1536]{2,1,0:T(8,128)(2,1)S(1)}, bf16[2,64,1536]{2,1,0:T(8,128)(2,1)S(1)}, u32[]{:S(2)}, u32[]{:S(2)}) collective-permute-start(bf16[2,64,1536]{2,1,0:T(8,128)(2,1)S(1)} %pad_maximum_fusion.refs_0_), channel_id=1, source_target_pairs={{0,128},{16,400},{32,160},{48,432},{64,192},{80,464},{96,224},{112... | collective-permute-start | bytes 1179656 | tf_op jit(solution)/shard_map/ppermute | solution.py:251
  28.1 2.4 %collective-permute-start.2 = (bf16[2,64,1536]{2,1,0:T(8,128)(2,1)S(1)}, bf16[2,64,1536]{2,1,0:T(8,128)(2,1)S(1)}, u32[]{:S(2)}, u32[]{:S(2)}) collective-permute-start(bf16[2,64,1536]{2,1,0:T(8,128)(2,1)S(1)} %pad_maximum_fusion.refs_0_), channel_id=1, source_target_pairs={{0,64},{16,464},{32,96},{48,496},{64,128},{80,16},{96,160},{112,48... | collective-permute-start | bytes 1179656 | tf_op jit(solution)/shard_map/ppermute | solution.py:252
  30.6 6.3 %collective-permute-done.3.refs_2_ = bf16[2,64,1536]{2,1,0:T(8,128)(2,1)S(1)} collective-permute-done((bf16[2,64,1536]{2,1,0:T(8,128)(2,1)S(1)}, bf16[2,64,1536]{2,1,0:T(8,128)(2,1)S(1)}, u32[]{:S(2)}, u32[]{:S(2)}) %collective-permute-start.3) | collective-permute-done | bytes 393248 | tf_op jit(solution)/shard_map/ppermute | solution.py:251
  36.9 4.1 %collective-permute-start.4 = (bf16[2,64,1536]{2,1,0:T(8,128)(2,1)S(1)}, bf16[2,64,1536]{2,1,0:T(8,128)(2,1)}, u32[]{:S(2)}, u32[]{:S(2)}) collective-permute-start(bf16[2,64,1536]{2,1,0:T(8,128)(2,1)S(1)} %collective-permute-done.3.refs_2_), channel_id=1, source_target_pairs={{0,64},{16,464},{32,96},{48,496},{64,128},{80,16},{96,160},{112,48... | collective-permute-start | bytes 1179656 | tf_op jit(solution)/shard_map/ppermute | solution.py:253
  41.1 4.0 %collective-permute-start.5 = (bf16[64,1536]{1,0:T(8,128)(2,1)S(1)}, bf16[64,1536]{1,0:T(8,128)(2,1)S(1)}, u32[]{:S(2)}, u32[]{:S(2)}) collective-permute-start(bf16[64,1536]{1,0:T(8,128)(2,1)S(1)} %slice_bitcast_fusion), channel_id=1, source_target_pairs={{0,128},{16,400},{32,160},{48,432},{64,192},{80,464},{96,224},{112... | collective-permute-start | bytes 589832 | tf_op jit(solution)/shard_map/ppermute | solution.py:254
  45.1 1.9 %collective-permute-start.7 = (bf16[2,64,1536]{2,1,0:T(8,128)(2,1)S(1)}, bf16[2,64,1536]{2,1,0:T(8,128)(2,1)}, u32[]{:S(2)}, u32[]{:S(2)}) collective-permute-start(bf16[2,64,1536]{2,1,0:T(8,128)(2,1)S(1)} %collective-permute-done.3.refs_2_), channel_id=1, source_target_pairs={{0,16},{16,0},{32,48},{48,32},{64,80},{80,64},{96,112},{112,96},{1... | collective-permute-start | bytes 1179656 | tf_op jit(solution)/shard_map/ppermute | solution.py:256
  47.0 2.4 %collective-permute-start.6 = (bf16[2,64,1536]{2,1,0:T(8,128)(2,1)S(1)}, bf16[2,64,1536]{2,1,0:T(8,128)(2,1)}, u32[]{:S(2)}, u32[]{:S(2)}) collective-permute-start(bf16[2,64,1536]{2,1,0:T(8,128)(2,1)S(1)} %collective-permute-done.2.refs_1_), channel_id=1, source_target_pairs={{0,16},{16,0},{32,48},{48,32},{64,80},{80,64},{96,112},{112,96},{1... | collective-permute-start | bytes 1179656 | tf_op jit(solution)/shard_map/ppermute | solution.py:256
  49.4 0.0 collective-permute-done.4.refs_3_
  49.5 1.9 %collective-permute-start.8 = (bf16[2,64,1536]{2,1,0:T(8,128)(2,1)}, bf16[2,64,1536]{2,1,0:T(8,128)(2,1)}, u32[]{:S(2)}, u32[]{:S(2)}) collective-permute-start(bf16[2,64,1536]{2,1,0:T(8,128)(2,1)} %collective-permute-done.4.refs_3_), channel_id=1, source_target_pairs={{0,16},{16,0},{32,48},{48,32},{64,80},{80,64},{96,112},{112,96},{1... | collective-permute-start | bytes 1179656 | tf_op jit(solution)/shard_map/ppermute | solution.py:256
  51.4 0.0 collective-permute-done.5.refs_4_
  51.4 0.0 copy-start.7
  51.4 3.8 %collective-permute-start.9 = (bf16[64,1536]{1,0:T(8,128)(2,1)S(1)}, bf16[64,1536]{1,0:T(8,128)(2,1)}, u32[]{:S(2)}, u32[]{:S(2)}) collective-permute-start(bf16[64,1536]{1,0:T(8,128)(2,1)S(1)} %collective-permute-done.5.refs_4_), channel_id=1, source_target_pairs={{0,16},{16,0},{32,48},{48,32},{64,80},{80,64},{96,112},{112,96},{1... | collective-permute-start | bytes 589832 | tf_op jit(solution)/shard_map/ppermute | solution.py:256
  55.2 0.1 pad_add_fusion.at_ref
  55.3 1.1 collective-permute-done.9.refs_8_
  56.4 6.0 %shard_map.106.grad_ref = bf16[512,1024]{1,0:T(8,128)(2,1)S(1)} custom-call(s32[4]{0:T(128)S(1)} %pad_add_fusion.at_ref, bf16[2,64,1536]{2,1,0:T(8,128)(2,1)} %copy-done.4, bf16[2,64,1536]{2,1,0:T(8,128)(2,1)} %copy-done.6, bf16[2,64,1536]{2,1,0:T(8,128)(2,1)} %copy-done.5, bf16[2,64,1536]{2,1,0:T(8,128)(2,1)} %collective-permute-done.4.refs_3_, ...), custom_call_target="tpu_custom_call" | custom-call | flops 22817013760 | bytes 8388608 | tf_op jit(solution)/shard_map/pallas_call | solution.py:258
  62.5 0.7 shard_map.107
  63.2 0.0 copy-start
  63.2 0.0 copy-start.1
  63.2 0.0 copy-start.2
  63.3 23.8 %all_to_all.15 = bf16[32,16,512]{2,1,0:T(8,128)(2,1)S(1)} all-to-all(bf16[32,16,512]{2,1,0:T(8,128)(2,1)S(1)} %bitcast.11), channel_id=1, replica_groups={{0,1,2,3,4,5,6,7,8,9,10,11,12,13,14,15,16,17,18,19,20,21,22,23,24,25,26..., dimensions={0} | all-to-all | bytes 1048576 | tf_op jit(solution)/shard_map/all_to_all | solution.py:282
  87.0 0.2 shard_map.108
  87.2 20.6 %all_to_all.16.parts_ref = bf16[16,64,128]{2,1,0:T(8,128)(2,1)S(1)} all-to-all(bf16[16,64,128]{2,1,0:T(8,128)(2,1)S(1)} %shard_map.108), channel_id=1, replica_groups={{480,416,352,288,224,160,96,32,448,384,320,256,192,128,64,0},{496,432,3..., dimensions={0} | all-to-all | bytes 524288 | tf_op jit(solution)/shard_map/all_to_all | solution.py:298
  107.8 5.9 %collective-permute-start.10 = (f32[64,128]{1,0:T(8,128)S(1)}, f32[64,128]{1,0:T(8,128)S(1)}, u32[]{:S(2)}, u32[]{:S(2)}) collective-permute-start(f32[64,128]{1,0:T(8,128)S(1)} %shard_map.109.mine_ref), channel_id=1, source_target_pairs={{0,16},{16,0},{32,48},{48,32},{64,80},{80,64},{96,112},{112,96},{1... | collective-permute-start | bytes 98312 | tf_op jit(solution)/shard_map/ppermute | solution.py:300
  113.7 0.8 collective-permute-done.10.other_ref
  114.6 1.6 %shard_map.110 = (f32[8,64,128]{2,1,0:T(8,128)}, f32[8,64,128]{2,1,0:T(8,128)}) custom-call(s32[4]{0:T(128)S(1)} %pad_add_fusion.at_ref, s32[8,16]{1,0:T(8,128)S(1)} %copy-done.2, f32[64,128]{1,0:T(8,128)S(1)} %shard_map.109.mine_ref, f32[64,128]{1,0:T(8,128)S(1)} %collective-permute-done.10.other_ref, f32[8,64,128]{2,1,0:T(8,128)S(1)} %copy-done, ...), custom_call_target="tpu_custom_call" | custom-call | bytes 2097152 | tf_op jit(solution)/shard_map/pallas_call | solution.py:302
  (20 shorter events, 0.1 us)
Async XLA Ops:
  1.6 13.7 %collective-permute-start = (bf16[64,1536]{1,0:T(8,128)(2,1)S(1)}, bf16[64,1536]{1,0:T(8,128)(2,1)S(1)}, u32[]{:S(2)}, u32[]{:S(2)}) collective-permute-start(bf16[64,1536]{1,0:T(8,128)(2,1)S(1)} %shard_map.104), channel_id=1, source_target_pairs={{0,8},{1,9},{2,10},{3,11},{4,12},{5,13},{6,14},{7,15},{8,0},{9,1},... | collective-permute-start | bytes 589832 | tf_op jit(solution)/shard_map/ppermute | solution.py:238
  4.9 51.6 %copy-start.3 = (f32[1024]{0:T(1024)S(1)}, f32[1024]{0:T(1024)}, u32[]{:S(2)}) copy-start(f32[1024]{0:T(1024)} %param.12) | copy-start | bytes 12292
  4.9 57.6 %all-to-all-start = ((bf16[16,8,16,512]{3,2,1,0:T(8,128)(2,1)}), bf16[16,8,16,512]{3,2,1,0:T(8,128)(2,1)S(1)}, u32[]{:S(2)}, u32[]{:S(2)}) async-start(bf16[16,8,16,512]{3,2,1,0:T(8,128)(2,1)} %shard_map.105), calls=%async_computation | async-start | bytes 4194304 | tf_op jit(solution)/shard_map/all_to_all | solution.py:249
  15.3 5.7 %collective-permute-start.1 = (bf16[64,1536]{1,0:T(8,128)(2,1)S(1)}, bf16[64,1536]{1,0:T(8,128)(2,1)S(1)}, u32[]{:S(2)}, u32[]{:S(2)}) collective-permute-start(bf16[64,1536]{1,0:T(8,128)(2,1)S(1)} %collective-permute-done), channel_id=1, source_target_pairs={{0,16},{16,0},{32,48},{48,32},{64,80},{80,64},{96,112},{112,96},{1... | collective-permute-start | bytes 589832 | tf_op jit(solution)/shard_map/ppermute | solution.py:250
  21.1 35.4 %copy-start.4 = (bf16[2,64,1536]{2,1,0:T(8,128)(2,1)}, bf16[2,64,1536]{2,1,0:T(8,128)(2,1)S(1)}, u32[]{:S(2)}) copy-start(bf16[2,64,1536]{2,1,0:T(8,128)(2,1)S(1)} %pad_maximum_fusion.refs_0_) | copy-start | bytes 1179652
  21.1 15.8 %collective-permute-start.3 = (bf16[2,64,1536]{2,1,0:T(8,128)(2,1)S(1)}, bf16[2,64,1536]{2,1,0:T(8,128)(2,1)S(1)}, u32[]{:S(2)}, u32[]{:S(2)}) collective-permute-start(bf16[2,64,1536]{2,1,0:T(8,128)(2,1)S(1)} %pad_maximum_fusion.refs_0_), channel_id=1, source_target_pairs={{0,128},{16,400},{32,160},{48,432},{64,192},{80,464},{96,224},{112... | collective-permute-start | bytes 1179656 | tf_op jit(solution)/shard_map/ppermute | solution.py:251
  28.1 18.9 %collective-permute-start.2 = (bf16[2,64,1536]{2,1,0:T(8,128)(2,1)S(1)}, bf16[2,64,1536]{2,1,0:T(8,128)(2,1)S(1)}, u32[]{:S(2)}, u32[]{:S(2)}) collective-permute-start(bf16[2,64,1536]{2,1,0:T(8,128)(2,1)S(1)} %pad_maximum_fusion.refs_0_), channel_id=1, source_target_pairs={{0,64},{16,464},{32,96},{48,496},{64,128},{80,16},{96,160},{112,48... | collective-permute-start | bytes 1179656 | tf_op jit(solution)/shard_map/ppermute | solution.py:252
  36.9 19.5 %copy-start.5 = (bf16[2,64,1536]{2,1,0:T(8,128)(2,1)}, bf16[2,64,1536]{2,1,0:T(8,128)(2,1)S(1)}, u32[]{:S(2)}) copy-start(bf16[2,64,1536]{2,1,0:T(8,128)(2,1)S(1)} %collective-permute-done.3.refs_2_) | copy-start | bytes 1179652
  36.9 12.5 %collective-permute-start.4 = (bf16[2,64,1536]{2,1,0:T(8,128)(2,1)S(1)}, bf16[2,64,1536]{2,1,0:T(8,128)(2,1)}, u32[]{:S(2)}, u32[]{:S(2)}) collective-permute-start(bf16[2,64,1536]{2,1,0:T(8,128)(2,1)S(1)} %collective-permute-done.3.refs_2_), channel_id=1, source_target_pairs={{0,64},{16,464},{32,96},{48,496},{64,128},{80,16},{96,160},{112,48... | collective-permute-start | bytes 1179656 | tf_op jit(solution)/shard_map/ppermute | solution.py:253
  41.1 10.3 %collective-permute-start.5 = (bf16[64,1536]{1,0:T(8,128)(2,1)S(1)}, bf16[64,1536]{1,0:T(8,128)(2,1)S(1)}, u32[]{:S(2)}, u32[]{:S(2)}) collective-permute-start(bf16[64,1536]{1,0:T(8,128)(2,1)S(1)} %slice_bitcast_fusion), channel_id=1, source_target_pairs={{0,128},{16,400},{32,160},{48,432},{64,192},{80,464},{96,224},{112... | collective-permute-start | bytes 589832 | tf_op jit(solution)/shard_map/ppermute | solution.py:254
  45.1 11.3 %collective-permute-start.7 = (bf16[2,64,1536]{2,1,0:T(8,128)(2,1)S(1)}, bf16[2,64,1536]{2,1,0:T(8,128)(2,1)}, u32[]{:S(2)}, u32[]{:S(2)}) collective-permute-start(bf16[2,64,1536]{2,1,0:T(8,128)(2,1)S(1)} %collective-permute-done.3.refs_2_), channel_id=1, source_target_pairs={{0,16},{16,0},{32,48},{48,32},{64,80},{80,64},{96,112},{112,96},{1... | collective-permute-start | bytes 1179656 | tf_op jit(solution)/shard_map/ppermute | solution.py:256
  47.0 9.4 %copy-start.6 = (bf16[2,64,1536]{2,1,0:T(8,128)(2,1)}, bf16[2,64,1536]{2,1,0:T(8,128)(2,1)S(1)}, u32[]{:S(2)}) copy-start(bf16[2,64,1536]{2,1,0:T(8,128)(2,1)S(1)} %collective-permute-done.2.refs_1_) | copy-start | bytes 1179652
  47.0 9.4 %collective-permute-start.6 = (bf16[2,64,1536]{2,1,0:T(8,128)(2,1)S(1)}, bf16[2,64,1536]{2,1,0:T(8,128)(2,1)}, u32[]{:S(2)}, u32[]{:S(2)}) collective-permute-start(bf16[2,64,1536]{2,1,0:T(8,128)(2,1)S(1)} %collective-permute-done.2.refs_1_), channel_id=1, source_target_pairs={{0,16},{16,0},{32,48},{48,32},{64,80},{80,64},{96,112},{112,96},{1... | collective-permute-start | bytes 1179656 | tf_op jit(solution)/shard_map/ppermute | solution.py:256
  49.5 6.9 %collective-permute-start.8 = (bf16[2,64,1536]{2,1,0:T(8,128)(2,1)}, bf16[2,64,1536]{2,1,0:T(8,128)(2,1)}, u32[]{:S(2)}, u32[]{:S(2)}) collective-permute-start(bf16[2,64,1536]{2,1,0:T(8,128)(2,1)} %collective-permute-done.4.refs_3_), channel_id=1, source_target_pairs={{0,16},{16,0},{32,48},{48,32},{64,80},{80,64},{96,112},{112,96},{1... | collective-permute-start | bytes 1179656 | tf_op jit(solution)/shard_map/ppermute | solution.py:256
  51.4 5.0 %copy-start.7 = (bf16[64,1536]{1,0:T(8,128)(2,1)}, bf16[64,1536]{1,0:T(8,128)(2,1)S(1)}, u32[]{:S(2)}) copy-start(bf16[64,1536]{1,0:T(8,128)(2,1)S(1)} %collective-permute-done.5.refs_4_) | copy-start | bytes 589828
  51.4 5.0 %collective-permute-start.9 = (bf16[64,1536]{1,0:T(8,128)(2,1)S(1)}, bf16[64,1536]{1,0:T(8,128)(2,1)}, u32[]{:S(2)}, u32[]{:S(2)}) collective-permute-start(bf16[64,1536]{1,0:T(8,128)(2,1)S(1)} %collective-permute-done.5.refs_4_), channel_id=1, source_target_pairs={{0,16},{16,0},{32,48},{48,32},{64,80},{80,64},{96,112},{112,96},{1... | collective-permute-start | bytes 589832 | tf_op jit(solution)/shard_map/ppermute | solution.py:256
  63.2 51.3 %copy-start = (f32[8,64,128]{2,1,0:T(8,128)S(1)}, f32[8,64,128]{2,1,0:T(8,128)}, u32[]{:S(2)}) copy-start(f32[8,64,128]{2,1,0:T(8,128)} %table_ref.1) | copy-start | bytes 786436
  63.2 51.3 %copy-start.1 = (f32[8,64,128]{2,1,0:T(8,128)S(1)}, f32[8,64,128]{2,1,0:T(8,128)}, u32[]{:S(2)}) copy-start(f32[8,64,128]{2,1,0:T(8,128)} %accum_ref.1) | copy-start | bytes 786436
  63.2 51.3 %copy-start.2 = (s32[8,16]{1,0:T(8,128)S(1)}, s32[8,16]{1,0:T(8,128)}, u32[]{:S(2)}) copy-start(s32[8,16]{1,0:T(8,128)} %ids_ref.1) | copy-start | bytes 1540
  107.8 6.7 %collective-permute-start.10 = (f32[64,128]{1,0:T(8,128)S(1)}, f32[64,128]{1,0:T(8,128)S(1)}, u32[]{:S(2)}, u32[]{:S(2)}) collective-permute-start(f32[64,128]{1,0:T(8,128)S(1)} %shard_map.109.mine_ref), channel_id=1, source_target_pairs={{0,16},{16,0},{32,48},{48,32},{64,80},{80,64},{96,112},{112,96},{1... | collective-permute-start | bytes 98312 | tf_op jit(solution)/shard_map/ppermute | solution.py:300
